TPU v7x, 32 devices: a whole 2x2x4 slice. The times are simulated.
32 devices in a mesh: group: 4 (over z), dev: 8 (over y, x, core).
Axes of the slice: x: 2, y: 2, z: 4, core: 2. Of those that a mesh axis runs over, the one named last changes fastest.
Arguments:
- expert_input: bfloat16 [2, 192, 4096], P(None, ('group', 'dev')), may hold values from -6 to 6
- expert_ids: int32 [2, 192, 2], P(None, ('group', 'dev')), may hold values from 0 to 3, all different within a row; in each aligned block of 6 rows (0 to 5, 6 to 11, ..., all dimensions but the last counted through in order) at most 3 rows name the same one
- combine: float32 [2, 192, 2], P(None, ('group', 'dev')), may hold values from 0.25 to 1
- gate_weight: bfloat16 [8, 4096, 6144], P('dev', None, 'group'), may hold values from -0.09375 to 0.09375
- up_weight: bfloat16 [8, 4096, 6144], P('dev', None, 'group'), may hold values from -0.09375 to 0.09375
- down_weight: bfloat16 [8, 6144, 4096], P('dev', 'group'), may hold values from -0.0546875 to 0.0546875
Outputs:
- moe_out: bfloat16 [2, 192, 4096], P(None, ('group', 'dev'))
Inputs may be any that keep to these rules, and one draw needn't show every extreme that they name: `expert_ids`: the two experts of a row differ; among the rows of one device in one step no expert is named more than 3 times.
All inputs are finite; a program needn't handle non-finite values.
Results may differ from a plain program's by a relative error of at most 0.017.
Values may be sent and summed in bfloat16 or wider, within the bound.
No kernel may reach another device: no remote copies, remote signals or barrier semaphores. Data moves between devices by JAX's collectives and lax.ppermute only.
A program may use at most 128 MiB of HBM per device.

v0:
```python
import jax
import jax.numpy as jnp
from jax import lax
from jax.sharding import PartitionSpec as P


def local(expert_input, expert_ids, combine, gate_weight, up_weight, down_weight):
    dev_count = lax.axis_size("dev")
    row_count = expert_input.shape[1]
    step_count = expert_input.shape[0]
    experts = dev_count // 2
    slot_count = max(2, (2 * row_count + experts - 1) // experts)
    expert_iota = jnp.arange(experts, dtype=jnp.int32)
    owner_iota = jnp.arange(dev_count, dtype=jnp.int32) // 2
    slot_iota = jnp.arange(slot_count, dtype=jnp.int32)
    results = []
    for moment in range(step_count):
        chosen_ids = expert_ids[moment].reshape(-1)
        named_hits = (chosen_ids[:, None] == expert_iota[None, :]).astype(jnp.int32)
        earlier = jnp.cumsum(named_hits, 0) - named_hits
        position = jnp.sum(earlier * named_hits, 1)
        routed = (chosen_ids[None, None, :] == owner_iota[:, None, None]) & (
            position[None, None, :] == slot_iota[None, :, None]
        )
        routed_rows = routed.astype(jnp.float32).reshape(dev_count, slot_count, row_count, 2)
        row_pick = jnp.sum(routed_rows, 3).astype(jnp.bfloat16)
        outgoing = jnp.einsum(
            "dpj,jx->dpx", row_pick, expert_input[moment], preferred_element_type=jnp.float32
        ).astype(jnp.bfloat16)
        incoming = lax.all_to_all(outgoing, "dev", split_axis=0, concat_axis=0, tiled=True)
        shard_piece = lax.all_gather(incoming[None], "group", axis=0, tiled=True)
        flat_rows = shard_piece.reshape(-1, shard_piece.shape[-1])
        gate_val = jnp.dot(flat_rows, gate_weight[0], preferred_element_type=jnp.float32)
        up_val = jnp.dot(flat_rows, up_weight[0], preferred_element_type=jnp.float32)
        hidden = (jax.nn.silu(gate_val) * up_val).astype(jnp.bfloat16)
        product = jnp.dot(hidden, down_weight[0], preferred_element_type=jnp.float32)
        partial_value = product.reshape(shard_piece.shape)
        own_rows = lax.psum_scatter(
            partial_value.astype(jnp.bfloat16), "group", scatter_dimension=0, tiled=True
        ).astype(jnp.float32)
        halves = own_rows[0].astype(jnp.bfloat16)
        returned = lax.all_to_all(halves, "dev", split_axis=0, concat_axis=0, tiled=True)
        weights = jnp.einsum(
            "dpjk,jk->dpj", routed_rows, combine[moment], precision=lax.Precision.HIGHEST
        )
        blended = jnp.einsum(
            "dpj,dpx->jx", weights, returned.astype(jnp.float32), precision=lax.Precision.HIGHEST
        )
        results.append(blended.astype(jnp.bfloat16))
    return jnp.stack(results, 0)


def solution(mesh):
    in_specs = (
        P(None, ("group", "dev"), None),
        P(None, ("group", "dev"), None),
        P(None, ("group", "dev"), None),
        P("dev", None, "group"),
        P("dev", None, "group"),
        P("dev", "group", None),
    )
    out_specs = P(None, ("group", "dev"), None)
    return jax.shard_map(local, mesh=mesh, in_specs=in_specs, out_specs=out_specs, check_vma=False)
```

profile of v0, /device:TPU:0, one launch (start us, length us, event | category | flops | bytes accessed | tf_op | source)
XLA Modules:
  0.0 163.0 jit_solution(5792170546066468889)
XLA Ops:
  6.5 0.7 slice_bitcast_fusion.3
  7.2 0.1 copy.72
  7.3 0.1 eq.125
  7.4 0.2 reduce_window_sum.18
  7.6 0.1 eq.129
  7.7 0.1 copy.62
  7.8 0.1 eq.114
  7.9 0.2 reduce_window_sum.17
  8.1 0.1 eq.118
  8.2 0.1 copy.61
  8.3 0.1 copy.71
  8.4 1.2 fusion.50
  9.5 0.1 broadcast_compare_fusion.1
  9.6 0.1 convert_reduce_fusion
  9.8 0.2 convolution_convert_fusion.1
  10.0 0.9 copy.65
  10.9 5.2 %all-to-all-start = ((bf16[8,3,4096]{2,1,0:T(4,128)(2,1)}), bf16[8,3,4096]{2,1,0:T(4,128)(2,1)S(1)}, u32[]{:S(2)}, u32[]{:S(2)}) async-start(bf16[8,3,4096]{2,1,0:T(4,128)(2,1)} %copy.65), calls=%async_computation | async-start | bytes 524288 | tf_op jit(solution)/shard_map/all_to_all | solution.py:30
  16.1 0.2 convolution_convert_fusion
  16.3 0.9 copy.75
  17.2 5.8 %all-to-all-done = bf16[8,3,4096]{2,1,0:T(4,128)(2,1)S(1)} async-done(((bf16[8,3,4096]{2,1,0:T(4,128)(2,1)}), bf16[8,3,4096]{2,1,0:T(4,128)(2,1)S(1)}, u32[]{:S(2)}, u32[]{:S(2)}) %all-to-all-start) | async-done | bytes 196640 | tf_op jit(solution)/shard_map/all_to_all | solution.py:30
  23.0 3.4 %all-to-all-start.2 = ((bf16[8,3,4096]{2,1,0:T(4,128)(2,1)}), bf16[8,3,4096]{2,1,0:T(4,128)(2,1)S(1)}, u32[]{:S(2)}, u32[]{:S(2)}) async-start(bf16[8,3,4096]{2,1,0:T(4,128)(2,1)} %copy.75), calls=%async_computation.3 | async-start | bytes 524288 | tf_op jit(solution)/shard_map/all_to_all | solution.py:30
  26.4 0.0 reduce-scatter.3.cloned.1.call-start
  26.5 0.2 copy.66
  26.6 19.8 %all-gather = bf16[32,3,4096]{2,0,1:T(8,128)(2,1)S(1)} all-gather(bf16[8,3,4096]{2,0,1:T(8,128)(2,1)S(1)} %copy.66), channel_id=2, replica_groups=mesh['group'=4,'dev'=8] {'group'}, dimensions={0}, use_global_device_ids=true | all-gather | bytes 983040 | tf_op jit(solution)/shard_map/all_gather | solution.py:31
  46.4 0.7 copy.67
  47.1 0.7 reshape.161
  47.8 6.7 %fusion.10 = f32[96,1536]{1,0:T(8,128)S(1)} fusion(bf16[96,4096]{1,0:T(8,128)(2,1)S(1)} %reshape.161, bf16[1,4096,1536]{2,1,0:T(8,128)(2,1)} %param.9), kind=kOutput, calls=%fused_computation.10 | convolution fusion | flops 1207959552 | bytes 13959168 | tf_op jit(solution)/shard_map/dot_general | solution.py:33
  54.5 6.7 %fusion.31 = bf16[96,1536]{1,0:T(8,128)(2,1)S(1)} fusion(bf16[96,4096]{1,0:T(8,128)(2,1)S(1)} %reshape.161, bf16[1,4096,1536]{2,1,0:T(8,128)(2,1)} %param.10, f32[96,1536]{1,0:T(8,128)S(1)} %fusion.10), kind=kOutput, calls=%fused_computation.25 | convolution fusion | flops 1208844288 | bytes 14254080 | tf_op jit(solution)/shard_map/dot_general | solution.py:34
  61.2 0.2 dot_general.44
  61.4 7.6 %fusion.12 = bf16[4,8,3,4096]{3,1,2,0:T(8,128)(2,1)} fusion(bf16[1,1536,4096]{2,1,0:T(8,128)(2,1)} %param.11, bf16[4,8,3,1536]{3,2,1,0:T(4,128)(2,1)S(1)} %dot_general.44), kind=kOutput, calls=%fused_computation.12 | convolution fusion | flops 1208352768 | bytes 13664256 | tf_op jit(solution)/shard_map/dot_general | solution.py:36
  69.0 0.0 reduce-scatter.3.cloned.1.call-update
  69.0 0.0 reduce-scatter.5.cloned.1.call-start
  69.1 0.0 all-to-all-done.2
  69.1 0.2 copy.76
  69.2 25.6 %all-gather.1 = bf16[32,3,4096]{2,0,1:T(8,128)(2,1)S(1)} all-gather(bf16[8,3,4096]{2,0,1:T(8,128)(2,1)S(1)} %copy.76), channel_id=3, replica_groups=mesh['group'=4,'dev'=8] {'group'}, dimensions={0}, use_global_device_ids=true | all-gather | bytes 983040 | tf_op jit(solution)/shard_map/all_gather | solution.py:31
  94.8 0.7 copy.77
  95.5 0.7 reshape.162
  96.2 6.7 %fusion.8 = f32[96,1536]{1,0:T(8,128)S(1)} fusion(bf16[96,4096]{1,0:T(8,128)(2,1)S(1)} %reshape.162, bf16[1,4096,1536]{2,1,0:T(8,128)(2,1)} %param.9), kind=kOutput, calls=%fused_computation.8 | convolution fusion | flops 1207959552 | bytes 13959168 | tf_op jit(solution)/shard_map/dot_general | solution.py:33
  102.9 6.7 %fusion.28 = bf16[96,1536]{1,0:T(8,128)(2,1)S(1)} fusion(bf16[96,4096]{1,0:T(8,128)(2,1)S(1)} %reshape.162, bf16[1,4096,1536]{2,1,0:T(8,128)(2,1)} %param.10, f32[96,1536]{1,0:T(8,128)S(1)} %fusion.8), kind=kOutput, calls=%fused_computation.24 | convolution fusion | flops 1208844288 | bytes 14254080 | tf_op jit(solution)/shard_map/dot_general | solution.py:34
  109.7 0.0 copy-start
  109.7 0.2 dot_general.51
  109.8 7.6 %fusion.15 = bf16[4,8,3,4096]{3,1,2,0:T(8,128)(2,1)} fusion(bf16[1,1536,4096]{2,1,0:T(8,128)(2,1)} %param.11, bf16[4,8,3,1536]{3,2,1,0:T(4,128)(2,1)S(1)} %dot_general.51), kind=kOutput, calls=%fused_computation.13 | convolution fusion | flops 1208352768 | bytes 13664256 | tf_op jit(solution)/shard_map/dot_general | solution.py:36
  117.4 0.0 reduce-scatter.5.cloned.1.call-update
  117.4 0.0 copy-done
  117.4 0.1 copy.83
  117.5 0.1 copy.88
  117.6 0.0 reduce-scatter.3.cloned.1.call-done
  117.6 1.8 %copy.69 = bf16[8,3,4096]{2,1,0:T(4,128)(2,1)} copy(bf16[8,3,4096]{2,0,1:T(8,128)(2,1)} %bitcast.87) | data formatting | bytes 393216 | tf_op jit(solution)/shard_map/convert_element_type | solution.py:41
  119.4 4.1 %all-to-all-start.1 = ((bf16[8,3,4096]{2,1,0:T(4,128)(2,1)}), bf16[8,3,4096]{2,1,0:T(4,128)(2,1)S(1)}, u32[]{:S(2)}, u32[]{:S(2)}) async-start(bf16[8,3,4096]{2,1,0:T(4,128)(2,1)} %copy.69), calls=%async_computation.2 | async-start | bytes 524288 | tf_op jit(solution)/shard_map/all_to_all | solution.py:42
  123.5 0.2 fusion.40
  123.7 19.0 %reduce-scatter.5.cloned.1.call-done = bf16[1,8,3,4096]{3,1,2,0:T(8,128)(2,1)} async-done(((bf16[4,8,3,4096]{3,1,2,0:T(8,128)(2,1)}), bf16[1,8,3,4096]{3,1,2,0:T(8,128)(2,1)}) %reduce-scatter.5.cloned.1.call-update) | async-done | bytes 196624 | tf_op jit(solution)/shard_map/reduce_scatter | solution.py:38
  142.7 1.8 %copy.79 = bf16[8,3,4096]{2,1,0:T(4,128)(2,1)} copy(bf16[8,3,4096]{2,0,1:T(8,128)(2,1)} %bitcast.88) | data formatting | bytes 393216 | tf_op jit(solution)/shard_map/convert_element_type | solution.py:41
  144.5 0.0 all-to-all-done.1
  144.5 3.7 %all-to-all-start.3 = ((bf16[8,3,4096]{2,1,0:T(4,128)(2,1)}), bf16[8,3,4096]{2,1,0:T(4,128)(2,1)S(1)}, u32[]{:S(2)}, u32[]{:S(2)}) async-start(bf16[8,3,4096]{2,1,0:T(4,128)(2,1)} %copy.79), calls=%async_computation.5 | async-start | bytes 524288 | tf_op jit(solution)/shard_map/all_to_all | solution.py:42
  148.1 0.2 fusion.38
  148.3 0.3 fusion.21
  148.7 6.4 %all-to-all-done.3 = bf16[8,3,4096]{2,1,0:T(4,128)(2,1)S(1)} async-done(((bf16[8,3,4096]{2,1,0:T(4,128)(2,1)}), bf16[8,3,4096]{2,1,0:T(4,128)(2,1)S(1)}, u32[]{:S(2)}, u32[]{:S(2)}) %all-to-all-start.3) | async-done | bytes 196640 | tf_op jit(solution)/shard_map/all_to_all | solution.py:42
  155.1 0.3 fusion.20
  155.4 0.7 copy.81
  (9 shorter events, 0.1 us)
Async XLA Ops:
  10.9 12.1 %all-to-all-start = ((bf16[8,3,4096]{2,1,0:T(4,128)(2,1)}), bf16[8,3,4096]{2,1,0:T(4,128)(2,1)S(1)}, u32[]{:S(2)}, u32[]{:S(2)}) async-start(bf16[8,3,4096]{2,1,0:T(4,128)(2,1)} %copy.65), calls=%async_computation | async-start | bytes 524288 | tf_op jit(solution)/shard_map/all_to_all | solution.py:30
  23.0 46.0 %all-to-all-start.2 = ((bf16[8,3,4096]{2,1,0:T(4,128)(2,1)}), bf16[8,3,4096]{2,1,0:T(4,128)(2,1)S(1)}, u32[]{:S(2)}, u32[]{:S(2)}) async-start(bf16[8,3,4096]{2,1,0:T(4,128)(2,1)} %copy.75), calls=%async_computation.3 | async-start | bytes 524288 | tf_op jit(solution)/shard_map/all_to_all | solution.py:30
  26.4 91.2 %reduce-scatter.3.cloned.1.call-start = ((), (), s32[]{:S(2)}) async-start(), calls=%async_computation.6 | async-start | bytes 983040 | tf_op jit(solution)/shard_map/reduce_scatter | solution.py:38
  69.0 73.7 %reduce-scatter.5.cloned.1.call-start = ((), (), s32[]{:S(2)}) async-start(), calls=%async_computation.7 | async-start | bytes 983040 | tf_op jit(solution)/shard_map/reduce_scatter | solution.py:38
  109.7 7.8 %copy-start = (f32[2,6,2]{1,2,0:T(2,128)S(1)}, f32[2,6,2]{1,2,0:T(2,128)}, u32[]{:S(2)}) copy-start(f32[2,6,2]{1,2,0:T(2,128)} %param.8) | copy-start | bytes 292
  119.4 25.0 %all-to-all-start.1 = ((bf16[8,3,4096]{2,1,0:T(4,128)(2,1)}), bf16[8,3,4096]{2,1,0:T(4,128)(2,1)S(1)}, u32[]{:S(2)}, u32[]{:S(2)}) async-start(bf16[8,3,4096]{2,1,0:T(4,128)(2,1)} %copy.69), calls=%async_computation.2 | async-start | bytes 524288 | tf_op jit(solution)/shard_map/all_to_all | solution.py:42
  144.5 10.6 %all-to-all-start.3 = ((bf16[8,3,4096]{2,1,0:T(4,128)(2,1)}), bf16[8,3,4096]{2,1,0:T(4,128)(2,1)S(1)}, u32[]{:S(2)}, u32[]{:S(2)}) async-start(bf16[8,3,4096]{2,1,0:T(4,128)(2,1)} %copy.79), calls=%async_computation.5 | async-start | bytes 524288 | tf_op jit(solution)/shard_map/all_to_all | solution.py:42
Sparse Core Ops, SparseCore 0:
  69.1 29.8 reduce-scatter.2
  117.5 25.0 reduce-scatter.4
where the time goes:
time: 164 us; the launch traced here: 163 us
  blocking collectives  45.4 us (28%)
  matrix products  43.5 us (27%)
  waiting for transfers between devices  31.3 us (19%)
  starting transfers between devices  16.4 us (10%)
  between operations  13.6 us (8%)
  local copies, waits for them, and re-layouts  12.2 us (7%)
    all_gather x2, blocking collectives, local(): shard_piece = lax.all_gather(incoming[None], 'group', axis=0, tiled=True)  45.4 us
    reduce_scatter x2, waiting for transfers between devices, local(): lax.psum_scatter(partial_value.astype(jnp.bfloat16), 'group', scatter_dim...  19 us
    dot_general x2, matrix products, local(): jnp.dot(hidden, down_weight[0], preferred_element_type=jnp.float32)  15.1 us
    dot_general x2, matrix products, local(): jnp.dot(flat_rows, up_weight[0], preferred_element_type=jnp.float32)  13.5 us
    dot_general x2, matrix products, local(): jnp.dot(flat_rows, gate_weight[0], preferred_element_type=jnp.float32)  13.4 us
    all_to_all x2, starting transfers between devices, local(): lax.all_to_all(outgoing, 'dev', split_axis=0, concat_axis=0, tiled=True)  8.58 us
    all_to_all x2, starting transfers between devices, local(): lax.all_to_all(halves, 'dev', split_axis=0, concat_axis=0, tiled=True)  7.73 us
    all_to_all x2, waiting for transfers between devices, local(): lax.all_to_all(halves, 'dev', split_axis=0, concat_axis=0, tiled=True)  6.41 us
  transfers between devices with their start and end apart: 6, of which 3 were waited for; matrix products, arithmetic and copies ran while one was open for 31% of the time, Pallas kernels for 0%

commit v1 on v0

v1 whole, which is shorter than its diff:
```python
import functools

import jax
import jax.numpy as jnp
from jax import lax
from jax.experimental import pallas as pl
from jax.experimental.pallas import tpu as pltpu
from jax.sharding import PartitionSpec as P

BF = jnp.bfloat16
F32 = jnp.float32
LANES = 128
SUB = 8
FOLD = 16


def whole(memory_space=pltpu.VMEM):
    return pl.BlockSpec(memory_space=memory_space)


def call(body, outs, args, name, spaces=None, scratch=(), limit=12):
    spaces = spaces or [pltpu.VMEM] * len(args)
    return pl.pallas_call(
        body,
        out_shape=[jax.ShapeDtypeStruct(s, BF) for s in outs],
        in_specs=[whole(s) for s in spaces],
        out_specs=[whole() for _ in outs],
        scratch_shapes=list(scratch),
        name=name,
        compiler_params=pltpu.CompilerParams(vmem_limit_bytes=limit << 20),
    )(*args)


def pack_body(experts, slots, ids_ref, combine_ref, x_ref, o_ref):
    steps, rows, width = x_ref.shape
    half = width // 2
    own = lax.axis_index("dev") // 2
    table_rows = experts * steps * slots
    row_at = lax.broadcasted_iota(jnp.int32, (table_rows, LANES), 0)
    lane = lax.broadcasted_iota(jnp.int32, (table_rows, LANES), 1)
    group, place = lane // FOLD, lane % FOLD
    low = jnp.where((group == 1) & (place >= 12), place - 4, jnp.where((group == 1) & (place >= SUB), -1, place))
    table = jnp.zeros((table_rows, LANES), F32)
    for t in range(steps):
        counts = [jnp.int32(0)] * experts
        for r in range(rows):
            for k in range(2):
                e = ids_ref[t, r, k]
                position = jnp.int32(0)
                for c in range(experts):
                    position = jnp.where(e == c, counts[c], position)
                counts = [counts[c] + (e == c).astype(jnp.int32) for c in range(experts)]
                slot = ((e ^ own) * steps + t) * slots + position
                hit = (row_at == slot) & (low == t * rows + r)
                table = jnp.where(hit, combine_ref[t, r, k], table)
    ones = jnp.where(table != 0.0, 1.0, 0.0)
    high = table.astype(BF).astype(F32)
    middle = (table - high).astype(BF).astype(F32)
    rest = table - high - middle
    coded = jnp.where(
        group <= 1, ones, jnp.where(group == 2, high, jnp.where(group == 3, middle, jnp.where(group == 4, rest, 0.0)))
    ).astype(BF)
    flat = jnp.concatenate([x_ref[t].astype(F32) for t in range(steps)], 0)
    tail = flat[SUB:]
    o_ref[:, :width] = flat[:SUB].astype(BF)
    o_ref[:, width : width + half] = jnp.concatenate([tail[:, :half], tail[:, half:]], 0).astype(BF)
    for b in range(table_rows // SUB):
        start = width + half + b * LANES
        o_ref[:, start : start + LANES] = coded[b * SUB : (b + 1) * SUB]


def tables_of(packed, experts, pair, width, group):
    base = width + width // 2
    members = len(packed)
    table_rows = experts * pair
    total = table_rows * members
    blocks = []
    for k, ref in enumerate(packed):
        tab = jnp.concatenate(
            [ref[:, base + b * LANES : base + (b + 1) * LANES] for b in range(table_rows // SUB)], 0
        ).astype(F32)
        at = k % (LANES // FOLD)
        shift = (at - group) * FOLD % LANES
        moved = pltpu.roll(tab, shift, 1) if shift else tab
        lane = lax.broadcasted_iota(jnp.int32, moved.shape, 1)
        moved = jnp.where(lane // FOLD == at, moved, 0.0)
        tiles = [jnp.zeros_like(moved)] * -(-members * FOLD // LANES)
        tiles[k * FOLD // LANES] = moved
        blocks.append(jnp.concatenate(tiles, 1))
    stacked = jnp.concatenate(blocks, 0).astype(BF)
    to = lax.broadcasted_iota(jnp.int32, (total, total), 0)
    source = lax.broadcasted_iota(jnp.int32, (total, total), 1)
    e, k, p = to // (members * pair), to // pair % members, to % pair
    order = jnp.where(source == k * table_rows + e * pair + p, 1.0, 0.0).astype(BF)
    return jnp.dot(order, stacked, preferred_element_type=F32).astype(BF)[:, : members * FOLD]


def route_body(experts, pair, width, *refs):
    members = len(refs) - experts
    packed, outs = refs[:members], refs[members:]
    half = width // 2
    block = members * pair
    for side in range(2):
        pick = tables_of(packed, experts, pair, width, side)
        rows = jnp.concatenate(
            [part for ref in packed for part in (ref[:, side * half : (side + 1) * half], ref[:, width : width + half])], 0
        )
        got = jnp.dot(pick, rows, preferred_element_type=F32).astype(BF)
        for j in range(experts):
            outs[j][:, side * half : (side + 1) * half] = got[j * block : (j + 1) * block]


def up_body(count, *refs):
    blocks, gate_ref, up_ref, hidden_ref, rows_ref = refs[:count], refs[count], refs[count + 1], refs[count + 2], refs[count + 3]
    rows = jnp.concatenate([b[...] for b in blocks], 0)
    rows_ref[...] = rows
    tile = 256

    def step(j, carry):
        columns = pl.ds(pl.multiple_of(j * tile, tile), tile)
        gate = jnp.dot(rows_ref[...], gate_ref[:, columns], preferred_element_type=F32)
        up = jnp.dot(rows_ref[...], up_ref[:, columns], preferred_element_type=F32)
        hidden_ref[:, columns] = (jax.nn.silu(gate) * up).astype(BF)
        return carry

    lax.fori_loop(0, hidden_ref.shape[1] // tile, step, 0)


def down_body(hidden_ref, down_ref, own_ref, other_ref):
    tile = 512
    mine = own_ref.shape[0]

    def step(j, carry):
        columns = pl.ds(pl.multiple_of(j * tile, tile), tile)
        value = jnp.dot(hidden_ref[...], down_ref[:, columns], preferred_element_type=F32).astype(BF)
        own_ref[:, columns] = value[:mine]
        other_ref[:, columns] = value[mine:]
        return carry

    lax.fori_loop(0, own_ref.shape[1] // tile, step, 0)


def add_body(own_ref, got_ref, *outs):
    block = outs[0].shape[0]
    for j, out in enumerate(outs):
        at = slice(j * block, (j + 1) * block)
        out[...] = (own_ref[at].astype(F32) + got_ref[at].astype(F32)).astype(BF)


def blend_body(experts, pair, width, members, *refs):
    packed, values, outs = refs[:members], refs[members : members + experts], refs[members + experts :]
    half = width // 2
    parts = [tables_of(packed, experts, pair, width, g) for g in (2, 3, 4)]
    weights = jnp.concatenate(parts, 1)
    span = members * FOLD
    tails = []
    for side in range(2):
        cols = slice(side * half, (side + 1) * half)
        value = jnp.concatenate([v[:, cols] for v in values], 0)
        total = lax.dot_general(weights, value, (((0,), (0,)), ((), ())), preferred_element_type=F32)
        total = total[:span] + total[span : 2 * span] + total[2 * span :]
        for k, out in enumerate(outs):
            out[:, cols] = total[k * FOLD : k * FOLD + SUB].astype(BF)
        tails.append([total[k * FOLD + SUB : k * FOLD + SUB + 4] for k in range(members)])
    for k, out in enumerate(outs):
        out[:, width : width + half] = jnp.concatenate([tails[0][k], tails[1][k]], 0).astype(BF)


def finish_body(*refs):
    parts, out_ref = refs[:-1], refs[-1]
    steps, rows, width = out_ref.shape
    half = width // 2
    total = parts[0][...].astype(F32)
    for p in parts[1:]:
        total = total + p[...].astype(F32)
    tail = total[:, width : width + half]
    tail = jnp.concatenate([tail[:4], tail[4:]], 1)
    flat = jnp.concatenate([total[:, :width], tail], 0)
    for t in range(steps):
        out_ref[t] = flat[t * rows : (t + 1) * rows].astype(BF)


def local(expert_input, expert_ids, combine, gate_weight, up_weight, down_weight):
    members = lax.axis_size("group")
    devices = lax.axis_size("dev")
    experts = devices // 2
    steps, row_count, width = expert_input.shape
    slots = max(2, (2 * row_count + experts - 1) // experts)
    pair = steps * slots
    packed_width = width + width // 2 + experts * pair // SUB * LANES
    block = members * pair

    (packed,) = call(
        functools.partial(pack_body, experts, slots),
        [(SUB, packed_width)],
        (expert_ids, combine, expert_input),
        "pack",
        [pltpu.SMEM, pltpu.SMEM, pltpu.VMEM],
    )
    far = sorted(range(1, members), key=lambda k: -min(k, members - k))
    gathered = {0: packed}
    for k in far:
        gathered[k] = lax.ppermute(packed, "group", [(i, (i + k) % members) for i in range(members)])
    gathered = [gathered[k] for k in range(members)]

    routed = call(
        functools.partial(route_body, experts, pair, width), [(block, width)] * experts, gathered, "route"
    )

    def exchange(arrays):
        order = sorted(range(1, experts), key=lambda j: -bin(j).count("1"))
        got = {0: arrays[0]}
        for j in order:
            got[j] = lax.ppermute(arrays[j], "dev", [(i, i ^ (2 * j)) for i in range(devices)])
        return [got[j] for j in range(experts)]

    def swap(array):
        return lax.ppermute(array, "dev", [(i, i ^ 1) for i in range(devices)])

    mine = exchange(routed)
    theirs = [swap(a) for a in mine]
    rows_all = 2 * experts * block
    hidden_units = gate_weight.shape[2]
    (hidden,) = call(
        functools.partial(up_body, 2 * experts),
        [(rows_all, hidden_units)],
        (*mine, *theirs, gate_weight[0], up_weight[0]),
        "gate_up",
        scratch=[pltpu.VMEM((rows_all, width), BF)],
    )
    own, other = call(down_body, [(rows_all // 2, width)] * 2, (hidden, down_weight[0]), "down")
    halves = call(add_body, [(block, width)] * experts, (own, swap(other)), "add")
    returned = exchange(halves)
    blended = call(
        functools.partial(blend_body, experts, pair, width, members),
        [(SUB, width + width // 2)] * members,
        (*gathered, *returned),
        "blend",
    )
    final = {0: blended[0]}
    for k in far:
        final[k] = lax.ppermute(blended[k], "group", [(i, (i - k) % members) for i in range(members)])
    (out,) = call(finish_body, [expert_input.shape], [final[k] for k in range(members)], "finish")
    return out


def solution(mesh):
    in_specs = (
        P(None, ("group", "dev"), None),
        P(None, ("group", "dev"), None),
        P(None, ("group", "dev"), None),
        P("dev", None, "group"),
        P("dev", None, "group"),
        P("dev", "group", None),
    )
    out_specs = P(None, ("group", "dev"), None)
    return jax.shard_map(local, mesh=mesh, in_specs=in_specs, out_specs=out_specs, check_vma=False)
```

time: 164 us -> 78.9 us (0.48)
  blocking collectives: 45.4 us -> 0 us
  matrix products: 43.5 us -> 0 us
  between operations: 13.6 us -> 0.1 us
  Pallas kernels: 0 us -> 12.9 us
  waiting for transfers between devices: 31.3 us -> 35.1 us
  starting transfers between devices: 16.4 us -> 18.2 us
    all_gather x2 -> x0, blocking collectives: 45.4 us -> none  [local(): shard_piece = lax.all_gather(incoming[None], 'group', axis=0, tiled=True)]
    dot_general x12 -> x0, matrix products: 43.5 us -> none  [the longest x2 15.1 us: local(): jnp.dot(hidden, down_weight[0], preferred_element_type=jnp.float32)]
    ppermute x0 -> x17, waiting for transfers between devices: none -> 35.1 us  [the longest x6 16.9 us: exchange(): lax.ppermute(arrays[j], 'dev', [(i, i ^ 2 * j) for i in range(devices)])]
    reduce_scatter x2 -> x0, waiting for transfers between devices: 19 us -> none  [local(): lax.psum_scatter(partial_value.astype(jnp.bfloat16), 'group', scatter_dim...]
    ppermute x0 -> x17, starting transfers between devices: none -> 18.2 us  [the longest x6 7.11 us: exchange(): lax.ppermute(arrays[j], 'dev', [(i, i ^ 2 * j) for i in range(devices)])]
    all_to_all x4 -> x0, starting transfers between devices: 16.3 us -> none  [the longest x2 8.58 us: local(): lax.all_to_all(outgoing, 'dev', split_axis=0, concat_axis=0, tiled=True)]
    pallas_call x0 -> x7, Pallas kernels: none -> 12.9 us  [call(): pl.pallas_call(body, out_shape=[jax.ShapeDtypeStruct(s, BF) for s in outs...]
    all_to_all x4 -> x0, waiting for transfers between devices: 12.2 us -> none  [the longest x2 6.41 us: local(): lax.all_to_all(halves, 'dev', split_axis=0, concat_axis=0, tiled=True)]
  transfers between devices with their start and end apart: 6 -> 17, of which waited for: 3 -> 12; matrix products, arithmetic and copies ran while one was open for 31% -> 0% of each run, Pallas kernels for 0% -> 0%
where the time goes in v1:
time: 78.9 us; the launch traced here: 78.6 us
  waiting for transfers between devices  35.1 us (44%)
  starting transfers between devices  18.2 us (23%)
  Pallas kernels  12.9 us (16%)
  local copies, waits for them, and re-layouts  12.4 us (16%)
    ppermute x6, waiting for transfers between devices, exchange(): lax.ppermute(arrays[j], 'dev', [(i, i ^ 2 * j) for i in range(devices)])  16.9 us
    pallas_call x7, Pallas kernels, call(): pl.pallas_call(body, out_shape=[jax.ShapeDtypeStruct(s, BF) for s in outs...  12.9 us
    unnamed x13, local copies, waits for them, and re-layouts  11.7 us
    ppermute x3, waiting for transfers between devices, local(): lax.ppermute(packed, 'group', [(i, (i + k) % members) for i in range(memb...  8.2 us
    ppermute x6, starting transfers between devices, exchange(): lax.ppermute(arrays[j], 'dev', [(i, i ^ 2 * j) for i in range(devices)])  7.11 us
    ppermute x3, waiting for transfers between devices, local(): lax.ppermute(blended[k], 'group', [(i, (i - k) % members) for i in range(...  6.67 us
    ppermute x3, starting transfers between devices, local(): lax.ppermute(packed, 'group', [(i, (i + k) % members) for i in range(memb...  6.11 us
    ppermute x3, starting transfers between devices, local(): lax.ppermute(blended[k], 'group', [(i, (i - k) % members) for i in range(...  4.18 us
  transfers between devices with their start and end apart: 17, of which 12 were waited for; matrix products, arithmetic and copies ran while one was open for 0% of the time, Pallas kernels for 0%

profile of v1, /device:TPU:0, one launch (start us, length us, event | category | flops | bytes accessed | tf_op | source)
XLA Modules:
  0.0 78.6 jit_solution(4075495674561485135)
XLA Ops:
  0.0 0.8 copy.7.ids_ref
  0.8 0.8 copy.8.combine_ref
  1.5 1.0 %copy.9.x_ref = bf16[2,6,4096]{2,1,0:T(8,128)(2,1)S(1)} copy(bf16[2,6,4096]{2,0,1:T(2,128)(2,1)} %param.6) | data formatting | bytes 196608 | tf_op args[0]
  2.5 1.0 %pack.1.refs_0_ = bf16[8,6528]{1,0:T(8,128)(2,1)S(1)} custom-call(s32[2,6,2]{2,1,0:T(8,128)S(1)} %copy.7.ids_ref, f32[2,6,2]{2,1,0:T(8,128)S(1)} %copy.8.combine_ref, bf16[2,6,4096]{2,1,0:T(8,128)(2,1)S(1)} %copy.9.x_ref), custom_call_target="tpu_custom_call" | custom-call | tf_op jit(solution)/shard_map/pack/pallas_call | solution.py:23
  3.5 5.1 %collective-permute-start.2 = (bf16[8,6528]{1,0:T(8,128)(2,1)S(1)}, bf16[8,6528]{1,0:T(8,128)(2,1)S(1)}, u32[]{:S(2)}, u32[]{:S(2)}) collective-permute-start(bf16[8,6528]{1,0:T(8,128)(2,1)S(1)} %pack.1.refs_0_), channel_id=1, source_target_pairs={{0,24},{8,0},{16,8},{24,16},{1,25},{9,1},{17,9},{25,17},{2,26},{10... | collective-permute-start | bytes 313352 | tf_op jit(solution)/shard_map/ppermute | solution.py:203
  8.6 0.0 collective-permute-start.1
  8.6 1.0 %collective-permute-start = (bf16[8,6528]{1,0:T(8,128)(2,1)S(1)}, bf16[8,6528]{1,0:T(8,128)(2,1)S(1)}, u32[]{:S(2)}, u32[]{:S(2)}) collective-permute-start(bf16[8,6528]{1,0:T(8,128)(2,1)S(1)} %pack.1.refs_0_), channel_id=1, source_target_pairs={{0,8},{8,16},{16,24},{24,0},{1,9},{9,17},{17,25},{25,1},{2,10},{10... | collective-permute-start | bytes 313352 | tf_op jit(solution)/shard_map/ppermute | solution.py:203
  9.6 2.3 %collective-permute-done.2.refs_3_ = bf16[8,6528]{1,0:T(8,128)(2,1)S(1)} collective-permute-done((bf16[8,6528]{1,0:T(8,128)(2,1)S(1)}, bf16[8,6528]{1,0:T(8,128)(2,1)S(1)}, u32[]{:S(2)}, u32[]{:S(2)}) %collective-permute-start.2) | collective-permute-done | bytes 104480 | tf_op jit(solution)/shard_map/ppermute | solution.py:203
  12.0 5.9 %collective-permute-done.1.refs_2_ = bf16[8,6528]{1,0:T(8,128)(2,1)S(1)} collective-permute-done((bf16[8,6528]{1,0:T(8,128)(2,1)S(1)}, bf16[8,6528]{1,0:T(8,128)(2,1)S(1)}, u32[]{:S(2)}, u32[]{:S(2)}) %collective-permute-start.1) | collective-permute-done | bytes 104480 | tf_op jit(solution)/shard_map/ppermute | solution.py:203
  17.8 0.0 collective-permute-done.refs_1_
  17.8 0.0 slice-start
  17.8 0.7 route.1
  18.5 1.6 %collective-permute-start.3 = (bf16[24,4096]{1,0:T(8,128)(2,1)S(1)}, bf16[24,4096]{1,0:T(8,128)(2,1)S(1)}, u32[]{:S(2)}, u32[]{:S(2)}) collective-permute-start(bf16[24,4096]{1,0:T(8,128)(2,1)S(1)} %get-tuple-element.20), channel_id=1, source_target_pairs={{0,2},{1,3},{2,0},{3,1},{4,6},{5,7},{6,4},{7,5},{8,10},{9,11},{10,... | collective-permute-start | bytes 589832 | tf_op jit(solution)/shard_map/ppermute | solution.py:214
  20.1 1.5 %collective-permute-start.4 = (bf16[24,4096]{1,0:T(8,128)(2,1)S(1)}, bf16[24,4096]{1,0:T(8,128)(2,1)S(1)}, u32[]{:S(2)}, u32[]{:S(2)}) collective-permute-start(bf16[24,4096]{1,0:T(8,128)(2,1)S(1)} %get-tuple-element.21), channel_id=1, source_target_pairs={{0,4},{1,5},{2,6},{3,7},{4,0},{5,1},{6,2},{7,3},{8,12},{9,13},{10,... | collective-permute-start | bytes 589832 | tf_op jit(solution)/shard_map/ppermute | solution.py:214
  21.6 0.5 collective-permute-start.5
  22.1 0.0 collective-permute-start.6
  22.1 4.3 %collective-permute-done.3.refs_1_ = bf16[24,4096]{1,0:T(8,128)(2,1)S(1)} collective-permute-done((bf16[24,4096]{1,0:T(8,128)(2,1)S(1)}, bf16[24,4096]{1,0:T(8,128)(2,1)S(1)}, u32[]{:S(2)}, u32[]{:S(2)}) %collective-permute-start.3) | collective-permute-done | bytes 196640 | tf_op jit(solution)/shard_map/ppermute | solution.py:214
  26.4 0.0 collective-permute-start.7
  26.4 3.9 %collective-permute-done.4.refs_2_ = bf16[24,4096]{1,0:T(8,128)(2,1)S(1)} collective-permute-done((bf16[24,4096]{1,0:T(8,128)(2,1)S(1)}, bf16[24,4096]{1,0:T(8,128)(2,1)S(1)}, u32[]{:S(2)}, u32[]{:S(2)}) %collective-permute-start.4) | collective-permute-done | bytes 196640 | tf_op jit(solution)/shard_map/ppermute | solution.py:214
  30.3 0.0 collective-permute-start.8
  30.3 0.0 collective-permute-done.5.refs_3_
  30.3 0.5 collective-permute-start.9
  30.8 0.0 collective-permute-done.6.refs_4_
  30.8 0.0 collective-permute-done.7.refs_5_
  30.8 0.9 %collective-permute-done.8.refs_6_ = bf16[24,4096]{1,0:T(8,128)(2,1)S(1)} collective-permute-done((bf16[24,4096]{1,0:T(8,128)(2,1)S(1)}, bf16[24,4096]{1,0:T(8,128)(2,1)S(1)}, u32[]{:S(2)}, u32[]{:S(2)}) %collective-permute-start.8) | collective-permute-done | bytes 196640 | tf_op jit(solution)/shard_map/ppermute | solution.py:218
  31.7 0.3 collective-permute-done.9.refs_7_
  32.0 0.0 copy-start
  32.0 4.6 %copy-done = bf16[1,4096,1536]{2,1,0:T(8,128)(2,1)S(1)} copy-done((bf16[1,4096,1536]{2,1,0:T(8,128)(2,1)S(1)}, bf16[1,4096,1536]{2,1,0:T(8,128)(2,1)}, u32[]{:S(2)}) %copy-start) | copy-done | bytes 12582936
  36.6 0.0 copy-start.1
  36.6 4.6 %copy-done.1 = bf16[1,4096,1536]{2,1,0:T(8,128)(2,1)S(1)} copy-done((bf16[1,4096,1536]{2,1,0:T(8,128)(2,1)S(1)}, bf16[1,4096,1536]{2,1,0:T(8,128)(2,1)}, u32[]{:S(2)}) %copy-start.1) | copy-done | bytes 12582936
  41.2 0.0 slice-start.1
  41.2 0.0 slice-start.2
  41.2 6.1 %gate_up.1.hidden_ref = bf16[192,1536]{1,0:T(8,128)(2,1)S(1)} custom-call(bf16[24,4096]{1,0:T(8,128)(2,1)S(1)} %get-tuple-element.19.refs_0_, bf16[24,4096]{1,0:T(8,128)(2,1)S(1)} %collective-permute-done.3.refs_1_, bf16[24,4096]{1,0:T(8,128)(2,1)S(1)} %collective-permute-done.4.refs_2_, bf16[24,4096]{1,0:T(8,128)(2,1)S(1)} %collective-permute-done.5.refs_3_, ...), custom_call_target="tpu_custom_call" | custom-call | tf_op jit(solution)/shard_map/gate_up/pallas_call | solution.py:23
  47.3 0.0 slice-done
  47.3 0.0 slice-done.1
  47.3 0.0 slice-done.2
  47.4 3.9 %down.1 = (bf16[96,4096]{1,0:T(8,128)(2,1)S(1)}, bf16[96,4096]{1,0:T(8,128)(2,1)S(1)}) custom-call(bf16[192,1536]{1,0:T(8,128)(2,1)S(1)} %gate_up.1.hidden_ref, bf16[1536,4096]{1,0:T(8,128)(2,1)S(1)} %bitcast.5), custom_call_target="tpu_custom_call" | custom-call | tf_op jit(solution)/shard_map/down/pallas_call | solution.py:23
  51.3 0.3 collective-permute-start.10
  51.6 2.1 %collective-permute-done.10.got_ref = bf16[96,4096]{1,0:T(8,128)(2,1)S(1)} collective-permute-done((bf16[96,4096]{1,0:T(8,128)(2,1)S(1)}, bf16[96,4096]{1,0:T(8,128)(2,1)S(1)}, u32[]{:S(2)}, u32[]{:S(2)}) %collective-permute-start.10) | collective-permute-done | bytes 786464 | tf_op jit(solution)/shard_map/ppermute | solution.py:218
  53.6 0.2 add.1
  53.8 1.0 %collective-permute-start.11 = (bf16[24,4096]{1,0:T(8,128)(2,1)S(1)}, bf16[24,4096]{1,0:T(8,128)(2,1)S(1)}, u32[]{:S(2)}, u32[]{:S(2)}) collective-permute-start(bf16[24,4096]{1,0:T(8,128)(2,1)S(1)} %get-tuple-element.26), channel_id=1, source_target_pairs={{0,2},{1,3},{2,0},{3,1},{4,6},{5,7},{6,4},{7,5},{8,10},{9,11},{10,... | collective-permute-start | bytes 589832 | tf_op jit(solution)/shard_map/ppermute | solution.py:214
  54.8 1.1 %collective-permute-start.12 = (bf16[24,4096]{1,0:T(8,128)(2,1)S(1)}, bf16[24,4096]{1,0:T(8,128)(2,1)S(1)}, u32[]{:S(2)}, u32[]{:S(2)}) collective-permute-start(bf16[24,4096]{1,0:T(8,128)(2,1)S(1)} %get-tuple-element.27), channel_id=1, source_target_pairs={{0,4},{1,5},{2,6},{3,7},{4,0},{5,1},{6,2},{7,3},{8,12},{9,13},{10,... | collective-permute-start | bytes 589832 | tf_op jit(solution)/shard_map/ppermute | solution.py:214
  55.9 1.4 %collective-permute-start.13 = (bf16[24,4096]{1,0:T(8,128)(2,1)S(1)}, bf16[24,4096]{1,0:T(8,128)(2,1)S(1)}, u32[]{:S(2)}, u32[]{:S(2)}) collective-permute-start(bf16[24,4096]{1,0:T(8,128)(2,1)S(1)} %get-tuple-element.28), channel_id=1, source_target_pairs={{0,6},{1,7},{2,4},{3,5},{4,2},{5,3},{6,0},{7,1},{8,14},{9,15},{10,... | collective-permute-start | bytes 589832 | tf_op jit(solution)/shard_map/ppermute | solution.py:214
  57.4 4.2 %collective-permute-done.11.refs_5_ = bf16[24,4096]{1,0:T(8,128)(2,1)S(1)} collective-permute-done((bf16[24,4096]{1,0:T(8,128)(2,1)S(1)}, bf16[24,4096]{1,0:T(8,128)(2,1)S(1)}, u32[]{:S(2)}, u32[]{:S(2)}) %collective-permute-start.11) | collective-permute-done | bytes 196640 | tf_op jit(solution)/shard_map/ppermute | solution.py:214
  61.6 2.9 %collective-permute-done.12.refs_6_ = bf16[24,4096]{1,0:T(8,128)(2,1)S(1)} collective-permute-done((bf16[24,4096]{1,0:T(8,128)(2,1)S(1)}, bf16[24,4096]{1,0:T(8,128)(2,1)S(1)}, u32[]{:S(2)}, u32[]{:S(2)}) %collective-permute-start.12) | collective-permute-done | bytes 196640 | tf_op jit(solution)/shard_map/ppermute | solution.py:214
  64.5 1.6 %collective-permute-done.13.refs_7_ = bf16[24,4096]{1,0:T(8,128)(2,1)S(1)} collective-permute-done((bf16[24,4096]{1,0:T(8,128)(2,1)S(1)}, bf16[24,4096]{1,0:T(8,128)(2,1)S(1)}, u32[]{:S(2)}, u32[]{:S(2)}) %collective-permute-start.13) | collective-permute-done | bytes 196640 | tf_op jit(solution)/shard_map/ppermute | solution.py:214
  66.1 0.9 %blend.1 = (bf16[8,6144]{1,0:T(8,128)(2,1)S(1)}, bf16[8,6144]{1,0:T(8,128)(2,1)S(1)}, bf16[8,6144]{1,0:T(8,128)(2,1)S(1)}, bf16[8,6144]{1,0:T(8,128)(2,1)S(1)}) custom-call(bf16[8,6528]{1,0:T(8,128)(2,1)S(1)} %pack.1.refs_0_, bf16[8,6528]{1,0:T(8,128)(2,1)S(1)} %collective-permute-done.refs_1_, bf16[8,6528]{1,0:T(8,128)(2,1)S(1)} %collective-permute-done.1.refs_2_, ...), custom_call_target="tpu_custom_call" | custom-call | tf_op jit(solution)/shard_map/blend/pallas_call | solution.py:23
  67.0 0.7 collective-permute-start.14
  67.7 1.5 %collective-permute-start.15 = (bf16[8,6144]{1,0:T(8,128)(2,1)S(1)}, bf16[8,6144]{1,0:T(8,128)(2,1)S(1)}, u32[]{:S(2)}, u32[]{:S(2)}) collective-permute-start(bf16[8,6144]{1,0:T(8,128)(2,1)S(1)} %get-tuple-element.31), channel_id=1, source_target_pairs={{0,16},{8,24},{16,0},{24,8},{1,17},{9,25},{17,1},{25,9},{2,18},{10... | collective-permute-start | bytes 294920 | tf_op jit(solution)/shard_map/ppermute | solution.py:242
  69.2 1.9 %collective-permute-start.16 = (bf16[8,6144]{1,0:T(8,128)(2,1)S(1)}, bf16[8,6144]{1,0:T(8,128)(2,1)S(1)}, u32[]{:S(2)}, u32[]{:S(2)}) collective-permute-start(bf16[8,6144]{1,0:T(8,128)(2,1)S(1)} %get-tuple-element.32), channel_id=1, source_target_pairs={{0,8},{8,16},{16,24},{24,0},{1,9},{9,17},{17,25},{25,1},{2,10},{10... | collective-permute-start | bytes 294920 | tf_op jit(solution)/shard_map/ppermute | solution.py:242
  71.2 1.1 %collective-permute-done.14.refs_1_ = bf16[8,6144]{1,0:T(8,128)(2,1)S(1)} collective-permute-done((bf16[8,6144]{1,0:T(8,128)(2,1)S(1)}, bf16[8,6144]{1,0:T(8,128)(2,1)S(1)}, u32[]{:S(2)}, u32[]{:S(2)}) %collective-permute-start.14) | collective-permute-done | bytes 98336 | tf_op jit(solution)/shard_map/ppermute | solution.py:242
  72.3 5.6 %collective-permute-done.15.refs_2_ = bf16[8,6144]{1,0:T(8,128)(2,1)S(1)} collective-permute-done((bf16[8,6144]{1,0:T(8,128)(2,1)S(1)}, bf16[8,6144]{1,0:T(8,128)(2,1)S(1)}, u32[]{:S(2)}, u32[]{:S(2)}) %collective-permute-start.15) | collective-permute-done | bytes 98336 | tf_op jit(solution)/shard_map/ppermute | solution.py:242
  77.8 0.0 collective-permute-done.16.refs_3_
  77.8 0.1 finish.1
  77.9 0.7 copy.10
  (1 shorter events, 0.0 us)
Async XLA Ops:
  3.5 8.4 %collective-permute-start.2 = (bf16[8,6528]{1,0:T(8,128)(2,1)S(1)}, bf16[8,6528]{1,0:T(8,128)(2,1)S(1)}, u32[]{:S(2)}, u32[]{:S(2)}) collective-permute-start(bf16[8,6528]{1,0:T(8,128)(2,1)S(1)} %pack.1.refs_0_), channel_id=1, source_target_pairs={{0,24},{8,0},{16,8},{24,16},{1,25},{9,1},{17,9},{25,17},{2,26},{10... | collective-permute-start | bytes 313352 | tf_op jit(solution)/shard_map/ppermute | solution.py:203
  8.6 9.2 %collective-permute-start.1 = (bf16[8,6528]{1,0:T(8,128)(2,1)S(1)}, bf16[8,6528]{1,0:T(8,128)(2,1)S(1)}, u32[]{:S(2)}, u32[]{:S(2)}) collective-permute-start(bf16[8,6528]{1,0:T(8,128)(2,1)S(1)} %pack.1.refs_0_), channel_id=1, source_target_pairs={{0,16},{8,24},{16,0},{24,8},{1,17},{9,25},{17,1},{25,9},{2,18},{10... | collective-permute-start | bytes 313352 | tf_op jit(solution)/shard_map/ppermute | solution.py:203
  8.6 9.2 %collective-permute-start = (bf16[8,6528]{1,0:T(8,128)(2,1)S(1)}, bf16[8,6528]{1,0:T(8,128)(2,1)S(1)}, u32[]{:S(2)}, u32[]{:S(2)}) collective-permute-start(bf16[8,6528]{1,0:T(8,128)(2,1)S(1)} %pack.1.refs_0_), channel_id=1, source_target_pairs={{0,8},{8,16},{16,24},{24,0},{1,9},{9,17},{17,25},{25,1},{2,10},{10... | collective-permute-start | bytes 313352 | tf_op jit(solution)/shard_map/ppermute | solution.py:203
  17.8 29.5 %slice-start = ((s8[12582912]{0:T(1024)(128)(4,1)}), s8[4194304]{0:T(1024)(128)(4,1)S(1)}, s32[]{:S(2)}) async-start(s8[12582912]{0:T(1024)(128)(4,1)} %bitcast.3), calls=%async_computation | async-start | bytes 8388608
  18.5 7.9 %collective-permute-start.3 = (bf16[24,4096]{1,0:T(8,128)(2,1)S(1)}, bf16[24,4096]{1,0:T(8,128)(2,1)S(1)}, u32[]{:S(2)}, u32[]{:S(2)}) collective-permute-start(bf16[24,4096]{1,0:T(8,128)(2,1)S(1)} %get-tuple-element.20), channel_id=1, source_target_pairs={{0,2},{1,3},{2,0},{3,1},{4,6},{5,7},{6,4},{7,5},{8,10},{9,11},{10,... | collective-permute-start | bytes 589832 | tf_op jit(solution)/shard_map/ppermute | solution.py:214
  20.1 10.2 %collective-permute-start.4 = (bf16[24,4096]{1,0:T(8,128)(2,1)S(1)}, bf16[24,4096]{1,0:T(8,128)(2,1)S(1)}, u32[]{:S(2)}, u32[]{:S(2)}) collective-permute-start(bf16[24,4096]{1,0:T(8,128)(2,1)S(1)} %get-tuple-element.21), channel_id=1, source_target_pairs={{0,4},{1,5},{2,6},{3,7},{4,0},{5,1},{6,2},{7,3},{8,12},{9,13},{10,... | collective-permute-start | bytes 589832 | tf_op jit(solution)/shard_map/ppermute | solution.py:214
  21.6 8.7 %collective-permute-start.5 = (bf16[24,4096]{1,0:T(8,128)(2,1)S(1)}, bf16[24,4096]{1,0:T(8,128)(2,1)S(1)}, u32[]{:S(2)}, u32[]{:S(2)}) collective-permute-start(bf16[24,4096]{1,0:T(8,128)(2,1)S(1)} %get-tuple-element.22), channel_id=1, source_target_pairs={{0,6},{1,7},{2,4},{3,5},{4,2},{5,3},{6,0},{7,1},{8,14},{9,15},{10,... | collective-permute-start | bytes 589832 | tf_op jit(solution)/shard_map/ppermute | solution.py:214
  22.1 8.7 %collective-permute-start.6 = (bf16[24,4096]{1,0:T(8,128)(2,1)S(1)}, bf16[24,4096]{1,0:T(8,128)(2,1)S(1)}, u32[]{:S(2)}, u32[]{:S(2)}) collective-permute-start(bf16[24,4096]{1,0:T(8,128)(2,1)S(1)} %get-tuple-element.19.refs_0_), channel_id=1, source_target_pairs={{0,1},{1,0},{2,3},{3,2},{4,5},{5,4},{6,7},{7,6},{8,9},{9,8},{10,11... | collective-permute-start | bytes 589832 | tf_op jit(solution)/shard_map/ppermute | solution.py:218
  26.4 4.4 %collective-permute-start.7 = (bf16[24,4096]{1,0:T(8,128)(2,1)S(1)}, bf16[24,4096]{1,0:T(8,128)(2,1)S(1)}, u32[]{:S(2)}, u32[]{:S(2)}) collective-permute-start(bf16[24,4096]{1,0:T(8,128)(2,1)S(1)} %collective-permute-done.3.refs_1_), channel_id=1, source_target_pairs={{0,1},{1,0},{2,3},{3,2},{4,5},{5,4},{6,7},{7,6},{8,9},{9,8},{10,11... | collective-permute-start | bytes 589832 | tf_op jit(solution)/shard_map/ppermute | solution.py:218
  30.3 1.4 %collective-permute-start.8 = (bf16[24,4096]{1,0:T(8,128)(2,1)S(1)}, bf16[24,4096]{1,0:T(8,128)(2,1)S(1)}, u32[]{:S(2)}, u32[]{:S(2)}) collective-permute-start(bf16[24,4096]{1,0:T(8,128)(2,1)S(1)} %collective-permute-done.4.refs_2_), channel_id=1, source_target_pairs={{0,1},{1,0},{2,3},{3,2},{4,5},{5,4},{6,7},{7,6},{8,9},{9,8},{10,11... | collective-permute-start | bytes 589832 | tf_op jit(solution)/shard_map/ppermute | solution.py:218
  30.3 1.7 %collective-permute-start.9 = (bf16[24,4096]{1,0:T(8,128)(2,1)S(1)}, bf16[24,4096]{1,0:T(8,128)(2,1)S(1)}, u32[]{:S(2)}, u32[]{:S(2)}) collective-permute-start(bf16[24,4096]{1,0:T(8,128)(2,1)S(1)} %collective-permute-done.5.refs_3_), channel_id=1, source_target_pairs={{0,1},{1,0},{2,3},{3,2},{4,5},{5,4},{6,7},{7,6},{8,9},{9,8},{10,11... | collective-permute-start | bytes 589832 | tf_op jit(solution)/shard_map/ppermute | solution.py:218
  32.0 4.6 %copy-start = (bf16[1,4096,1536]{2,1,0:T(8,128)(2,1)S(1)}, bf16[1,4096,1536]{2,1,0:T(8,128)(2,1)}, u32[]{:S(2)}) copy-start(bf16[1,4096,1536]{2,1,0:T(8,128)(2,1)} %param.9) | copy-start | bytes 37748740
  36.6 4.6 %copy-start.1 = (bf16[1,4096,1536]{2,1,0:T(8,128)(2,1)S(1)}, bf16[1,4096,1536]{2,1,0:T(8,128)(2,1)}, u32[]{:S(2)}) copy-start(bf16[1,4096,1536]{2,1,0:T(8,128)(2,1)} %param.10) | copy-start | bytes 37748740
  41.2 6.2 %slice-start.1 = ((s8[12582912]{0:T(1024)(128)(4,1)}), s8[4194304]{0:T(1024)(128)(4,1)S(1)}, s32[]{:S(2)}) async-start(s8[12582912]{0:T(1024)(128)(4,1)} %bitcast.3), calls=%async_computation.1 | async-start | bytes 8388608
  41.2 6.2 %slice-start.2 = ((s8[12582912]{0:T(1024)(128)(4,1)}), s8[4194304]{0:T(1024)(128)(4,1)S(1)}, s32[]{:S(2)}) async-start(s8[12582912]{0:T(1024)(128)(4,1)} %bitcast.3), calls=%async_computation.2 | async-start | bytes 8388608
  51.3 2.4 %collective-permute-start.10 = (bf16[96,4096]{1,0:T(8,128)(2,1)S(1)}, bf16[96,4096]{1,0:T(8,128)(2,1)S(1)}, u32[]{:S(2)}, u32[]{:S(2)}) collective-permute-start(bf16[96,4096]{1,0:T(8,128)(2,1)S(1)} %get-tuple-element.24), channel_id=1, source_target_pairs={{0,1},{1,0},{2,3},{3,2},{4,5},{5,4},{6,7},{7,6},{8,9},{9,8},{10,11... | collective-permute-start | bytes 2359304 | tf_op jit(solution)/shard_map/ppermute | solution.py:218
  53.8 7.8 %collective-permute-start.11 = (bf16[24,4096]{1,0:T(8,128)(2,1)S(1)}, bf16[24,4096]{1,0:T(8,128)(2,1)S(1)}, u32[]{:S(2)}, u32[]{:S(2)}) collective-permute-start(bf16[24,4096]{1,0:T(8,128)(2,1)S(1)} %get-tuple-element.26), channel_id=1, source_target_pairs={{0,2},{1,3},{2,0},{3,1},{4,6},{5,7},{6,4},{7,5},{8,10},{9,11},{10,... | collective-permute-start | bytes 589832 | tf_op jit(solution)/shard_map/ppermute | solution.py:214
  54.8 9.6 %collective-permute-start.12 = (bf16[24,4096]{1,0:T(8,128)(2,1)S(1)}, bf16[24,4096]{1,0:T(8,128)(2,1)S(1)}, u32[]{:S(2)}, u32[]{:S(2)}) collective-permute-start(bf16[24,4096]{1,0:T(8,128)(2,1)S(1)} %get-tuple-element.27), channel_id=1, source_target_pairs={{0,4},{1,5},{2,6},{3,7},{4,0},{5,1},{6,2},{7,3},{8,12},{9,13},{10,... | collective-permute-start | bytes 589832 | tf_op jit(solution)/shard_map/ppermute | solution.py:214
  55.9 10.2 %collective-permute-start.13 = (bf16[24,4096]{1,0:T(8,128)(2,1)S(1)}, bf16[24,4096]{1,0:T(8,128)(2,1)S(1)}, u32[]{:S(2)}, u32[]{:S(2)}) collective-permute-start(bf16[24,4096]{1,0:T(8,128)(2,1)S(1)} %get-tuple-element.28), channel_id=1, source_target_pairs={{0,6},{1,7},{2,4},{3,5},{4,2},{5,3},{6,0},{7,1},{8,14},{9,15},{10,... | collective-permute-start | bytes 589832 | tf_op jit(solution)/shard_map/ppermute | solution.py:214
  67.0 5.3 %collective-permute-start.14 = (bf16[8,6144]{1,0:T(8,128)(2,1)S(1)}, bf16[8,6144]{1,0:T(8,128)(2,1)S(1)}, u32[]{:S(2)}, u32[]{:S(2)}) collective-permute-start(bf16[8,6144]{1,0:T(8,128)(2,1)S(1)} %get-tuple-element.30), channel_id=1, source_target_pairs={{0,24},{8,0},{16,8},{24,16},{1,25},{9,1},{17,9},{25,17},{2,26},{10... | collective-permute-start | bytes 294920 | tf_op jit(solution)/shard_map/ppermute | solution.py:242
  67.7 10.2 %collective-permute-start.15 = (bf16[8,6144]{1,0:T(8,128)(2,1)S(1)}, bf16[8,6144]{1,0:T(8,128)(2,1)S(1)}, u32[]{:S(2)}, u32[]{:S(2)}) collective-permute-start(bf16[8,6144]{1,0:T(8,128)(2,1)S(1)} %get-tuple-element.31), channel_id=1, source_target_pairs={{0,16},{8,24},{16,0},{24,8},{1,17},{9,25},{17,1},{25,9},{2,18},{10... | collective-permute-start | bytes 294920 | tf_op jit(solution)/shard_map/ppermute | solution.py:242
  69.2 8.6 %collective-permute-start.16 = (bf16[8,6144]{1,0:T(8,128)(2,1)S(1)}, bf16[8,6144]{1,0:T(8,128)(2,1)S(1)}, u32[]{:S(2)}, u32[]{:S(2)}) collective-permute-start(bf16[8,6144]{1,0:T(8,128)(2,1)S(1)} %get-tuple-element.32), channel_id=1, source_target_pairs={{0,8},{8,16},{16,24},{24,0},{1,9},{9,17},{17,25},{25,1},{2,10},{10... | collective-permute-start | bytes 294920 | tf_op jit(solution)/shard_map/ppermute | solution.py:242

commit v2 on v1

v2 whole, which is shorter than its diff:
```python
import functools

import jax
import jax.numpy as jnp
from jax import lax
from jax.experimental import pallas as pl
from jax.experimental.pallas import tpu as pltpu
from jax.sharding import PartitionSpec as P

BF = jnp.bfloat16
F32 = jnp.float32
LANES = 128
SUB = 8
FOLD = 16
UNIT_TILE = 256
PIECES = 8
PARTS = 2


def whole(memory_space=pltpu.VMEM):
    return pl.BlockSpec(memory_space=memory_space)


def pinned(array):
    return pltpu.with_memory_space_constraint(array, pltpu.HBM)


def call(body, outs, args, name, spaces=None, scratch=(), limit=12, flops=0, moved=0):
    spaces = spaces or [pltpu.VMEM] * len(args)
    return pl.pallas_call(
        body,
        out_shape=[jax.ShapeDtypeStruct(s, BF) if isinstance(s, tuple) else s for s in outs],
        in_specs=[whole(s) for s in spaces],
        out_specs=[whole() for _ in outs],
        scratch_shapes=list(scratch),
        name=name,
        compiler_params=pltpu.CompilerParams(vmem_limit_bytes=limit << 20),
        cost_estimate=pl.CostEstimate(flops=flops, bytes_accessed=moved, transcendentals=0),
    )(*args)


def by_core(first, second):
    core = lax.axis_index("dev") % 2
    pl.when(core == 0)(first)
    pl.when(core == 1)(second)


def padded(rows):
    missing = -rows.shape[0] % SUB
    return jnp.concatenate([rows, jnp.zeros((missing, rows.shape[1]), rows.dtype)], 0) if missing else rows


def weigh_rows(weights, value, span):
    total = lax.dot_general(weights, value, (((0,), (0,)), ((), ())), preferred_element_type=F32)
    return total[:span] + total[span : 2 * span] + total[2 * span :]


def pack_body(experts, slots, ids_hbm, combine_hbm, x_hbm, *refs):
    outs, table_out, (ids_ref, combine_ref, x_ref, sems) = refs[:-5], refs[-5], refs[-4:]
    copies = [
        pltpu.make_async_copy(source, target, sems.at[i])
        for i, (source, target) in enumerate(((ids_hbm, ids_ref), (combine_hbm, combine_ref), (x_hbm, x_ref)))
    ]
    for copy in copies:
        copy.start()
    rows, steps, width = x_ref.shape
    half = width // 2
    pair = steps * slots
    own = lax.axis_index("dev") // 2
    table_rows = experts * pair
    row_at = lax.broadcasted_iota(jnp.int32, (table_rows, LANES), 0)
    lane = lax.broadcasted_iota(jnp.int32, (table_rows, LANES), 1)
    group, place = lane // FOLD, lane % FOLD
    low = jnp.where((group == 1) & (place >= 12), place - 4, jnp.where((group == 1) & (place >= SUB), -1, place))
    table = jnp.zeros((table_rows, LANES), F32)
    copies[0].wait()
    copies[1].wait()
    for t in range(steps):
        counts = [jnp.int32(0)] * experts
        for r in range(rows):
            for k in range(2):
                e = ids_ref[t, k, r]
                position = jnp.int32(0)
                for c in range(experts):
                    position = jnp.where(e == c, counts[c], position)
                counts = [counts[c] + (e == c).astype(jnp.int32) for c in range(experts)]
                slot = ((e ^ own) * steps + t) * slots + position
                hit = (row_at == slot) & (low == r * steps + t)
                table = jnp.where(hit, combine_ref[t, k, r], table)
    ones = jnp.where(table != 0.0, 1.0, 0.0)
    high = table.astype(BF).astype(F32)
    middle = (table - high).astype(BF).astype(F32)
    rest = table - high - middle
    coded = jnp.where(
        group <= 1, ones, jnp.where(group == 2, high, jnp.where(group == 3, middle, jnp.where(group == 4, rest, 0.0)))
    ).astype(BF)
    table_out[...] = coded
    copies[2].wait()
    flat = jnp.concatenate([x_ref[r].astype(F32) for r in range(rows)], 0)

    def first():
        tail = flat[SUB:]
        top = flat[:SUB].astype(BF)
        fold = jnp.concatenate([tail[:, :half], tail[:, half:]], 0).astype(BF)
        for out in outs:
            out[:, :width] = top
            out[:, width : width + half] = fold
            for b in range(table_rows // SUB):
                start = width + half + b * LANES
                out[:, start : start + LANES] = coded[b * SUB : (b + 1) * SUB]

    def second():
        source = jnp.concatenate([flat, jnp.zeros((FOLD - flat.shape[0], width), F32)], 0).astype(BF)
        got = jnp.dot(coded[:, :FOLD], source, preferred_element_type=F32)
        for j, out in enumerate(outs):
            if j < experts:
                out[:, :width] = padded(got[j * pair : (j + 1) * pair]).astype(BF)
            else:
                out[:, :width] = jnp.zeros((SUB, width), BF)
            out[:, width:] = jnp.zeros((SUB, out.shape[1] - width), BF)

    by_core(first, second)


def tables_of(packed, experts, pair, width, group):
    base = width + width // 2
    members = len(packed)
    table_rows = experts * pair
    total = table_rows * members
    blocks = []
    for k, ref in enumerate(packed):
        tab = jnp.concatenate(
            [ref[:, base + b * LANES : base + (b + 1) * LANES] for b in range(table_rows // SUB)], 0
        ).astype(F32)
        at = k % (LANES // FOLD)
        shift = (at - group) * FOLD % LANES
        moved = pltpu.roll(tab, shift, 1) if shift else tab
        lane = lax.broadcasted_iota(jnp.int32, moved.shape, 1)
        moved = jnp.where(lane // FOLD == at, moved, 0.0)
        tiles = [jnp.zeros_like(moved)] * -(-members * FOLD // LANES)
        tiles[k * FOLD // LANES] = moved
        blocks.append(jnp.concatenate(tiles, 1))
    stacked = jnp.concatenate(blocks, 0).astype(BF)
    to = lax.broadcasted_iota(jnp.int32, (total, total), 0)
    source = lax.broadcasted_iota(jnp.int32, (total, total), 1)
    e, k, p = to // (members * pair), to // pair % members, to % pair
    order = jnp.where(source == k * table_rows + e * pair + p, 1.0, 0.0).astype(BF)
    return jnp.dot(order, stacked, preferred_element_type=F32).astype(BF)[:, : members * FOLD]


def route_body(members, experts, pair, _, *refs):
    count = len(refs) // 2
    packed, outs = refs[:count], refs[count:]
    width = outs[0].shape[1]
    half = width // 2

    def first():
        block = members * pair
        for side in range(2):
            cols = slice(side * half, (side + 1) * half)
            pick = tables_of(packed[:members], experts, pair, width, side)
            rows = jnp.concatenate(
                [part for ref in packed[:members] for part in (ref[:, cols], ref[:, width : width + half])], 0
            )
            got = jnp.dot(pick, rows, preferred_element_type=F32).astype(BF)
            for j in range(experts):
                outs[j][:block, cols] = got[j * block : (j + 1) * block]

    def second():
        rows = jnp.concatenate([ref[:, :width].astype(F32)[:pair] for ref in packed[:experts]], 0).astype(BF)
        for k in range(members):
            outs[k][: experts * pair] = rows

    by_core(first, second)


def weigh_body(experts, pair, width, *refs):
    packed, out = refs[:-1], refs[-1]
    out[...] = jnp.concatenate([tables_of(packed, experts, pair, width, g) for g in (2, 3, 4)], 1)


def weight_copies(source, target, sems, first):
    size = target.shape[0] // PIECES
    return [
        pltpu.make_async_copy(source.at[0, pl.ds(p * size, size)], target.at[pl.ds(p * size, size)], sems.at[first + p])
        for p in range(PIECES)
    ]


def fetch_body(count, *refs):
    sources, targets, sems = refs[:count], refs[count + 1 : -1], refs[-1]
    copies = []
    for i, (source, target) in enumerate(zip(sources, targets)):
        copies += weight_copies(source, target, sems, i * PIECES)
    for copy in copies:
        copy.start()
    for copy in copies:
        copy.wait()


def fetch(weights, after, name):
    return call(
        functools.partial(fetch_body, len(weights)),
        [pltpu.VMEM(w.shape[1:], BF) for w in weights],
        (*[pinned(w) for w in weights], after),
        name,
        [pltpu.HBM] * len(weights) + [pl.ANY],
        [pltpu.SemaphoreType.DMA((PIECES * len(weights),))],
        limit=1,
        moved=sum(2 * w.size for w in weights),
    )


def up_body(members, experts, pair, *refs):
    count = (len(refs) - 7) // 2
    mine, theirs, refs = refs[:count], refs[count : 2 * count], refs[2 * count :]
    gate_ref, up_ref, down_hbm, hidden_ref, down_ref, rows_ref, sems = refs
    copies = weight_copies(down_hbm, down_ref, sems, 0)
    for copy in copies:
        copy.start()

    def parts(core, blocks):
        number, size = ((experts, members * pair), (members, experts * pair))[core]
        return [b[:size] for b in blocks[:number]]

    def fill(core):
        rows_ref[...] = jnp.concatenate(parts(core, mine) + parts(1 - core, theirs), 0)

    if members == experts:
        fill(0)
    else:
        by_core(lambda: fill(0), lambda: fill(1))
    for j in range(hidden_ref.shape[1] // UNIT_TILE):
        cols = slice(j * UNIT_TILE, (j + 1) * UNIT_TILE)
        gate = jnp.dot(rows_ref[...], gate_ref[:, cols], preferred_element_type=F32)
        up = jnp.dot(rows_ref[...], up_ref[:, cols], preferred_element_type=F32)
        hidden_ref[:, cols] = (jax.nn.silu(gate) * up).astype(BF)
    for copy in copies:
        copy.wait()


def down_body(part, hidden_ref, down_ref, own_ref, other_ref):
    mine, width = own_ref.shape
    tile = min(512, width)
    for j in range(width // tile):
        cols = slice(j * tile, (j + 1) * tile)
        at = slice(part * width + j * tile, part * width + (j + 1) * tile)
        value = jnp.dot(hidden_ref[...], down_ref[:, at], preferred_element_type=F32).astype(BF)
        own_ref[:, cols] = value[:mine]
        other_ref[:, cols] = value[mine:]


def add_body(members, experts, pair, *refs):
    owns, gots, outs = refs[:PARTS], refs[PARTS : 2 * PARTS], refs[2 * PARTS :]
    width = owns[0].shape[1]

    def split(core):
        number, size = ((experts, members * pair), (members, experts * pair))[core]
        for j in range(number):
            at = slice(j * size, (j + 1) * size)
            for p in range(PARTS):
                cols = slice(p * width, (p + 1) * width)
                outs[j][:size, cols] = (owns[p][at].astype(F32) + gots[p][at].astype(F32)).astype(BF)

    if members == experts:
        split(0)
    else:
        by_core(lambda: split(0), lambda: split(1))


def blend_body(members, experts, pair, weights_ref, *refs):
    count = len(refs) // 2
    values, outs = refs[:count], refs[count:]
    width = values[0].shape[1]
    half = width // 2

    def first():
        tails = []
        for side in range(2):
            cols = slice(side * half, (side + 1) * half)
            value = jnp.concatenate([v[: members * pair, cols] for v in values[:experts]], 0)
            total = weigh_rows(weights_ref[...], value, members * FOLD)
            for k in range(members):
                outs[k][:, cols] = total[k * FOLD : k * FOLD + SUB].astype(BF)
            tails.append([total[k * FOLD + SUB : k * FOLD + SUB + 4] for k in range(members)])
        for k in range(members):
            outs[k][:, width:] = jnp.concatenate([tails[0][k], tails[1][k]], 0).astype(BF)

    def second():
        total = values[0][: experts * pair].astype(F32)
        for v in values[1:members]:
            total = total + v[: experts * pair].astype(F32)
        for j in range(experts):
            outs[j][:, :width] = padded(total[j * pair : (j + 1) * pair]).astype(BF)
            outs[j][:, width:] = jnp.zeros((SUB, half), BF)

    by_core(first, second)


def finish_body(members, experts, pair, table_ref, *refs):
    parts, out_ref = refs[:-1], refs[-1]
    rows, steps, width = out_ref.shape
    half = width // 2

    def write(flat):
        for r in range(rows):
            out_ref[r] = flat[r * steps : (r + 1) * steps].astype(BF)

    def first():
        total = parts[0][...].astype(F32)
        for p in parts[1:members]:
            total = total + p[...].astype(F32)
        tail = total[:, width:]
        tail = jnp.concatenate([tail[:4], tail[4:]], 1)
        write(jnp.concatenate([total[:, :width], tail], 0))

    def second():
        value = jnp.concatenate([p[:, :width].astype(F32)[:pair] for p in parts[:experts]], 0).astype(BF)
        write(weigh_rows(table_ref[:, 2 * FOLD : 5 * FOLD], value, FOLD))

    by_core(first, second)


def local(expert_input, expert_ids, combine, gate_weight, up_weight, down_weight):
    members = lax.axis_size("group")
    devices = lax.axis_size("dev")
    experts = devices // 2
    steps, row_count, width = expert_input.shape
    slots = max(2, (2 * row_count + experts - 1) // experts)
    pair = steps * slots
    folded = width + width // 2
    table_rows = experts * pair
    packed_width = folded + table_rows // SUB * LANES
    count = max(members, experts)
    block = count * pair
    rows_half = members * experts * pair
    hidden_units = gate_weight.shape[2]

    def send(arrays, group_core, back):
        got = {0: arrays[0]}
        for i in sorted(range(1, count), key=lambda i: -min(i, count - i)):
            pairs = []
            for g in range(members):
                for d in range(devices):
                    if d % 2 == group_core:
                        if i < members:
                            pairs.append((g * devices + d, (g + (-i if back else i)) % members * devices + d))
                    elif i < experts:
                        pairs.append((g * devices + d, g * devices + (d ^ (2 * i))))
            got[i] = lax.ppermute(arrays[i], ("group", "dev"), pairs)
        return [got[i] for i in range(count)]

    def swap(array):
        return lax.ppermute(array, "dev", [(i, i ^ 1) for i in range(devices)])

    x = expert_input.transpose(1, 0, 2)
    ids = expert_ids.transpose(0, 2, 1)
    scale = combine.transpose(0, 2, 1)
    *packed, table = call(
        functools.partial(pack_body, experts, slots),
        [(SUB, packed_width)] * count + [(table_rows, LANES)],
        [pinned(a) for a in (ids, scale, x)],
        "pack",
        [pltpu.HBM] * 3,
        [
            pltpu.SMEM(ids.shape, ids.dtype),
            pltpu.SMEM(scale.shape, scale.dtype),
            pltpu.VMEM(x.shape, x.dtype),
            pltpu.SemaphoreType.DMA((3,)),
        ],
    )
    (gate,) = fetch([gate_weight], packed[0], "fetch_gate")
    arrived = send(packed, 0, False)
    routed = call(
        functools.partial(route_body, members, experts, pair),
        [(block, width)] * count,
        (gate, *arrived),
        "route",
        [pl.ANY] + [pltpu.VMEM] * count,
    )
    (up,) = fetch([up_weight], routed[0], "fetch_up")
    mine = send(routed, 1, False)
    mine[-1], up = lax.optimization_barrier((mine[-1], up))
    theirs = [swap(a) for a in mine]
    (weights,) = call(
        functools.partial(weigh_body, experts, pair, width),
        [(rows_half, 3 * members * FOLD)],
        arrived[:members],
        "weigh",
    )
    hidden, down = call(
        functools.partial(up_body, members, experts, pair),
        [(2 * rows_half, hidden_units), pltpu.VMEM(down_weight.shape[1:], BF)],
        (*mine, *theirs, gate, up, pinned(down_weight)),
        "gate_up",
        [pltpu.VMEM] * (2 * count + 2) + [pltpu.HBM],
        scratch=[pltpu.VMEM((2 * rows_half, width), BF), pltpu.SemaphoreType.DMA((PIECES,))],
        flops=8 * rows_half * width * hidden_units,
    )
    owns, others = [], []
    for p in range(PARTS):
        own, other = call(
            functools.partial(down_body, p),
            [(rows_half, width // PARTS)] * 2,
            (hidden, down),
            "down_%d" % p,
            flops=4 * rows_half * width * hidden_units // PARTS,
        )
        owns.append(own)
        others.append(swap(other))
    halves = call(
        functools.partial(add_body, members, experts, pair), [(block, width)] * count, (*owns, *others), "add"
    )
    returned = send(halves, 1, True)
    blended = call(
        functools.partial(blend_body, members, experts, pair), [(SUB, folded)] * count, (weights, *returned), "blend"
    )
    final = send(blended, 0, True)
    (out,) = call(
        functools.partial(finish_body, members, experts, pair), [(row_count, steps, width)], (table, *final), "finish"
    )
    return out.transpose(1, 0, 2)


def solution(mesh):
    in_specs = (
        P(None, ("group", "dev"), None),
        P(None, ("group", "dev"), None),
        P(None, ("group", "dev"), None),
        P("dev", None, "group"),
        P("dev", None, "group"),
        P("dev", "group", None),
    )
    out_specs = P(None, ("group", "dev"), None)
    return jax.shard_map(local, mesh=mesh, in_specs=in_specs, out_specs=out_specs, check_vma=False)
```

time: 78.9 us -> 57.8 us (0.73)
  waiting for transfers between devices: 35.1 us -> 16.2 us
  local copies, waits for them, and re-layouts: 12.4 us -> 0 us
  Pallas kernels: 12.9 us -> 23.4 us
    ppermute x12, waiting for transfers between devices: 31.8 us -> 13 us  [send(): got[i] = lax.ppermute(arrays[i], ('group', 'dev'), pairs)]
    unnamed x13 -> x0, local copies, waits for them, and re-layouts: 11.7 us -> none
    pallas_call x7 -> x11, Pallas kernels: 12.9 us -> 23.4 us  [call(): pl.pallas_call(body, out_shape=[jax.ShapeDtypeStruct(s, BF) if isinstance...]
    ppermute x12, starting transfers between devices: 17.4 us -> 16.6 us  [send(): got[i] = lax.ppermute(arrays[i], ('group', 'dev'), pairs)]
    ppermute x5 -> x6, waiting for transfers between devices: 3.26 us -> 3.21 us  [swap(): return lax.ppermute(array, 'dev', [(i, i ^ 1) for i in range(devices)])]
  transfers between devices with their start and end apart: 17 -> 18, of which waited for: 12 -> 11; matrix products, arithmetic and copies ran while one was open for 0% -> 0% of each run, Pallas kernels for 0% -> 17%
where the time goes in v2:
time: 57.8 us; the launch traced here: 57.6 us
  Pallas kernels  23.4 us (40%)
  starting transfers between devices  17.9 us (31%)
  waiting for transfers between devices  16.2 us (28%)
    pallas_call x11, Pallas kernels, call(): pl.pallas_call(body, out_shape=[jax.ShapeDtypeStruct(s, BF) if isinstance...  23.4 us
    ppermute x12, starting transfers between devices, send(): got[i] = lax.ppermute(arrays[i], ('group', 'dev'), pairs)  16.6 us
    ppermute x12, waiting for transfers between devices, send(): got[i] = lax.ppermute(arrays[i], ('group', 'dev'), pairs)  13 us
    ppermute x6, waiting for transfers between devices, swap(): return lax.ppermute(array, 'dev', [(i, i ^ 1) for i in range(devices)])  3.21 us
    ppermute x6, starting transfers between devices, swap(): return lax.ppermute(array, 'dev', [(i, i ^ 1) for i in range(devices)])  1.32 us
  transfers between devices with their start and end apart: 18, of which 11 were waited for; matrix products, arithmetic and copies ran while one was open for 0% of the time, Pallas kernels for 17%

profile of v2, /device:TPU:0, one launch (start us, length us, event | category | flops | bytes accessed | tf_op | source)
XLA Modules:
  0.0 57.6 jit_solution(14790497274990237882)
XLA Ops:
  0.0 1.0 %pack.1 = (bf16[8,6528]{1,0:T(8,128)(2,1)S(1)}, bf16[8,6528]{1,0:T(8,128)(2,1)S(1)}, bf16[8,6528]{1,0:T(8,128)(2,1)S(1)}, bf16[8,6528]{1,0:T(8,128)(2,1)S(1)}, bf16[24,128]{1,0:T(8,128)(2,1)S(1)}) custom-call(s32[2,2,6]{2,1,0:T(2,128)} %bitcast.5, f32[2,2,6]{2,1,0:T(2,128)} %bitcast.6, bf16[6,2,4096]{2,1,0:T(2,128)(2,1)} %bitcast.4), custom_call_target="tpu_custom_call" | custom-call | tf_op jit(solution)/shard_map/pack/pallas_call | solution.py:30
  1.0 3.1 %collective-permute-start = (bf16[8,6528]{1,0:T(8,128)(2,1)S(1)}, bf16[8,6528]{1,0:T(8,128)(2,1)S(1)}, u32[]{:S(2)}, u32[]{:S(2)}) collective-permute-start(bf16[8,6528]{1,0:T(8,128)(2,1)S(1)} %get-tuple-element.32), channel_id=1, source_target_pairs={{0,8},{1,3},{2,10},{3,1},{4,12},{5,7},{6,14},{7,5},{8,16},{9,11},{... | collective-permute-start | bytes 313352 | tf_op jit(solution)/shard_map/ppermute | solution.py:350
  4.1 2.6 %collective-permute-start.1 = (bf16[8,6528]{1,0:T(8,128)(2,1)S(1)}, bf16[8,6528]{1,0:T(8,128)(2,1)S(1)}, u32[]{:S(2)}, u32[]{:S(2)}) collective-permute-start(bf16[8,6528]{1,0:T(8,128)(2,1)S(1)} %get-tuple-element.33), channel_id=1, source_target_pairs={{0,16},{1,5},{2,18},{3,7},{4,20},{5,1},{6,22},{7,3},{8,24},{9,13},... | collective-permute-start | bytes 313352 | tf_op jit(solution)/shard_map/ppermute | solution.py:350
  6.7 1.3 %collective-permute-start.2 = (bf16[8,6528]{1,0:T(8,128)(2,1)S(1)}, bf16[8,6528]{1,0:T(8,128)(2,1)S(1)}, u32[]{:S(2)}, u32[]{:S(2)}) collective-permute-start(bf16[8,6528]{1,0:T(8,128)(2,1)S(1)} %get-tuple-element.34), channel_id=1, source_target_pairs={{0,24},{1,7},{2,26},{3,5},{4,28},{5,3},{6,30},{7,1},{8,0},{9,15},{... | collective-permute-start | bytes 313352 | tf_op jit(solution)/shard_map/ppermute | solution.py:350
  8.1 4.7 %fetch_gate.1._.refs_8_ = bf16[4096,1536]{1,0:T(8,128)(2,1)S(1)} custom-call(bf16[1,4096,1536]{2,1,0:T(8,128)(2,1)} %refs_0_.2, bf16[8,6528]{1,0:T(8,128)(2,1)S(1)} %get-tuple-element.31.refs_0_.refs_1_), custom_call_target="tpu_custom_call" | custom-call | bytes 12582912 | tf_op jit(solution)/shard_map/fetch_gate/pallas_call | solution.py:30
  12.8 0.0 collective-permute-done.refs_1_
  12.8 0.0 collective-permute-done.1.refs_2_
  12.8 0.0 collective-permute-done.2.refs_3_
  12.8 0.7 %route.1 = (bf16[24,4096]{1,0:T(8,128)(2,1)S(1)}, bf16[24,4096]{1,0:T(8,128)(2,1)S(1)}, bf16[24,4096]{1,0:T(8,128)(2,1)S(1)}, bf16[24,4096]{1,0:T(8,128)(2,1)S(1)}) custom-call(bf16[4096,1536]{1,0:T(8,128)(2,1)S(1)} %fetch_gate.1._.refs_8_, bf16[8,6528]{1,0:T(8,128)(2,1)S(1)} %get-tuple-element.31.refs_0_.refs_1_, ...), custom_call_target="tpu_custom_call" | custom-call | tf_op jit(solution)/shard_map/route/pallas_call | solution.py:30
  13.5 2.5 %collective-permute-start.5 = (bf16[24,4096]{1,0:T(8,128)(2,1)S(1)}, bf16[24,4096]{1,0:T(8,128)(2,1)S(1)}, u32[]{:S(2)}, u32[]{:S(2)}) collective-permute-start(bf16[24,4096]{1,0:T(8,128)(2,1)S(1)} %get-tuple-element.38), channel_id=1, source_target_pairs={{0,6},{1,25},{2,4},{3,27},{4,2},{5,29},{6,0},{7,31},{8,14},{9,1},{... | collective-permute-start | bytes 589832 | tf_op jit(solution)/shard_map/ppermute | solution.py:350
  16.0 0.5 collective-permute-start.3
  16.5 0.5 collective-permute-start.4
  17.1 0.0 collective-permute-start.6
  17.1 4.7 %fetch_up.1.refs_9_ = bf16[4096,1536]{1,0:T(8,128)(2,1)S(1)} custom-call(bf16[1,4096,1536]{2,1,0:T(8,128)(2,1)} %refs_0_.3, bf16[24,4096]{1,0:T(8,128)(2,1)S(1)} %get-tuple-element.35.refs_1_.refs_0_), custom_call_target="tpu_custom_call" | custom-call | bytes 12582912 | tf_op jit(solution)/shard_map/fetch_up/pallas_call | solution.py:30
  21.8 0.0 collective-permute-done.5.refs_3_
  21.8 0.5 collective-permute-done.3.refs_1_
  22.3 0.1 collective-permute-start.7
  22.4 0.0 collective-permute-done.4.refs_2_
  22.4 0.7 %collective-permute-start.8 = (bf16[24,4096]{1,0:T(8,128)(2,1)S(1)}, bf16[24,4096]{1,0:T(8,128)(2,1)S(1)}, u32[]{:S(2)}, u32[]{:S(2)}) collective-permute-start(bf16[24,4096]{1,0:T(8,128)(2,1)S(1)} %collective-permute-done.4.refs_2_), channel_id=1, source_target_pairs={{0,1},{1,0},{2,3},{3,2},{4,5},{5,4},{6,7},{7,6},{8,9},{9,8},{10,11... | collective-permute-start | bytes 589832 | tf_op jit(solution)/shard_map/ppermute | solution.py:354
  23.0 0.0 collective-permute-start.9
  23.0 0.0 collective-permute-done.6.refs_4_
  23.0 0.7 %collective-permute-done.7.refs_5_ = bf16[24,4096]{1,0:T(8,128)(2,1)S(1)} collective-permute-done((bf16[24,4096]{1,0:T(8,128)(2,1)S(1)}, bf16[24,4096]{1,0:T(8,128)(2,1)S(1)}, u32[]{:S(2)}, u32[]{:S(2)}) %collective-permute-start.7) | collective-permute-done | bytes 196640 | tf_op jit(solution)/shard_map/ppermute | solution.py:354
  23.7 0.4 collective-permute-done.8.refs_6_
  24.1 0.4 collective-permute-done.9.refs_7_
  24.5 7.7 %gate_up.1 = (bf16[192,1536]{1,0:T(8,128)(2,1)S(1)}, bf16[1536,4096]{1,0:T(8,128)(2,1)S(1)}) custom-call(bf16[24,4096]{1,0:T(8,128)(2,1)S(1)} %get-tuple-element.35.refs_1_.refs_0_, bf16[24,4096]{1,0:T(8,128)(2,1)S(1)} %collective-permute-done.3.refs_1_, bf16[24,4096]{1,0:T(8,128)(2,1)S(1)} %collective-permute-done.4.refs_2_, ...), custom_call_target="tpu_custom_call" | custom-call | flops 4831838208 | tf_op jit(solution)/shard_map/gate_up/pallas_call | solution.py:30
  32.2 1.4 %down_1.1 = (bf16[96,2048]{1,0:T(8,128)(2,1)S(1)}, bf16[96,2048]{1,0:T(8,128)(2,1)S(1)}) custom-call(bf16[192,1536]{1,0:T(8,128)(2,1)S(1)} %get-tuple-element.41.hidden_ref, bf16[1536,4096]{1,0:T(8,128)(2,1)S(1)} %get-tuple-element.42.down_ref), custom_call_target="tpu_custom_call" | custom-call | flops 1207959552 | tf_op jit(solution)/shard_map/down_1/pallas_call | solution.py:30
  33.6 1.4 %down_0.1 = (bf16[96,2048]{1,0:T(8,128)(2,1)S(1)}, bf16[96,2048]{1,0:T(8,128)(2,1)S(1)}) custom-call(bf16[192,1536]{1,0:T(8,128)(2,1)S(1)} %get-tuple-element.41.hidden_ref, bf16[1536,4096]{1,0:T(8,128)(2,1)S(1)} %get-tuple-element.42.down_ref), custom_call_target="tpu_custom_call" | custom-call | flops 1207959552 | tf_op jit(solution)/shard_map/down_0/pallas_call | solution.py:30
  35.0 0.3 collective-permute-start.11
  35.4 0.2 collective-permute-start.10
  35.6 1.2 %collective-permute-done.11.refs_3_ = bf16[96,2048]{1,0:T(8,128)(2,1)S(1)} collective-permute-done((bf16[96,2048]{1,0:T(8,128)(2,1)S(1)}, bf16[96,2048]{1,0:T(8,128)(2,1)S(1)}, u32[]{:S(2)}, u32[]{:S(2)}) %collective-permute-start.11) | collective-permute-done | bytes 393248 | tf_op jit(solution)/shard_map/ppermute | solution.py:354
  36.8 0.6 collective-permute-done.10.refs_2_
  37.4 0.2 add.1
  37.6 1.5 %collective-permute-start.12 = (bf16[24,4096]{1,0:T(8,128)(2,1)S(1)}, bf16[24,4096]{1,0:T(8,128)(2,1)S(1)}, u32[]{:S(2)}, u32[]{:S(2)}) collective-permute-start(bf16[24,4096]{1,0:T(8,128)(2,1)S(1)} %get-tuple-element.48), channel_id=1, source_target_pairs={{0,2},{1,25},{2,0},{3,27},{4,6},{5,29},{6,4},{7,31},{8,10},{9,1},{... | collective-permute-start | bytes 589832 | tf_op jit(solution)/shard_map/ppermute | solution.py:350
  39.1 1.5 %collective-permute-start.13 = (bf16[24,4096]{1,0:T(8,128)(2,1)S(1)}, bf16[24,4096]{1,0:T(8,128)(2,1)S(1)}, u32[]{:S(2)}, u32[]{:S(2)}) collective-permute-start(bf16[24,4096]{1,0:T(8,128)(2,1)S(1)} %get-tuple-element.49), channel_id=1, source_target_pairs={{0,4},{1,17},{2,6},{3,19},{4,0},{5,21},{6,2},{7,23},{8,12},{9,25},... | collective-permute-start | bytes 589832 | tf_op jit(solution)/shard_map/ppermute | solution.py:350
  40.6 0.5 collective-permute-start.14
  41.1 0.3 weigh.1.weights_ref
  41.4 1.9 %collective-permute-done.12.refs_1_ = bf16[24,4096]{1,0:T(8,128)(2,1)S(1)} collective-permute-done((bf16[24,4096]{1,0:T(8,128)(2,1)S(1)}, bf16[24,4096]{1,0:T(8,128)(2,1)S(1)}, u32[]{:S(2)}, u32[]{:S(2)}) %collective-permute-start.12) | collective-permute-done | bytes 196640 | tf_op jit(solution)/shard_map/ppermute | solution.py:350
  43.3 2.7 %collective-permute-done.13.refs_2_ = bf16[24,4096]{1,0:T(8,128)(2,1)S(1)} collective-permute-done((bf16[24,4096]{1,0:T(8,128)(2,1)S(1)}, bf16[24,4096]{1,0:T(8,128)(2,1)S(1)}, u32[]{:S(2)}, u32[]{:S(2)}) %collective-permute-start.13) | collective-permute-done | bytes 196640 | tf_op jit(solution)/shard_map/ppermute | solution.py:350
  45.9 1.2 %collective-permute-done.14.refs_3_ = bf16[24,4096]{1,0:T(8,128)(2,1)S(1)} collective-permute-done((bf16[24,4096]{1,0:T(8,128)(2,1)S(1)}, bf16[24,4096]{1,0:T(8,128)(2,1)S(1)}, u32[]{:S(2)}, u32[]{:S(2)}) %collective-permute-start.14) | collective-permute-done | bytes 196640 | tf_op jit(solution)/shard_map/ppermute | solution.py:350
  47.2 0.6 %blend.1 = (bf16[8,6144]{1,0:T(8,128)(2,1)S(1)}, bf16[8,6144]{1,0:T(8,128)(2,1)S(1)}, bf16[8,6144]{1,0:T(8,128)(2,1)S(1)}, bf16[8,6144]{1,0:T(8,128)(2,1)S(1)}) custom-call(bf16[96,192]{1,0:T(8,128)(2,1)S(1)} %weigh.1.weights_ref, bf16[24,4096]{1,0:T(8,128)(2,1)S(1)} %get-tuple-element.47.refs_0_, bf16[24,4096]{1,0:T(8,128)(2,1)S(1)} %collective-permute-done.12.refs_1_, ...), custom_call_target="tpu_custom_call" | custom-call | tf_op jit(solution)/shard_map/blend/pallas_call | solution.py:30
  47.8 1.6 %collective-permute-start.15 = (bf16[8,6144]{1,0:T(8,128)(2,1)S(1)}, bf16[8,6144]{1,0:T(8,128)(2,1)S(1)}, u32[]{:S(2)}, u32[]{:S(2)}) collective-permute-start(bf16[8,6144]{1,0:T(8,128)(2,1)S(1)} %get-tuple-element.52), channel_id=1, source_target_pairs={{0,24},{1,3},{2,26},{3,1},{4,28},{5,7},{6,30},{7,5},{8,0},{9,11},{... | collective-permute-start | bytes 294920 | tf_op jit(solution)/shard_map/ppermute | solution.py:350
  49.4 0.2 collective-permute-start.16
  49.6 0.7 %collective-permute-start.17 = (bf16[8,6144]{1,0:T(8,128)(2,1)S(1)}, bf16[8,6144]{1,0:T(8,128)(2,1)S(1)}, u32[]{:S(2)}, u32[]{:S(2)}) collective-permute-start(bf16[8,6144]{1,0:T(8,128)(2,1)S(1)} %get-tuple-element.54), channel_id=1, source_target_pairs={{0,8},{1,7},{2,10},{3,5},{4,12},{5,3},{6,14},{7,1},{8,16},{9,15},{... | collective-permute-start | bytes 294920 | tf_op jit(solution)/shard_map/ppermute | solution.py:350
  50.3 2.2 %collective-permute-done.15.refs_1_ = bf16[8,6144]{1,0:T(8,128)(2,1)S(1)} collective-permute-done((bf16[8,6144]{1,0:T(8,128)(2,1)S(1)}, bf16[8,6144]{1,0:T(8,128)(2,1)S(1)}, u32[]{:S(2)}, u32[]{:S(2)}) %collective-permute-start.15) | collective-permute-done | bytes 98336 | tf_op jit(solution)/shard_map/ppermute | solution.py:350
  52.4 4.5 %collective-permute-done.16.refs_2_ = bf16[8,6144]{1,0:T(8,128)(2,1)S(1)} collective-permute-done((bf16[8,6144]{1,0:T(8,128)(2,1)S(1)}, bf16[8,6144]{1,0:T(8,128)(2,1)S(1)}, u32[]{:S(2)}, u32[]{:S(2)}) %collective-permute-start.16) | collective-permute-done | bytes 98336 | tf_op jit(solution)/shard_map/ppermute | solution.py:350
  56.9 0.0 collective-permute-done.17.refs_3_
  56.9 0.7 %finish.1 = bf16[6,2,4096]{2,1,0:T(2,128)(2,1)} custom-call(bf16[24,128]{1,0:T(8,128)(2,1)S(1)} %get-tuple-element.30.table_ref, bf16[8,6144]{1,0:T(8,128)(2,1)S(1)} %get-tuple-element.51.refs_0_, bf16[8,6144]{1,0:T(8,128)(2,1)S(1)} %collective-permute-done.15.refs_1_, bf16[8,6144]{1,0:T(8,128)(2,1)S(1)} %collective-permute-done.16.refs_2_, ...), custom_call_target="tpu_custom_call" | custom-call | tf_op jit(solution)/shard_map/finish/pallas_call | solution.py:30
Async XLA Ops:
  1.0 11.7 %collective-permute-start = (bf16[8,6528]{1,0:T(8,128)(2,1)S(1)}, bf16[8,6528]{1,0:T(8,128)(2,1)S(1)}, u32[]{:S(2)}, u32[]{:S(2)}) collective-permute-start(bf16[8,6528]{1,0:T(8,128)(2,1)S(1)} %get-tuple-element.32), channel_id=1, source_target_pairs={{0,8},{1,3},{2,10},{3,1},{4,12},{5,7},{6,14},{7,5},{8,16},{9,11},{... | collective-permute-start | bytes 313352 | tf_op jit(solution)/shard_map/ppermute | solution.py:350
  4.1 8.7 %collective-permute-start.1 = (bf16[8,6528]{1,0:T(8,128)(2,1)S(1)}, bf16[8,6528]{1,0:T(8,128)(2,1)S(1)}, u32[]{:S(2)}, u32[]{:S(2)}) collective-permute-start(bf16[8,6528]{1,0:T(8,128)(2,1)S(1)} %get-tuple-element.33), channel_id=1, source_target_pairs={{0,16},{1,5},{2,18},{3,7},{4,20},{5,1},{6,22},{7,3},{8,24},{9,13},... | collective-permute-start | bytes 313352 | tf_op jit(solution)/shard_map/ppermute | solution.py:350
  6.7 6.1 %collective-permute-start.2 = (bf16[8,6528]{1,0:T(8,128)(2,1)S(1)}, bf16[8,6528]{1,0:T(8,128)(2,1)S(1)}, u32[]{:S(2)}, u32[]{:S(2)}) collective-permute-start(bf16[8,6528]{1,0:T(8,128)(2,1)S(1)} %get-tuple-element.34), channel_id=1, source_target_pairs={{0,24},{1,7},{2,26},{3,5},{4,28},{5,3},{6,30},{7,1},{8,0},{9,15},{... | collective-permute-start | bytes 313352 | tf_op jit(solution)/shard_map/ppermute | solution.py:350
  13.5 8.3 %collective-permute-start.5 = (bf16[24,4096]{1,0:T(8,128)(2,1)S(1)}, bf16[24,4096]{1,0:T(8,128)(2,1)S(1)}, u32[]{:S(2)}, u32[]{:S(2)}) collective-permute-start(bf16[24,4096]{1,0:T(8,128)(2,1)S(1)} %get-tuple-element.38), channel_id=1, source_target_pairs={{0,6},{1,25},{2,4},{3,27},{4,2},{5,29},{6,0},{7,31},{8,14},{9,1},{... | collective-permute-start | bytes 589832 | tf_op jit(solution)/shard_map/ppermute | solution.py:350
  16.0 6.3 %collective-permute-start.3 = (bf16[24,4096]{1,0:T(8,128)(2,1)S(1)}, bf16[24,4096]{1,0:T(8,128)(2,1)S(1)}, u32[]{:S(2)}, u32[]{:S(2)}) collective-permute-start(bf16[24,4096]{1,0:T(8,128)(2,1)S(1)} %get-tuple-element.36), channel_id=1, source_target_pairs={{0,2},{1,9},{2,0},{3,11},{4,6},{5,13},{6,4},{7,15},{8,10},{9,17},{... | collective-permute-start | bytes 589832 | tf_op jit(solution)/shard_map/ppermute | solution.py:350
  16.5 5.8 %collective-permute-start.4 = (bf16[24,4096]{1,0:T(8,128)(2,1)S(1)}, bf16[24,4096]{1,0:T(8,128)(2,1)S(1)}, u32[]{:S(2)}, u32[]{:S(2)}) collective-permute-start(bf16[24,4096]{1,0:T(8,128)(2,1)S(1)} %get-tuple-element.37), channel_id=1, source_target_pairs={{0,4},{1,17},{2,6},{3,19},{4,0},{5,21},{6,2},{7,23},{8,12},{9,25},... | collective-permute-start | bytes 589832 | tf_op jit(solution)/shard_map/ppermute | solution.py:350
  17.1 6.0 %collective-permute-start.6 = (bf16[24,4096]{1,0:T(8,128)(2,1)S(1)}, bf16[24,4096]{1,0:T(8,128)(2,1)S(1)}, u32[]{:S(2)}, u32[]{:S(2)}) collective-permute-start(bf16[24,4096]{1,0:T(8,128)(2,1)S(1)} %get-tuple-element.35.refs_1_.refs_0_), channel_id=1, source_target_pairs={{0,1},{1,0},{2,3},{3,2},{4,5},{5,4},{6,7},{7,6},{8,9},{9,8},{10,11... | collective-permute-start | bytes 589832 | tf_op jit(solution)/shard_map/ppermute | solution.py:354
  22.3 1.4 %collective-permute-start.7 = (bf16[24,4096]{1,0:T(8,128)(2,1)S(1)}, bf16[24,4096]{1,0:T(8,128)(2,1)S(1)}, u32[]{:S(2)}, u32[]{:S(2)}) collective-permute-start(bf16[24,4096]{1,0:T(8,128)(2,1)S(1)} %collective-permute-done.3.refs_1_), channel_id=1, source_target_pairs={{0,1},{1,0},{2,3},{3,2},{4,5},{5,4},{6,7},{7,6},{8,9},{9,8},{10,11... | collective-permute-start | bytes 589832 | tf_op jit(solution)/shard_map/ppermute | solution.py:354
  22.4 1.7 %collective-permute-start.8 = (bf16[24,4096]{1,0:T(8,128)(2,1)S(1)}, bf16[24,4096]{1,0:T(8,128)(2,1)S(1)}, u32[]{:S(2)}, u32[]{:S(2)}) collective-permute-start(bf16[24,4096]{1,0:T(8,128)(2,1)S(1)} %collective-permute-done.4.refs_2_), channel_id=1, source_target_pairs={{0,1},{1,0},{2,3},{3,2},{4,5},{5,4},{6,7},{7,6},{8,9},{9,8},{10,11... | collective-permute-start | bytes 589832 | tf_op jit(solution)/shard_map/ppermute | solution.py:354
  23.0 1.4 %collective-permute-start.9 = (bf16[24,4096]{1,0:T(8,128)(2,1)S(1)}, bf16[24,4096]{1,0:T(8,128)(2,1)S(1)}, u32[]{:S(2)}, u32[]{:S(2)}) collective-permute-start(bf16[24,4096]{1,0:T(8,128)(2,1)S(1)} %collective-permute-done.5.refs_3_), channel_id=1, source_target_pairs={{0,1},{1,0},{2,3},{3,2},{4,5},{5,4},{6,7},{7,6},{8,9},{9,8},{10,11... | collective-permute-start | bytes 589832 | tf_op jit(solution)/shard_map/ppermute | solution.py:354
  35.0 1.8 %collective-permute-start.11 = (bf16[96,2048]{1,0:T(8,128)(2,1)S(1)}, bf16[96,2048]{1,0:T(8,128)(2,1)S(1)}, u32[]{:S(2)}, u32[]{:S(2)}) collective-permute-start(bf16[96,2048]{1,0:T(8,128)(2,1)S(1)} %get-tuple-element.46), channel_id=1, source_target_pairs={{0,1},{1,0},{2,3},{3,2},{4,5},{5,4},{6,7},{7,6},{8,9},{9,8},{10,11... | collective-permute-start | bytes 1179656 | tf_op jit(solution)/shard_map/ppermute | solution.py:354
  35.4 2.0 %collective-permute-start.10 = (bf16[96,2048]{1,0:T(8,128)(2,1)S(1)}, bf16[96,2048]{1,0:T(8,128)(2,1)S(1)}, u32[]{:S(2)}, u32[]{:S(2)}) collective-permute-start(bf16[96,2048]{1,0:T(8,128)(2,1)S(1)} %get-tuple-element.45), channel_id=1, source_target_pairs={{0,1},{1,0},{2,3},{3,2},{4,5},{5,4},{6,7},{7,6},{8,9},{9,8},{10,11... | collective-permute-start | bytes 1179656 | tf_op jit(solution)/shard_map/ppermute | solution.py:354
  37.6 5.7 %collective-permute-start.12 = (bf16[24,4096]{1,0:T(8,128)(2,1)S(1)}, bf16[24,4096]{1,0:T(8,128)(2,1)S(1)}, u32[]{:S(2)}, u32[]{:S(2)}) collective-permute-start(bf16[24,4096]{1,0:T(8,128)(2,1)S(1)} %get-tuple-element.48), channel_id=1, source_target_pairs={{0,2},{1,25},{2,0},{3,27},{4,6},{5,29},{6,4},{7,31},{8,10},{9,1},{... | collective-permute-start | bytes 589832 | tf_op jit(solution)/shard_map/ppermute | solution.py:350
  39.1 6.8 %collective-permute-start.13 = (bf16[24,4096]{1,0:T(8,128)(2,1)S(1)}, bf16[24,4096]{1,0:T(8,128)(2,1)S(1)}, u32[]{:S(2)}, u32[]{:S(2)}) collective-permute-start(bf16[24,4096]{1,0:T(8,128)(2,1)S(1)} %get-tuple-element.49), channel_id=1, source_target_pairs={{0,4},{1,17},{2,6},{3,19},{4,0},{5,21},{6,2},{7,23},{8,12},{9,25},... | collective-permute-start | bytes 589832 | tf_op jit(solution)/shard_map/ppermute | solution.py:350
  40.6 6.6 %collective-permute-start.14 = (bf16[24,4096]{1,0:T(8,128)(2,1)S(1)}, bf16[24,4096]{1,0:T(8,128)(2,1)S(1)}, u32[]{:S(2)}, u32[]{:S(2)}) collective-permute-start(bf16[24,4096]{1,0:T(8,128)(2,1)S(1)} %get-tuple-element.50), channel_id=1, source_target_pairs={{0,6},{1,9},{2,4},{3,11},{4,2},{5,13},{6,0},{7,15},{8,14},{9,17},{... | collective-permute-start | bytes 589832 | tf_op jit(solution)/shard_map/ppermute | solution.py:350
  47.8 4.7 %collective-permute-start.15 = (bf16[8,6144]{1,0:T(8,128)(2,1)S(1)}, bf16[8,6144]{1,0:T(8,128)(2,1)S(1)}, u32[]{:S(2)}, u32[]{:S(2)}) collective-permute-start(bf16[8,6144]{1,0:T(8,128)(2,1)S(1)} %get-tuple-element.52), channel_id=1, source_target_pairs={{0,24},{1,3},{2,26},{3,1},{4,28},{5,7},{6,30},{7,5},{8,0},{9,11},{... | collective-permute-start | bytes 294920 | tf_op jit(solution)/shard_map/ppermute | solution.py:350
  49.4 7.5 %collective-permute-start.16 = (bf16[8,6144]{1,0:T(8,128)(2,1)S(1)}, bf16[8,6144]{1,0:T(8,128)(2,1)S(1)}, u32[]{:S(2)}, u32[]{:S(2)}) collective-permute-start(bf16[8,6144]{1,0:T(8,128)(2,1)S(1)} %get-tuple-element.53), channel_id=1, source_target_pairs={{0,16},{1,5},{2,18},{3,7},{4,20},{5,1},{6,22},{7,3},{8,24},{9,13},... | collective-permute-start | bytes 294920 | tf_op jit(solution)/shard_map/ppermute | solution.py:350
  49.6 7.3 %collective-permute-start.17 = (bf16[8,6144]{1,0:T(8,128)(2,1)S(1)}, bf16[8,6144]{1,0:T(8,128)(2,1)S(1)}, u32[]{:S(2)}, u32[]{:S(2)}) collective-permute-start(bf16[8,6144]{1,0:T(8,128)(2,1)S(1)} %get-tuple-element.54), channel_id=1, source_target_pairs={{0,8},{1,7},{2,10},{3,5},{4,12},{5,3},{6,14},{7,1},{8,16},{9,15},{... | collective-permute-start | bytes 294920 | tf_op jit(solution)/shard_map/ppermute | solution.py:350

commit v3 on v2

--- a/solution.py
+++ b/solution.py
@@ -13,8 +13,18 @@
 SUB = 8
 FOLD = 16
 UNIT_TILE = 256
-PIECES = 8
-PARTS = 2
+CUTS = (0, 3, 4)
+BESIDE_TRANSFER = 10**10
+
+
+def group_peer(g, i, members, back):
+    if members & (members - 1) == 0:
+        return g ^ (-i % members)
+    return (g + (-i if back else i)) % members
+
+
+def plane_order(experts):
+    return [0] + sorted(range(1, experts), key=lambda j: (-bin(j).count("1"), j))
 
 
 def whole(memory_space=pltpu.VMEM):
@@ -25,7 +35,7 @@
     return pltpu.with_memory_space_constraint(array, pltpu.HBM)
 
 
-def call(body, outs, args, name, spaces=None, scratch=(), limit=12, flops=0, moved=0):
+def call(body, outs, args, name, spaces=None, scratch=(), limit=12, flops=0):
     spaces = spaces or [pltpu.VMEM] * len(args)
     return pl.pallas_call(
         body,
@@ -35,7 +45,7 @@
         scratch_shapes=list(scratch),
         name=name,
         compiler_params=pltpu.CompilerParams(vmem_limit_bytes=limit << 20),
-        cost_estimate=pl.CostEstimate(flops=flops, bytes_accessed=moved, transcendentals=0),
+        cost_estimate=pl.CostEstimate(flops=flops, bytes_accessed=0, transcendentals=0),
     )(*args)
 
 
@@ -67,6 +77,7 @@
     half = width // 2
     pair = steps * slots
     own = lax.axis_index("dev") // 2
+    offsets = plane_order(experts)
     table_rows = experts * pair
     row_at = lax.broadcasted_iota(jnp.int32, (table_rows, LANES), 0)
     lane = lax.broadcasted_iota(jnp.int32, (table_rows, LANES), 1)
@@ -84,7 +95,8 @@
                 for c in range(experts):
                     position = jnp.where(e == c, counts[c], position)
                 counts = [counts[c] + (e == c).astype(jnp.int32) for c in range(experts)]
-                slot = ((e ^ own) * steps + t) * slots + position
+                turn = sum(jnp.where((e ^ own) == offset, j, 0) for j, offset in enumerate(offsets))
+                slot = (turn * steps + t) * slots + position
                 hit = (row_at == slot) & (low == r * steps + t)
                 table = jnp.where(hit, combine_ref[t, k, r], table)
     ones = jnp.where(table != 0.0, 1.0, 0.0)
@@ -122,33 +134,37 @@
     by_core(first, second)
 
 
-def tables_of(packed, experts, pair, width, group):
+def tables_of(packed, experts, pair, width, groups):
     base = width + width // 2
     members = len(packed)
     table_rows = experts * pair
     total = table_rows * members
+    span = -(-members * FOLD // LANES) * LANES
     blocks = []
     for k, ref in enumerate(packed):
         tab = jnp.concatenate(
             [ref[:, base + b * LANES : base + (b + 1) * LANES] for b in range(table_rows // SUB)], 0
         ).astype(F32)
         at = k % (LANES // FOLD)
-        shift = (at - group) * FOLD % LANES
-        moved = pltpu.roll(tab, shift, 1) if shift else tab
-        lane = lax.broadcasted_iota(jnp.int32, moved.shape, 1)
-        moved = jnp.where(lane // FOLD == at, moved, 0.0)
-        tiles = [jnp.zeros_like(moved)] * -(-members * FOLD // LANES)
-        tiles[k * FOLD // LANES] = moved
+        here = lax.broadcasted_iota(jnp.int32, tab.shape, 1) // FOLD == at
+        tiles = []
+        for group in groups:
+            shift = (at - group) * FOLD % LANES
+            moved = jnp.where(here, pltpu.roll(tab, shift, 1) if shift else tab, 0.0)
+            row = [jnp.zeros_like(moved)] * (span // LANES)
+            row[k * FOLD // LANES] = moved
+            tiles += row
         blocks.append(jnp.concatenate(tiles, 1))
     stacked = jnp.concatenate(blocks, 0).astype(BF)
     to = lax.broadcasted_iota(jnp.int32, (total, total), 0)
     source = lax.broadcasted_iota(jnp.int32, (total, total), 1)
     e, k, p = to // (members * pair), to // pair % members, to % pair
     order = jnp.where(source == k * table_rows + e * pair + p, 1.0, 0.0).astype(BF)
-    return jnp.dot(order, stacked, preferred_element_type=F32).astype(BF)[:, : members * FOLD]
-
-
-def route_body(members, experts, pair, _, *refs):
+    all_groups = jnp.dot(order, stacked, preferred_element_type=F32).astype(BF)
+    return [all_groups[:, i * span : i * span + members * FOLD] for i in range(len(groups))]
+
+
+def route_body(members, experts, pair, *refs):
     count = len(refs) // 2
     packed, outs = refs[:count], refs[count:]
     width = outs[0].shape[1]
@@ -156,9 +172,8 @@
 
     def first():
         block = members * pair
-        for side in range(2):
+        for side, pick in enumerate(tables_of(packed[:members], experts, pair, width, (0, 1))):
             cols = slice(side * half, (side + 1) * half)
-            pick = tables_of(packed[:members], experts, pair, width, side)
             rows = jnp.concatenate(
                 [part for ref in packed[:members] for part in (ref[:, cols], ref[:, width : width + half])], 0
             )
@@ -176,48 +191,13 @@
 
 def weigh_body(experts, pair, width, *refs):
     packed, out = refs[:-1], refs[-1]
-    out[...] = jnp.concatenate([tables_of(packed, experts, pair, width, g) for g in (2, 3, 4)], 1)
-
-
-def weight_copies(source, target, sems, first):
-    size = target.shape[0] // PIECES
-    return [
-        pltpu.make_async_copy(source.at[0, pl.ds(p * size, size)], target.at[pl.ds(p * size, size)], sems.at[first + p])
-        for p in range(PIECES)
-    ]
-
-
-def fetch_body(count, *refs):
-    sources, targets, sems = refs[:count], refs[count + 1 : -1], refs[-1]
-    copies = []
-    for i, (source, target) in enumerate(zip(sources, targets)):
-        copies += weight_copies(source, target, sems, i * PIECES)
-    for copy in copies:
-        copy.start()
-    for copy in copies:
-        copy.wait()
-
-
-def fetch(weights, after, name):
-    return call(
-        functools.partial(fetch_body, len(weights)),
-        [pltpu.VMEM(w.shape[1:], BF) for w in weights],
-        (*[pinned(w) for w in weights], after),
-        name,
-        [pltpu.HBM] * len(weights) + [pl.ANY],
-        [pltpu.SemaphoreType.DMA((PIECES * len(weights),))],
-        limit=1,
-        moved=sum(2 * w.size for w in weights),
-    )
+    out[...] = jnp.concatenate(tables_of(packed, experts, pair, width, (2, 3, 4)), 1)
 
 
 def up_body(members, experts, pair, *refs):
-    count = (len(refs) - 7) // 2
+    count = (len(refs) - 4) // 2
     mine, theirs, refs = refs[:count], refs[count : 2 * count], refs[2 * count :]
-    gate_ref, up_ref, down_hbm, hidden_ref, down_ref, rows_ref, sems = refs
-    copies = weight_copies(down_hbm, down_ref, sems, 0)
-    for copy in copies:
-        copy.start()
+    gate_ref, up_ref, hidden_ref, rows_ref = refs
 
     def parts(core, blocks):
         number, size = ((experts, members * pair), (members, experts * pair))[core]
@@ -235,32 +215,32 @@
         gate = jnp.dot(rows_ref[...], gate_ref[:, cols], preferred_element_type=F32)
         up = jnp.dot(rows_ref[...], up_ref[:, cols], preferred_element_type=F32)
         hidden_ref[:, cols] = (jax.nn.silu(gate) * up).astype(BF)
-    for copy in copies:
-        copy.wait()
-
-
-def down_body(part, hidden_ref, down_ref, own_ref, other_ref):
+
+
+def down_body(first, hidden_ref, down_ref, own_ref, other_ref):
     mine, width = own_ref.shape
     tile = min(512, width)
     for j in range(width // tile):
         cols = slice(j * tile, (j + 1) * tile)
-        at = slice(part * width + j * tile, part * width + (j + 1) * tile)
+        at = slice(first + j * tile, first + (j + 1) * tile)
         value = jnp.dot(hidden_ref[...], down_ref[:, at], preferred_element_type=F32).astype(BF)
         own_ref[:, cols] = value[:mine]
         other_ref[:, cols] = value[mine:]
 
 
 def add_body(members, experts, pair, *refs):
-    owns, gots, outs = refs[:PARTS], refs[PARTS : 2 * PARTS], refs[2 * PARTS :]
-    width = owns[0].shape[1]
+    parts = len(CUTS) - 1
+    owns, gots, outs = refs[:parts], refs[parts : 2 * parts], refs[2 * parts :]
 
     def split(core):
         number, size = ((experts, members * pair), (members, experts * pair))[core]
         for j in range(number):
             at = slice(j * size, (j + 1) * size)
-            for p in range(PARTS):
-                cols = slice(p * width, (p + 1) * width)
-                outs[j][:size, cols] = (owns[p][at].astype(F32) + gots[p][at].astype(F32)).astype(BF)
+            first = 0
+            for own_ref, got_ref in zip(owns, gots):
+                cols = slice(first, first + own_ref.shape[1])
+                outs[j][:size, cols] = (own_ref[at].astype(F32) + got_ref[at].astype(F32)).astype(BF)
+                first += own_ref.shape[1]
 
     if members == experts:
         split(0)
@@ -336,6 +316,8 @@
     rows_half = members * experts * pair
     hidden_units = gate_weight.shape[2]
 
+    offsets = plane_order(experts)
+
     def send(arrays, group_core, back):
         got = {0: arrays[0]}
         for i in sorted(range(1, count), key=lambda i: -min(i, count - i)):
@@ -344,9 +326,9 @@
                 for d in range(devices):
                     if d % 2 == group_core:
                         if i < members:
-                            pairs.append((g * devices + d, (g + (-i if back else i)) % members * devices + d))
+                            pairs.append((g * devices + d, group_peer(g, i, members, back) * devices + d))
                     elif i < experts:
-                        pairs.append((g * devices + d, g * devices + (d ^ (2 * i))))
+                        pairs.append((g * devices + d, g * devices + (d ^ (2 * offsets[i]))))
             got[i] = lax.ppermute(arrays[i], ("group", "dev"), pairs)
         return [got[i] for i in range(count)]
 
@@ -368,19 +350,17 @@
             pltpu.VMEM(x.shape, x.dtype),
             pltpu.SemaphoreType.DMA((3,)),
         ],
-    )
-    (gate,) = fetch([gate_weight], packed[0], "fetch_gate")
+        flops=BESIDE_TRANSFER,
+    )
     arrived = send(packed, 0, False)
     routed = call(
         functools.partial(route_body, members, experts, pair),
         [(block, width)] * count,
-        (gate, *arrived),
+        arrived,
         "route",
-        [pl.ANY] + [pltpu.VMEM] * count,
-    )
-    (up,) = fetch([up_weight], routed[0], "fetch_up")
+        flops=BESIDE_TRANSFER,
+    )
     mine = send(routed, 1, False)
-    mine[-1], up = lax.optimization_barrier((mine[-1], up))
     theirs = [swap(a) for a in mine]
     (weights,) = call(
         functools.partial(weigh_body, experts, pair, width),
@@ -388,23 +368,24 @@
         arrived[:members],
         "weigh",
     )
-    hidden, down = call(
+    (hidden,) = call(
         functools.partial(up_body, members, experts, pair),
-        [(2 * rows_half, hidden_units), pltpu.VMEM(down_weight.shape[1:], BF)],
-        (*mine, *theirs, gate, up, pinned(down_weight)),
+        [(2 * rows_half, hidden_units)],
+        (*mine, *theirs, gate_weight[0], up_weight[0]),
         "gate_up",
-        [pltpu.VMEM] * (2 * count + 2) + [pltpu.HBM],
-        scratch=[pltpu.VMEM((2 * rows_half, width), BF), pltpu.SemaphoreType.DMA((PIECES,))],
+        [pltpu.VMEM] * (2 * count + 2),
+        scratch=[pltpu.VMEM((2 * rows_half, width), BF)],
         flops=8 * rows_half * width * hidden_units,
     )
     owns, others = [], []
-    for p in range(PARTS):
+    for p, (low, high) in enumerate(zip(CUTS, CUTS[1:])):
+        low, high = low * width // CUTS[-1], high * width // CUTS[-1]
         own, other = call(
-            functools.partial(down_body, p),
-            [(rows_half, width // PARTS)] * 2,
-            (hidden, down),
+            functools.partial(down_body, low),
+            [(rows_half, high - low)] * 2,
+            (hidden, down_weight[0]),
             "down_%d" % p,
-            flops=4 * rows_half * width * hidden_units // PARTS,
+            flops=4 * rows_half * (high - low) * hidden_units,
         )
         owns.append(own)
         others.append(swap(other))

time: 57.8 us -> 52.1 us (0.901)
  Pallas kernels: 23.4 us -> 11.5 us
  waiting for transfers between devices: 16.2 us -> 21.8 us
  starting transfers between devices: 17.9 us -> 18.5 us
    pallas_call x11 -> x9, Pallas kernels: 23.4 us -> 11.5 us  [call(): pl.pallas_call(body, out_shape=[jax.ShapeDtypeStruct(s, BF) if isinstance...]
    ppermute x12, waiting for transfers between devices: 13 us -> 19.5 us  [send(): got[i] = lax.ppermute(arrays[i], ('group', 'dev'), pairs)]
    ppermute x6, waiting for transfers between devices: 3.21 us -> 2.37 us  [swap(): return lax.ppermute(array, 'dev', [(i, i ^ 1) for i in range(devices)])]
    ppermute x12, starting transfers between devices: 16.6 us -> 17.3 us  [send(): got[i] = lax.ppermute(arrays[i], ('group', 'dev'), pairs)]
  transfers between devices with their start and end apart: 18 -> 18, of which waited for: 11 -> 12; matrix products, arithmetic and copies ran while one was open for 0% -> 0% of each run, Pallas kernels for 17% -> 2%
where the time goes in v3:
time: 52.1 us; the launch traced here: 52 us
  waiting for transfers between devices  21.8 us (42%)
  starting transfers between devices  18.5 us (36%)
  Pallas kernels  11.5 us (22%)
    ppermute x12, waiting for transfers between devices, send(): got[i] = lax.ppermute(arrays[i], ('group', 'dev'), pairs)  19.5 us
    ppermute x12, starting transfers between devices, send(): got[i] = lax.ppermute(arrays[i], ('group', 'dev'), pairs)  17.3 us
    pallas_call x9, Pallas kernels, call(): pl.pallas_call(body, out_shape=[jax.ShapeDtypeStruct(s, BF) if isinstance...  11.5 us
    ppermute x6, waiting for transfers between devices, swap(): return lax.ppermute(array, 'dev', [(i, i ^ 1) for i in range(devices)])  2.37 us
    ppermute x6, starting transfers between devices, swap(): return lax.ppermute(array, 'dev', [(i, i ^ 1) for i in range(devices)])  1.15 us
  transfers between devices with their start and end apart: 18, of which 12 were waited for; matrix products, arithmetic and copies ran while one was open for 0% of the time, Pallas kernels for 2%

profile of v3, /device:TPU:0, one launch (start us, length us, event | category | flops | bytes accessed | tf_op | source)
XLA Modules:
  0.0 52.0 jit_solution(12471948375541064741)
XLA Ops:
  0.0 0.0 slice-start.3
  0.0 0.0 slice-start.4
  0.0 0.0 slice-start.6
  0.0 0.0 slice-start.7
  0.0 1.2 %pack.1 = (bf16[8,6528]{1,0:T(8,128)(2,1)S(1)}, bf16[8,6528]{1,0:T(8,128)(2,1)S(1)}, bf16[8,6528]{1,0:T(8,128)(2,1)S(1)}, bf16[8,6528]{1,0:T(8,128)(2,1)S(1)}, bf16[24,128]{1,0:T(8,128)(2,1)S(1)}) custom-call(s32[2,2,6]{2,1,0:T(2,128)} %bitcast.18, f32[2,2,6]{2,1,0:T(2,128)} %bitcast.19, bf16[6,2,4096]{2,1,0:T(2,128)(2,1)} %bitcast.17), custom_call_target="tpu_custom_call" | custom-call | flops 10000000000 | tf_op jit(solution)/shard_map/pack/pallas_call | solution.py:40
  1.3 5.1 %collective-permute-start = (bf16[8,6528]{1,0:T(8,128)(2,1)S(1)}, bf16[8,6528]{1,0:T(8,128)(2,1)S(1)}, u32[]{:S(2)}, u32[]{:S(2)}) collective-permute-start(bf16[8,6528]{1,0:T(8,128)(2,1)S(1)} %get-tuple-element.28), channel_id=1, source_target_pairs={{0,24},{1,7},{2,26},{3,5},{4,28},{5,3},{6,30},{7,1},{8,16},{9,15},... | collective-permute-start | bytes 313352 | tf_op jit(solution)/shard_map/ppermute | solution.py:332
  6.4 0.0 collective-permute-start.1
  6.4 0.6 %collective-permute-start.2 = (bf16[8,6528]{1,0:T(8,128)(2,1)S(1)}, bf16[8,6528]{1,0:T(8,128)(2,1)S(1)}, u32[]{:S(2)}, u32[]{:S(2)}) collective-permute-start(bf16[8,6528]{1,0:T(8,128)(2,1)S(1)} %get-tuple-element.30), channel_id=1, source_target_pairs={{0,8},{1,5},{2,10},{3,7},{4,12},{5,1},{6,14},{7,3},{8,0},{9,13},{1... | collective-permute-start | bytes 313352 | tf_op jit(solution)/shard_map/ppermute | solution.py:332
  7.0 2.1 %collective-permute-done.refs_1_ = bf16[8,6528]{1,0:T(8,128)(2,1)S(1)} collective-permute-done((bf16[8,6528]{1,0:T(8,128)(2,1)S(1)}, bf16[8,6528]{1,0:T(8,128)(2,1)S(1)}, u32[]{:S(2)}, u32[]{:S(2)}) %collective-permute-start) | collective-permute-done | bytes 104480 | tf_op jit(solution)/shard_map/ppermute | solution.py:332
  9.2 3.0 %collective-permute-done.1.refs_2_ = bf16[8,6528]{1,0:T(8,128)(2,1)S(1)} collective-permute-done((bf16[8,6528]{1,0:T(8,128)(2,1)S(1)}, bf16[8,6528]{1,0:T(8,128)(2,1)S(1)}, u32[]{:S(2)}, u32[]{:S(2)}) %collective-permute-start.1) | collective-permute-done | bytes 104480 | tf_op jit(solution)/shard_map/ppermute | solution.py:332
  12.2 0.0 collective-permute-done.2.refs_3_
  12.2 0.0 slice-start.5
  12.2 0.0 slice-start.8
  12.2 0.0 slice-start
  12.2 0.0 slice-start.1
  12.2 0.6 %route.1 = (bf16[24,4096]{1,0:T(8,128)(2,1)S(1)}, bf16[24,4096]{1,0:T(8,128)(2,1)S(1)}, bf16[24,4096]{1,0:T(8,128)(2,1)S(1)}, bf16[24,4096]{1,0:T(8,128)(2,1)S(1)}) custom-call(bf16[8,6528]{1,0:T(8,128)(2,1)S(1)} %get-tuple-element.27.refs_0_, bf16[8,6528]{1,0:T(8,128)(2,1)S(1)} %collective-permute-done.refs_1_, ...), custom_call_target="tpu_custom_call" | custom-call | flops 10000000000 | tf_op jit(solution)/shard_map/route/pallas_call | solution.py:40
  12.8 2.5 %collective-permute-start.3 = (bf16[24,4096]{1,0:T(8,128)(2,1)S(1)}, bf16[24,4096]{1,0:T(8,128)(2,1)S(1)}, u32[]{:S(2)}, u32[]{:S(2)}) collective-permute-start(bf16[24,4096]{1,0:T(8,128)(2,1)S(1)} %get-tuple-element.32), channel_id=1, source_target_pairs={{0,6},{1,25},{2,4},{3,27},{4,2},{5,29},{6,0},{7,31},{8,14},{9,17},... | collective-permute-start | bytes 589832 | tf_op jit(solution)/shard_map/ppermute | solution.py:332
  15.3 0.5 %collective-permute-start.4 = (bf16[24,4096]{1,0:T(8,128)(2,1)S(1)}, bf16[24,4096]{1,0:T(8,128)(2,1)S(1)}, u32[]{:S(2)}, u32[]{:S(2)}) collective-permute-start(bf16[24,4096]{1,0:T(8,128)(2,1)S(1)} %get-tuple-element.33), channel_id=1, source_target_pairs={{0,2},{1,17},{2,0},{3,19},{4,6},{5,21},{6,4},{7,23},{8,10},{9,25},... | collective-permute-start | bytes 589832 | tf_op jit(solution)/shard_map/ppermute | solution.py:332
  15.9 0.5 collective-permute-start.5
  16.4 0.0 collective-permute-start.6
  16.4 3.1 %collective-permute-done.3.refs_1_ = bf16[24,4096]{1,0:T(8,128)(2,1)S(1)} collective-permute-done((bf16[24,4096]{1,0:T(8,128)(2,1)S(1)}, bf16[24,4096]{1,0:T(8,128)(2,1)S(1)}, u32[]{:S(2)}, u32[]{:S(2)}) %collective-permute-start.3) | collective-permute-done | bytes 196640 | tf_op jit(solution)/shard_map/ppermute | solution.py:332
  19.4 0.0 collective-permute-start.7
  19.4 2.2 %collective-permute-done.4.refs_2_ = bf16[24,4096]{1,0:T(8,128)(2,1)S(1)} collective-permute-done((bf16[24,4096]{1,0:T(8,128)(2,1)S(1)}, bf16[24,4096]{1,0:T(8,128)(2,1)S(1)}, u32[]{:S(2)}, u32[]{:S(2)}) %collective-permute-start.4) | collective-permute-done | bytes 196640 | tf_op jit(solution)/shard_map/ppermute | solution.py:332
  21.6 0.0 collective-permute-start.8
  21.6 0.0 collective-permute-done.5.refs_3_
  21.6 0.5 collective-permute-start.9
  22.1 0.0 collective-permute-done.6.refs_4_
  22.1 0.0 collective-permute-done.7.refs_5_
  22.1 0.9 %collective-permute-done.8.refs_6_ = bf16[24,4096]{1,0:T(8,128)(2,1)S(1)} collective-permute-done((bf16[24,4096]{1,0:T(8,128)(2,1)S(1)}, bf16[24,4096]{1,0:T(8,128)(2,1)S(1)}, u32[]{:S(2)}, u32[]{:S(2)}) %collective-permute-start.8) | collective-permute-done | bytes 196640 | tf_op jit(solution)/shard_map/ppermute | solution.py:336
  23.1 0.3 collective-permute-done.9.refs_7_
  23.3 0.0 slice-done.3
  23.3 0.0 slice-done.4
  23.3 0.0 slice-done.6
  23.3 0.0 slice-done.7
  23.4 0.0 slice-done.5
  23.4 0.0 slice-done.8
  23.4 0.0 slice-start.2
  23.4 5.0 %gate_up.1.hidden_ref = bf16[192,1536]{1,0:T(8,128)(2,1)S(1)} custom-call(bf16[24,4096]{1,0:T(8,128)(2,1)S(1)} %get-tuple-element.31.refs_0_, bf16[24,4096]{1,0:T(8,128)(2,1)S(1)} %collective-permute-done.3.refs_1_, bf16[24,4096]{1,0:T(8,128)(2,1)S(1)} %collective-permute-done.4.refs_2_, bf16[24,4096]{1,0:T(8,128)(2,1)S(1)} %collective-permute-done.5.refs_3_, ...), custom_call_target="tpu_custom_call" | custom-call | flops 4831838208 | tf_op jit(solution)/shard_map/gate_up/pallas_call | solution.py:40
  28.5 0.0 slice-done
  28.5 0.0 slice-done.1
  28.5 0.0 slice-done.2
  28.5 2.0 %down_0.1 = (bf16[96,3072]{1,0:T(8,128)(2,1)S(1)}, bf16[96,3072]{1,0:T(8,128)(2,1)S(1)}) custom-call(bf16[192,1536]{1,0:T(8,128)(2,1)S(1)} %gate_up.1.hidden_ref, bf16[1536,4096]{1,0:T(8,128)(2,1)S(1)} %bitcast.9), custom_call_target="tpu_custom_call" | custom-call | flops 1811939328 | tf_op jit(solution)/shard_map/down_0/pallas_call | solution.py:40
  30.5 0.3 collective-permute-start.10
  30.8 0.8 %down_1.1 = (bf16[96,1024]{1,0:T(8,128)(2,1)S(1)}, bf16[96,1024]{1,0:T(8,128)(2,1)S(1)}) custom-call(bf16[192,1536]{1,0:T(8,128)(2,1)S(1)} %gate_up.1.hidden_ref, bf16[1536,4096]{1,0:T(8,128)(2,1)S(1)} %bitcast.10), custom_call_target="tpu_custom_call" | custom-call | flops 603979776 | tf_op jit(solution)/shard_map/down_1/pallas_call | solution.py:40
  31.6 0.3 collective-permute-start.11
  31.9 1.2 %collective-permute-done.11.refs_3_ = bf16[96,1024]{1,0:T(8,128)(2,1)S(1)} collective-permute-done((bf16[96,1024]{1,0:T(8,128)(2,1)S(1)}, bf16[96,1024]{1,0:T(8,128)(2,1)S(1)}, u32[]{:S(2)}, u32[]{:S(2)}) %collective-permute-start.11) | collective-permute-done | bytes 196640 | tf_op jit(solution)/shard_map/ppermute | solution.py:336
  33.1 0.0 collective-permute-done.10.refs_2_
  33.1 0.2 add.1
  33.3 2.1 %collective-permute-start.12 = (bf16[24,4096]{1,0:T(8,128)(2,1)S(1)}, bf16[24,4096]{1,0:T(8,128)(2,1)S(1)}, u32[]{:S(2)}, u32[]{:S(2)}) collective-permute-start(bf16[24,4096]{1,0:T(8,128)(2,1)S(1)} %get-tuple-element.40), channel_id=1, source_target_pairs={{0,6},{1,25},{2,4},{3,27},{4,2},{5,29},{6,0},{7,31},{8,14},{9,17},... | collective-permute-start | bytes 589832 | tf_op jit(solution)/shard_map/ppermute | solution.py:332
  35.4 0.6 %collective-permute-start.13 = (bf16[24,4096]{1,0:T(8,128)(2,1)S(1)}, bf16[24,4096]{1,0:T(8,128)(2,1)S(1)}, u32[]{:S(2)}, u32[]{:S(2)}) collective-permute-start(bf16[24,4096]{1,0:T(8,128)(2,1)S(1)} %get-tuple-element.41), channel_id=1, source_target_pairs={{0,2},{1,17},{2,0},{3,19},{4,6},{5,21},{6,4},{7,23},{8,10},{9,25},... | collective-permute-start | bytes 589832 | tf_op jit(solution)/shard_map/ppermute | solution.py:332
  35.9 0.9 %collective-permute-start.14 = (bf16[24,4096]{1,0:T(8,128)(2,1)S(1)}, bf16[24,4096]{1,0:T(8,128)(2,1)S(1)}, u32[]{:S(2)}, u32[]{:S(2)}) collective-permute-start(bf16[24,4096]{1,0:T(8,128)(2,1)S(1)} %get-tuple-element.42), channel_id=1, source_target_pairs={{0,4},{1,9},{2,6},{3,11},{4,0},{5,13},{6,2},{7,15},{8,12},{9,1},{1... | collective-permute-start | bytes 589832 | tf_op jit(solution)/shard_map/ppermute | solution.py:332
  36.8 0.3 weigh.1.weights_ref
  37.1 2.8 %collective-permute-done.12.refs_1_ = bf16[24,4096]{1,0:T(8,128)(2,1)S(1)} collective-permute-done((bf16[24,4096]{1,0:T(8,128)(2,1)S(1)}, bf16[24,4096]{1,0:T(8,128)(2,1)S(1)}, u32[]{:S(2)}, u32[]{:S(2)}) %collective-permute-start.12) | collective-permute-done | bytes 196640 | tf_op jit(solution)/shard_map/ppermute | solution.py:332
  40.0 1.7 %collective-permute-done.13.refs_2_ = bf16[24,4096]{1,0:T(8,128)(2,1)S(1)} collective-permute-done((bf16[24,4096]{1,0:T(8,128)(2,1)S(1)}, bf16[24,4096]{1,0:T(8,128)(2,1)S(1)}, u32[]{:S(2)}, u32[]{:S(2)}) %collective-permute-start.13) | collective-permute-done | bytes 196640 | tf_op jit(solution)/shard_map/ppermute | solution.py:332
  41.7 0.4 collective-permute-done.14.refs_3_
  42.0 0.6 %blend.1 = (bf16[8,6144]{1,0:T(8,128)(2,1)S(1)}, bf16[8,6144]{1,0:T(8,128)(2,1)S(1)}, bf16[8,6144]{1,0:T(8,128)(2,1)S(1)}, bf16[8,6144]{1,0:T(8,128)(2,1)S(1)}) custom-call(bf16[96,192]{1,0:T(8,128)(2,1)S(1)} %weigh.1.weights_ref, bf16[24,4096]{1,0:T(8,128)(2,1)S(1)} %get-tuple-element.39.refs_0_, bf16[24,4096]{1,0:T(8,128)(2,1)S(1)} %collective-permute-done.12.refs_1_, ...), custom_call_target="tpu_custom_call" | custom-call | tf_op jit(solution)/shard_map/blend/pallas_call | solution.py:40
  42.6 2.3 %collective-permute-start.15 = (bf16[8,6144]{1,0:T(8,128)(2,1)S(1)}, bf16[8,6144]{1,0:T(8,128)(2,1)S(1)}, u32[]{:S(2)}, u32[]{:S(2)}) collective-permute-start(bf16[8,6144]{1,0:T(8,128)(2,1)S(1)} %get-tuple-element.44), channel_id=1, source_target_pairs={{0,24},{1,7},{2,26},{3,5},{4,28},{5,3},{6,30},{7,1},{8,16},{9,15},... | collective-permute-start | bytes 294920 | tf_op jit(solution)/shard_map/ppermute | solution.py:332
  44.9 0.4 collective-permute-start.16
  45.3 1.8 %collective-permute-start.17 = (bf16[8,6144]{1,0:T(8,128)(2,1)S(1)}, bf16[8,6144]{1,0:T(8,128)(2,1)S(1)}, u32[]{:S(2)}, u32[]{:S(2)}) collective-permute-start(bf16[8,6144]{1,0:T(8,128)(2,1)S(1)} %get-tuple-element.46), channel_id=1, source_target_pairs={{0,8},{1,5},{2,10},{3,7},{4,12},{5,1},{6,14},{7,3},{8,0},{9,13},{1... | collective-permute-start | bytes 294920 | tf_op jit(solution)/shard_map/ppermute | solution.py:332
  47.1 2.0 %collective-permute-done.15.refs_1_ = bf16[8,6144]{1,0:T(8,128)(2,1)S(1)} collective-permute-done((bf16[8,6144]{1,0:T(8,128)(2,1)S(1)}, bf16[8,6144]{1,0:T(8,128)(2,1)S(1)}, u32[]{:S(2)}, u32[]{:S(2)}) %collective-permute-start.15) | collective-permute-done | bytes 98336 | tf_op jit(solution)/shard_map/ppermute | solution.py:332
  49.1 2.1 %collective-permute-done.16.refs_2_ = bf16[8,6144]{1,0:T(8,128)(2,1)S(1)} collective-permute-done((bf16[8,6144]{1,0:T(8,128)(2,1)S(1)}, bf16[8,6144]{1,0:T(8,128)(2,1)S(1)}, u32[]{:S(2)}, u32[]{:S(2)}) %collective-permute-start.16) | collective-permute-done | bytes 98336 | tf_op jit(solution)/shard_map/ppermute | solution.py:332
  51.3 0.0 collective-permute-done.17.refs_3_
  51.3 0.7 %finish.1 = bf16[6,2,4096]{2,1,0:T(2,128)(2,1)} custom-call(bf16[24,128]{1,0:T(8,128)(2,1)S(1)} %get-tuple-element.26.table_ref, bf16[8,6144]{1,0:T(8,128)(2,1)S(1)} %get-tuple-element.43.refs_0_, bf16[8,6144]{1,0:T(8,128)(2,1)S(1)} %collective-permute-done.15.refs_1_, bf16[8,6144]{1,0:T(8,128)(2,1)S(1)} %collective-permute-done.16.refs_2_, ...), custom_call_target="tpu_custom_call" | custom-call | tf_op jit(solution)/shard_map/finish/pallas_call | solution.py:40
  (3 shorter events, 0.0 us)
Async XLA Ops:
  0.0 23.3 %slice-start.3 = ((s8[12582912]{0:T(1024)(128)(4,1)}), s8[4194304]{0:T(1024)(128)(4,1)S(1)}, s32[]{:S(2)}) async-start(s8[12582912]{0:T(1024)(128)(4,1)} %bitcast.11), calls=%async_computation.3 | async-start | bytes 8388608
  0.0 23.3 %slice-start.4 = ((s8[12582912]{0:T(1024)(128)(4,1)}), s8[4194304]{0:T(1024)(128)(4,1)S(1)}, s32[]{:S(2)}) async-start(s8[12582912]{0:T(1024)(128)(4,1)} %bitcast.11), calls=%async_computation.4 | async-start | bytes 8388608
  0.0 23.3 %slice-start.6 = ((s8[12582912]{0:T(1024)(128)(4,1)}), s8[4194304]{0:T(1024)(128)(4,1)S(1)}, s32[]{:S(2)}) async-start(s8[12582912]{0:T(1024)(128)(4,1)} %bitcast.14), calls=%async_computation.6 | async-start | bytes 8388608
  0.0 23.3 %slice-start.7 = ((s8[12582912]{0:T(1024)(128)(4,1)}), s8[4194304]{0:T(1024)(128)(4,1)S(1)}, s32[]{:S(2)}) async-start(s8[12582912]{0:T(1024)(128)(4,1)} %bitcast.14), calls=%async_computation.7 | async-start | bytes 8388608
  1.3 7.9 %collective-permute-start = (bf16[8,6528]{1,0:T(8,128)(2,1)S(1)}, bf16[8,6528]{1,0:T(8,128)(2,1)S(1)}, u32[]{:S(2)}, u32[]{:S(2)}) collective-permute-start(bf16[8,6528]{1,0:T(8,128)(2,1)S(1)} %get-tuple-element.28), channel_id=1, source_target_pairs={{0,24},{1,7},{2,26},{3,5},{4,28},{5,3},{6,30},{7,1},{8,16},{9,15},... | collective-permute-start | bytes 313352 | tf_op jit(solution)/shard_map/ppermute | solution.py:332
  6.4 5.8 %collective-permute-start.1 = (bf16[8,6528]{1,0:T(8,128)(2,1)S(1)}, bf16[8,6528]{1,0:T(8,128)(2,1)S(1)}, u32[]{:S(2)}, u32[]{:S(2)}) collective-permute-start(bf16[8,6528]{1,0:T(8,128)(2,1)S(1)} %get-tuple-element.29), channel_id=1, source_target_pairs={{0,16},{1,3},{2,18},{3,1},{4,20},{5,7},{6,22},{7,5},{8,24},{9,11},... | collective-permute-start | bytes 313352 | tf_op jit(solution)/shard_map/ppermute | solution.py:332
  6.4 5.8 %collective-permute-start.2 = (bf16[8,6528]{1,0:T(8,128)(2,1)S(1)}, bf16[8,6528]{1,0:T(8,128)(2,1)S(1)}, u32[]{:S(2)}, u32[]{:S(2)}) collective-permute-start(bf16[8,6528]{1,0:T(8,128)(2,1)S(1)} %get-tuple-element.30), channel_id=1, source_target_pairs={{0,8},{1,5},{2,10},{3,7},{4,12},{5,1},{6,14},{7,3},{8,0},{9,13},{1... | collective-permute-start | bytes 313352 | tf_op jit(solution)/shard_map/ppermute | solution.py:332
  12.2 11.2 %slice-start.5 = ((s8[12582912]{0:T(1024)(128)(4,1)}), s8[4194304]{0:T(1024)(128)(4,1)S(1)}, s32[]{:S(2)}) async-start(s8[12582912]{0:T(1024)(128)(4,1)} %bitcast.11), calls=%async_computation.5 | async-start | bytes 8388608
  12.2 11.2 %slice-start.8 = ((s8[12582912]{0:T(1024)(128)(4,1)}), s8[4194304]{0:T(1024)(128)(4,1)S(1)}, s32[]{:S(2)}) async-start(s8[12582912]{0:T(1024)(128)(4,1)} %bitcast.14), calls=%async_computation.8 | async-start | bytes 8388608
  12.2 16.3 %slice-start = ((s8[12582912]{0:T(1024)(128)(4,1)}), s8[4194304]{0:T(1024)(128)(4,1)S(1)}, s32[]{:S(2)}) async-start(s8[12582912]{0:T(1024)(128)(4,1)} %bitcast.7), calls=%async_computation | async-start | bytes 8388608
  12.2 16.3 %slice-start.1 = ((s8[12582912]{0:T(1024)(128)(4,1)}), s8[4194304]{0:T(1024)(128)(4,1)S(1)}, s32[]{:S(2)}) async-start(s8[12582912]{0:T(1024)(128)(4,1)} %bitcast.7), calls=%async_computation.1 | async-start | bytes 8388608
  12.8 6.6 %collective-permute-start.3 = (bf16[24,4096]{1,0:T(8,128)(2,1)S(1)}, bf16[24,4096]{1,0:T(8,128)(2,1)S(1)}, u32[]{:S(2)}, u32[]{:S(2)}) collective-permute-start(bf16[24,4096]{1,0:T(8,128)(2,1)S(1)} %get-tuple-element.32), channel_id=1, source_target_pairs={{0,6},{1,25},{2,4},{3,27},{4,2},{5,29},{6,0},{7,31},{8,14},{9,17},... | collective-permute-start | bytes 589832 | tf_op jit(solution)/shard_map/ppermute | solution.py:332
  15.3 6.3 %collective-permute-start.4 = (bf16[24,4096]{1,0:T(8,128)(2,1)S(1)}, bf16[24,4096]{1,0:T(8,128)(2,1)S(1)}, u32[]{:S(2)}, u32[]{:S(2)}) collective-permute-start(bf16[24,4096]{1,0:T(8,128)(2,1)S(1)} %get-tuple-element.33), channel_id=1, source_target_pairs={{0,2},{1,17},{2,0},{3,19},{4,6},{5,21},{6,4},{7,23},{8,10},{9,25},... | collective-permute-start | bytes 589832 | tf_op jit(solution)/shard_map/ppermute | solution.py:332
  15.9 5.8 %collective-permute-start.5 = (bf16[24,4096]{1,0:T(8,128)(2,1)S(1)}, bf16[24,4096]{1,0:T(8,128)(2,1)S(1)}, u32[]{:S(2)}, u32[]{:S(2)}) collective-permute-start(bf16[24,4096]{1,0:T(8,128)(2,1)S(1)} %get-tuple-element.34), channel_id=1, source_target_pairs={{0,4},{1,9},{2,6},{3,11},{4,0},{5,13},{6,2},{7,15},{8,12},{9,1},{1... | collective-permute-start | bytes 589832 | tf_op jit(solution)/shard_map/ppermute | solution.py:332
  16.4 5.8 %collective-permute-start.6 = (bf16[24,4096]{1,0:T(8,128)(2,1)S(1)}, bf16[24,4096]{1,0:T(8,128)(2,1)S(1)}, u32[]{:S(2)}, u32[]{:S(2)}) collective-permute-start(bf16[24,4096]{1,0:T(8,128)(2,1)S(1)} %get-tuple-element.31.refs_0_), channel_id=1, source_target_pairs={{0,1},{1,0},{2,3},{3,2},{4,5},{5,4},{6,7},{7,6},{8,9},{9,8},{10,11... | collective-permute-start | bytes 589832 | tf_op jit(solution)/shard_map/ppermute | solution.py:336
  19.4 2.7 %collective-permute-start.7 = (bf16[24,4096]{1,0:T(8,128)(2,1)S(1)}, bf16[24,4096]{1,0:T(8,128)(2,1)S(1)}, u32[]{:S(2)}, u32[]{:S(2)}) collective-permute-start(bf16[24,4096]{1,0:T(8,128)(2,1)S(1)} %collective-permute-done.3.refs_1_), channel_id=1, source_target_pairs={{0,1},{1,0},{2,3},{3,2},{4,5},{5,4},{6,7},{7,6},{8,9},{9,8},{10,11... | collective-permute-start | bytes 589832 | tf_op jit(solution)/shard_map/ppermute | solution.py:336
  21.6 1.4 %collective-permute-start.8 = (bf16[24,4096]{1,0:T(8,128)(2,1)S(1)}, bf16[24,4096]{1,0:T(8,128)(2,1)S(1)}, u32[]{:S(2)}, u32[]{:S(2)}) collective-permute-start(bf16[24,4096]{1,0:T(8,128)(2,1)S(1)} %collective-permute-done.4.refs_2_), channel_id=1, source_target_pairs={{0,1},{1,0},{2,3},{3,2},{4,5},{5,4},{6,7},{7,6},{8,9},{9,8},{10,11... | collective-permute-start | bytes 589832 | tf_op jit(solution)/shard_map/ppermute | solution.py:336
  21.6 1.7 %collective-permute-start.9 = (bf16[24,4096]{1,0:T(8,128)(2,1)S(1)}, bf16[24,4096]{1,0:T(8,128)(2,1)S(1)}, u32[]{:S(2)}, u32[]{:S(2)}) collective-permute-start(bf16[24,4096]{1,0:T(8,128)(2,1)S(1)} %collective-permute-done.5.refs_3_), channel_id=1, source_target_pairs={{0,1},{1,0},{2,3},{3,2},{4,5},{5,4},{6,7},{7,6},{8,9},{9,8},{10,11... | collective-permute-start | bytes 589832 | tf_op jit(solution)/shard_map/ppermute | solution.py:336
  23.4 5.1 %slice-start.2 = ((s8[12582912]{0:T(1024)(128)(4,1)}), s8[4194304]{0:T(1024)(128)(4,1)S(1)}, s32[]{:S(2)}) async-start(s8[12582912]{0:T(1024)(128)(4,1)} %bitcast.7), calls=%async_computation.2 | async-start | bytes 8388608
  30.5 2.6 %collective-permute-start.10 = (bf16[96,3072]{1,0:T(8,128)(2,1)S(1)}, bf16[96,3072]{1,0:T(8,128)(2,1)S(1)}, u32[]{:S(2)}, u32[]{:S(2)}) collective-permute-start(bf16[96,3072]{1,0:T(8,128)(2,1)S(1)} %get-tuple-element.37), channel_id=1, source_target_pairs={{0,1},{1,0},{2,3},{3,2},{4,5},{5,4},{6,7},{7,6},{8,9},{9,8},{10,11... | collective-permute-start | bytes 1769480 | tf_op jit(solution)/shard_map/ppermute | solution.py:336
  31.6 1.5 %collective-permute-start.11 = (bf16[96,1024]{1,0:T(8,128)(2,1)S(1)}, bf16[96,1024]{1,0:T(8,128)(2,1)S(1)}, u32[]{:S(2)}, u32[]{:S(2)}) collective-permute-start(bf16[96,1024]{1,0:T(8,128)(2,1)S(1)} %get-tuple-element.38), channel_id=1, source_target_pairs={{0,1},{1,0},{2,3},{3,2},{4,5},{5,4},{6,7},{7,6},{8,9},{9,8},{10,11... | collective-permute-start | bytes 589832 | tf_op jit(solution)/shard_map/ppermute | solution.py:336
  33.3 6.7 %collective-permute-start.12 = (bf16[24,4096]{1,0:T(8,128)(2,1)S(1)}, bf16[24,4096]{1,0:T(8,128)(2,1)S(1)}, u32[]{:S(2)}, u32[]{:S(2)}) collective-permute-start(bf16[24,4096]{1,0:T(8,128)(2,1)S(1)} %get-tuple-element.40), channel_id=1, source_target_pairs={{0,6},{1,25},{2,4},{3,27},{4,2},{5,29},{6,0},{7,31},{8,14},{9,17},... | collective-permute-start | bytes 589832 | tf_op jit(solution)/shard_map/ppermute | solution.py:332
  35.4 6.3 %collective-permute-start.13 = (bf16[24,4096]{1,0:T(8,128)(2,1)S(1)}, bf16[24,4096]{1,0:T(8,128)(2,1)S(1)}, u32[]{:S(2)}, u32[]{:S(2)}) collective-permute-start(bf16[24,4096]{1,0:T(8,128)(2,1)S(1)} %get-tuple-element.41), channel_id=1, source_target_pairs={{0,2},{1,17},{2,0},{3,19},{4,6},{5,21},{6,4},{7,23},{8,10},{9,25},... | collective-permute-start | bytes 589832 | tf_op jit(solution)/shard_map/ppermute | solution.py:332
  35.9 6.1 %collective-permute-start.14 = (bf16[24,4096]{1,0:T(8,128)(2,1)S(1)}, bf16[24,4096]{1,0:T(8,128)(2,1)S(1)}, u32[]{:S(2)}, u32[]{:S(2)}) collective-permute-start(bf16[24,4096]{1,0:T(8,128)(2,1)S(1)} %get-tuple-element.42), channel_id=1, source_target_pairs={{0,4},{1,9},{2,6},{3,11},{4,0},{5,13},{6,2},{7,15},{8,12},{9,1},{1... | collective-permute-start | bytes 589832 | tf_op jit(solution)/shard_map/ppermute | solution.py:332
  42.6 6.5 %collective-permute-start.15 = (bf16[8,6144]{1,0:T(8,128)(2,1)S(1)}, bf16[8,6144]{1,0:T(8,128)(2,1)S(1)}, u32[]{:S(2)}, u32[]{:S(2)}) collective-permute-start(bf16[8,6144]{1,0:T(8,128)(2,1)S(1)} %get-tuple-element.44), channel_id=1, source_target_pairs={{0,24},{1,7},{2,26},{3,5},{4,28},{5,3},{6,30},{7,1},{8,16},{9,15},... | collective-permute-start | bytes 294920 | tf_op jit(solution)/shard_map/ppermute | solution.py:332
  44.9 6.3 %collective-permute-start.16 = (bf16[8,6144]{1,0:T(8,128)(2,1)S(1)}, bf16[8,6144]{1,0:T(8,128)(2,1)S(1)}, u32[]{:S(2)}, u32[]{:S(2)}) collective-permute-start(bf16[8,6144]{1,0:T(8,128)(2,1)S(1)} %get-tuple-element.45), channel_id=1, source_target_pairs={{0,16},{1,3},{2,18},{3,1},{4,20},{5,7},{6,22},{7,5},{8,24},{9,11},... | collective-permute-start | bytes 294920 | tf_op jit(solution)/shard_map/ppermute | solution.py:332
  45.3 6.0 %collective-permute-start.17 = (bf16[8,6144]{1,0:T(8,128)(2,1)S(1)}, bf16[8,6144]{1,0:T(8,128)(2,1)S(1)}, u32[]{:S(2)}, u32[]{:S(2)}) collective-permute-start(bf16[8,6144]{1,0:T(8,128)(2,1)S(1)} %get-tuple-element.46), channel_id=1, source_target_pairs={{0,8},{1,5},{2,10},{3,7},{4,12},{5,1},{6,14},{7,3},{8,0},{9,13},{1... | collective-permute-start | bytes 294920 | tf_op jit(solution)/shard_map/ppermute | solution.py:332

commit v4 on v3

--- a/solution.py
+++ b/solution.py
@@ -18,9 +18,10 @@
 
 
 def group_peer(g, i, members, back):
-    if members & (members - 1) == 0:
-        return g ^ (-i % members)
-    return (g + (-i if back else i)) % members
+    ring = [n ^ (n >> 1) for n in range(members)]
+    if sorted(ring) != list(range(members)):
+        ring = list(range(members))
+    return ring[(ring.index(g) + (i if back else -i)) % members]
 
 
 def plane_order(experts):
@@ -61,7 +62,7 @@
 
 
 def weigh_rows(weights, value, span):
-    total = lax.dot_general(weights, value, (((0,), (0,)), ((), ())), preferred_element_type=F32)
+    total = jnp.dot(weights, value, preferred_element_type=F32)
     return total[:span] + total[span : 2 * span] + total[2 * span :]
 
 
@@ -86,16 +87,16 @@
     table = jnp.zeros((table_rows, LANES), F32)
     copies[0].wait()
     copies[1].wait()
+    turns = sum(offsets.index(offset) << (4 * offset) for offset in range(experts))
+    turns = jnp.int32(turns - (1 << 32) if turns >> 31 else turns)
     for t in range(steps):
-        counts = [jnp.int32(0)] * experts
+        counts = jnp.int32(0)
         for r in range(rows):
             for k in range(2):
                 e = ids_ref[t, k, r]
-                position = jnp.int32(0)
-                for c in range(experts):
-                    position = jnp.where(e == c, counts[c], position)
-                counts = [counts[c] + (e == c).astype(jnp.int32) for c in range(experts)]
-                turn = sum(jnp.where((e ^ own) == offset, j, 0) for j, offset in enumerate(offsets))
+                position = (counts >> (4 * e)) & 15
+                counts = counts + (1 << (4 * e))
+                turn = (turns >> (4 * (e ^ own))) & 15
                 slot = (turn * steps + t) * slots + position
                 hit = (row_at == slot) & (low == r * steps + t)
                 table = jnp.where(hit, combine_ref[t, k, r], table)
@@ -191,7 +192,8 @@
 
 def weigh_body(experts, pair, width, *refs):
     packed, out = refs[:-1], refs[-1]
-    out[...] = jnp.concatenate(tables_of(packed, experts, pair, width, (2, 3, 4)), 1)
+    tables = tables_of(packed, experts, pair, width, (2, 3, 4))
+    out[...] = jnp.concatenate([t.astype(F32).T for t in tables], 0).astype(BF)
 
 
 def up_body(members, experts, pair, *refs):
@@ -296,7 +298,7 @@
 
     def second():
         value = jnp.concatenate([p[:, :width].astype(F32)[:pair] for p in parts[:experts]], 0).astype(BF)
-        write(weigh_rows(table_ref[:, 2 * FOLD : 5 * FOLD], value, FOLD))
+        write(weigh_rows(table_ref[:, 2 * FOLD : 5 * FOLD].astype(F32).T.astype(BF), value, FOLD))
 
     by_core(first, second)
 
@@ -364,7 +366,7 @@
     theirs = [swap(a) for a in mine]
     (weights,) = call(
         functools.partial(weigh_body, experts, pair, width),
-        [(rows_half, 3 * members * FOLD)],
+        [(3 * members * FOLD, rows_half)],
         arrived[:members],
         "weigh",
     )

time: 52.1 us -> 51.9 us (level)
  transfers between devices with their start and end apart: 18 -> 18, of which waited for: 12 -> 14; matrix products, arithmetic and copies ran while one was open for 0% -> 0% of each run, Pallas kernels for 2% -> 2%
where the time goes in v4:
time: 51.9 us; the launch traced here: 51.7 us
  waiting for transfers between devices  21.5 us (41%)
  starting transfers between devices  18.7 us (36%)
  Pallas kernels  11.3 us (22%)
    ppermute x12, waiting for transfers between devices, send(): got[i] = lax.ppermute(arrays[i], ('group', 'dev'), pairs)  19.1 us
    ppermute x12, starting transfers between devices, send(): got[i] = lax.ppermute(arrays[i], ('group', 'dev'), pairs)  17.5 us
    pallas_call x9, Pallas kernels, call(): pl.pallas_call(body, out_shape=[jax.ShapeDtypeStruct(s, BF) if isinstance...  11.3 us
    ppermute x6, waiting for transfers between devices, swap(): return lax.ppermute(array, 'dev', [(i, i ^ 1) for i in range(devices)])  2.37 us
    ppermute x6, starting transfers between devices, swap(): return lax.ppermute(array, 'dev', [(i, i ^ 1) for i in range(devices)])  1.15 us
  transfers between devices with their start and end apart: 18, of which 14 were waited for; matrix products, arithmetic and copies ran while one was open for 0% of the time, Pallas kernels for 2%

profile of v4, /device:TPU:0, one launch (start us, length us, event | category | flops | bytes accessed | tf_op | source)
XLA Modules:
  0.0 51.7 jit_solution(80925270282035589)
XLA Ops:
  0.0 0.0 slice-start.3
  0.0 0.0 slice-start.4
  0.0 0.0 slice-start.6
  0.0 0.0 slice-start.7
  0.0 1.2 %pack.1 = (bf16[8,6528]{1,0:T(8,128)(2,1)S(1)}, bf16[8,6528]{1,0:T(8,128)(2,1)S(1)}, bf16[8,6528]{1,0:T(8,128)(2,1)S(1)}, bf16[8,6528]{1,0:T(8,128)(2,1)S(1)}, bf16[24,128]{1,0:T(8,128)(2,1)S(1)}) custom-call(s32[2,2,6]{2,1,0:T(2,128)} %bitcast.18, f32[2,2,6]{2,1,0:T(2,128)} %bitcast.19, bf16[6,2,4096]{2,1,0:T(2,128)(2,1)} %bitcast.17), custom_call_target="tpu_custom_call" | custom-call | flops 10000000000 | tf_op jit(solution)/shard_map/pack/pallas_call | solution.py:41
  1.2 4.1 %collective-permute-start = (bf16[8,6528]{1,0:T(8,128)(2,1)S(1)}, bf16[8,6528]{1,0:T(8,128)(2,1)S(1)}, u32[]{:S(2)}, u32[]{:S(2)}) collective-permute-start(bf16[8,6528]{1,0:T(8,128)(2,1)S(1)} %get-tuple-element.28), channel_id=1, source_target_pairs={{0,16},{1,7},{2,18},{3,5},{4,20},{5,3},{6,22},{7,1},{8,0},{9,15},{... | collective-permute-start | bytes 313352 | tf_op jit(solution)/shard_map/ppermute | solution.py:334
  5.3 1.3 %collective-permute-start.1 = (bf16[8,6528]{1,0:T(8,128)(2,1)S(1)}, bf16[8,6528]{1,0:T(8,128)(2,1)S(1)}, u32[]{:S(2)}, u32[]{:S(2)}) collective-permute-start(bf16[8,6528]{1,0:T(8,128)(2,1)S(1)} %get-tuple-element.29), channel_id=1, source_target_pairs={{0,24},{1,3},{2,26},{3,1},{4,28},{5,7},{6,30},{7,5},{8,16},{9,11},... | collective-permute-start | bytes 313352 | tf_op jit(solution)/shard_map/ppermute | solution.py:334
  6.6 0.8 %collective-permute-start.2 = (bf16[8,6528]{1,0:T(8,128)(2,1)S(1)}, bf16[8,6528]{1,0:T(8,128)(2,1)S(1)}, u32[]{:S(2)}, u32[]{:S(2)}) collective-permute-start(bf16[8,6528]{1,0:T(8,128)(2,1)S(1)} %get-tuple-element.30), channel_id=1, source_target_pairs={{0,8},{1,5},{2,10},{3,7},{4,12},{5,1},{6,14},{7,3},{8,24},{9,13},{... | collective-permute-start | bytes 313352 | tf_op jit(solution)/shard_map/ppermute | solution.py:334
  7.4 0.1 collective-permute-done.refs_1_
  7.5 4.3 %collective-permute-done.1.refs_2_ = bf16[8,6528]{1,0:T(8,128)(2,1)S(1)} collective-permute-done((bf16[8,6528]{1,0:T(8,128)(2,1)S(1)}, bf16[8,6528]{1,0:T(8,128)(2,1)S(1)}, u32[]{:S(2)}, u32[]{:S(2)}) %collective-permute-start.1) | collective-permute-done | bytes 104480 | tf_op jit(solution)/shard_map/ppermute | solution.py:334
  11.9 1.1 %collective-permute-done.2.refs_3_ = bf16[8,6528]{1,0:T(8,128)(2,1)S(1)} collective-permute-done((bf16[8,6528]{1,0:T(8,128)(2,1)S(1)}, bf16[8,6528]{1,0:T(8,128)(2,1)S(1)}, u32[]{:S(2)}, u32[]{:S(2)}) %collective-permute-start.2) | collective-permute-done | bytes 104480 | tf_op jit(solution)/shard_map/ppermute | solution.py:334
  13.0 0.0 slice-start.5
  13.0 0.0 slice-start.8
  13.0 0.0 slice-start
  13.0 0.0 slice-start.1
  13.0 0.6 %route.1 = (bf16[24,4096]{1,0:T(8,128)(2,1)S(1)}, bf16[24,4096]{1,0:T(8,128)(2,1)S(1)}, bf16[24,4096]{1,0:T(8,128)(2,1)S(1)}, bf16[24,4096]{1,0:T(8,128)(2,1)S(1)}) custom-call(bf16[8,6528]{1,0:T(8,128)(2,1)S(1)} %get-tuple-element.27.refs_0_, bf16[8,6528]{1,0:T(8,128)(2,1)S(1)} %collective-permute-done.refs_1_, ...), custom_call_target="tpu_custom_call" | custom-call | flops 10000000000 | tf_op jit(solution)/shard_map/route/pallas_call | solution.py:41
  13.6 2.5 %collective-permute-start.3 = (bf16[24,4096]{1,0:T(8,128)(2,1)S(1)}, bf16[24,4096]{1,0:T(8,128)(2,1)S(1)}, u32[]{:S(2)}, u32[]{:S(2)}) collective-permute-start(bf16[24,4096]{1,0:T(8,128)(2,1)S(1)} %get-tuple-element.32), channel_id=1, source_target_pairs={{0,6},{1,17},{2,4},{3,19},{4,2},{5,21},{6,0},{7,23},{8,14},{9,1},{... | collective-permute-start | bytes 589832 | tf_op jit(solution)/shard_map/ppermute | solution.py:334
  16.1 0.5 %collective-permute-start.4 = (bf16[24,4096]{1,0:T(8,128)(2,1)S(1)}, bf16[24,4096]{1,0:T(8,128)(2,1)S(1)}, u32[]{:S(2)}, u32[]{:S(2)}) collective-permute-start(bf16[24,4096]{1,0:T(8,128)(2,1)S(1)} %get-tuple-element.33), channel_id=1, source_target_pairs={{0,2},{1,25},{2,0},{3,27},{4,6},{5,29},{6,4},{7,31},{8,10},{9,17},... | collective-permute-start | bytes 589832 | tf_op jit(solution)/shard_map/ppermute | solution.py:334
  16.6 0.5 collective-permute-start.5
  17.1 0.0 collective-permute-start.6
  17.1 3.1 %collective-permute-done.3.refs_1_ = bf16[24,4096]{1,0:T(8,128)(2,1)S(1)} collective-permute-done((bf16[24,4096]{1,0:T(8,128)(2,1)S(1)}, bf16[24,4096]{1,0:T(8,128)(2,1)S(1)}, u32[]{:S(2)}, u32[]{:S(2)}) %collective-permute-start.3) | collective-permute-done | bytes 196640 | tf_op jit(solution)/shard_map/ppermute | solution.py:334
  20.2 0.0 collective-permute-start.7
  20.2 2.2 %collective-permute-done.4.refs_2_ = bf16[24,4096]{1,0:T(8,128)(2,1)S(1)} collective-permute-done((bf16[24,4096]{1,0:T(8,128)(2,1)S(1)}, bf16[24,4096]{1,0:T(8,128)(2,1)S(1)}, u32[]{:S(2)}, u32[]{:S(2)}) %collective-permute-start.4) | collective-permute-done | bytes 196640 | tf_op jit(solution)/shard_map/ppermute | solution.py:334
  22.4 0.0 collective-permute-start.8
  22.4 0.0 collective-permute-done.5.refs_3_
  22.4 0.5 collective-permute-start.9
  22.9 0.0 collective-permute-done.6.refs_4_
  22.9 0.0 collective-permute-done.7.refs_5_
  22.9 0.9 %collective-permute-done.8.refs_6_ = bf16[24,4096]{1,0:T(8,128)(2,1)S(1)} collective-permute-done((bf16[24,4096]{1,0:T(8,128)(2,1)S(1)}, bf16[24,4096]{1,0:T(8,128)(2,1)S(1)}, u32[]{:S(2)}, u32[]{:S(2)}) %collective-permute-start.8) | collective-permute-done | bytes 196640 | tf_op jit(solution)/shard_map/ppermute | solution.py:338
  23.8 0.3 collective-permute-done.9.refs_7_
  24.1 0.0 slice-done.3
  24.1 0.0 slice-done.4
  24.1 0.0 slice-done.6
  24.1 0.0 slice-done.7
  24.1 0.0 slice-done.5
  24.1 0.0 slice-done.8
  24.2 0.0 slice-start.2
  24.2 5.0 %gate_up.1.hidden_ref = bf16[192,1536]{1,0:T(8,128)(2,1)S(1)} custom-call(bf16[24,4096]{1,0:T(8,128)(2,1)S(1)} %get-tuple-element.31.refs_0_, bf16[24,4096]{1,0:T(8,128)(2,1)S(1)} %collective-permute-done.3.refs_1_, bf16[24,4096]{1,0:T(8,128)(2,1)S(1)} %collective-permute-done.4.refs_2_, bf16[24,4096]{1,0:T(8,128)(2,1)S(1)} %collective-permute-done.5.refs_3_, ...), custom_call_target="tpu_custom_call" | custom-call | flops 4831838208 | tf_op jit(solution)/shard_map/gate_up/pallas_call | solution.py:41
  29.2 0.0 slice-done
  29.2 0.0 slice-done.1
  29.2 0.0 slice-done.2
  29.3 2.0 %down_0.1 = (bf16[96,3072]{1,0:T(8,128)(2,1)S(1)}, bf16[96,3072]{1,0:T(8,128)(2,1)S(1)}) custom-call(bf16[192,1536]{1,0:T(8,128)(2,1)S(1)} %gate_up.1.hidden_ref, bf16[1536,4096]{1,0:T(8,128)(2,1)S(1)} %bitcast.9), custom_call_target="tpu_custom_call" | custom-call | flops 1811939328 | tf_op jit(solution)/shard_map/down_0/pallas_call | solution.py:41
  31.3 0.3 collective-permute-start.10
  31.6 0.8 %down_1.1 = (bf16[96,1024]{1,0:T(8,128)(2,1)S(1)}, bf16[96,1024]{1,0:T(8,128)(2,1)S(1)}) custom-call(bf16[192,1536]{1,0:T(8,128)(2,1)S(1)} %gate_up.1.hidden_ref, bf16[1536,4096]{1,0:T(8,128)(2,1)S(1)} %bitcast.10), custom_call_target="tpu_custom_call" | custom-call | flops 603979776 | tf_op jit(solution)/shard_map/down_1/pallas_call | solution.py:41
  32.4 0.3 collective-permute-start.11
  32.7 1.2 %collective-permute-done.11.refs_3_ = bf16[96,1024]{1,0:T(8,128)(2,1)S(1)} collective-permute-done((bf16[96,1024]{1,0:T(8,128)(2,1)S(1)}, bf16[96,1024]{1,0:T(8,128)(2,1)S(1)}, u32[]{:S(2)}, u32[]{:S(2)}) %collective-permute-start.11) | collective-permute-done | bytes 196640 | tf_op jit(solution)/shard_map/ppermute | solution.py:338
  33.9 0.0 collective-permute-done.10.refs_2_
  33.9 0.2 add.1
  34.1 2.1 %collective-permute-start.12 = (bf16[24,4096]{1,0:T(8,128)(2,1)S(1)}, bf16[24,4096]{1,0:T(8,128)(2,1)S(1)}, u32[]{:S(2)}, u32[]{:S(2)}) collective-permute-start(bf16[24,4096]{1,0:T(8,128)(2,1)S(1)} %get-tuple-element.40), channel_id=1, source_target_pairs={{0,6},{1,9},{2,4},{3,11},{4,2},{5,13},{6,0},{7,15},{8,14},{9,25},{... | collective-permute-start | bytes 589832 | tf_op jit(solution)/shard_map/ppermute | solution.py:334
  36.1 0.5 %collective-permute-start.13 = (bf16[24,4096]{1,0:T(8,128)(2,1)S(1)}, bf16[24,4096]{1,0:T(8,128)(2,1)S(1)}, u32[]{:S(2)}, u32[]{:S(2)}) collective-permute-start(bf16[24,4096]{1,0:T(8,128)(2,1)S(1)} %get-tuple-element.41), channel_id=1, source_target_pairs={{0,2},{1,25},{2,0},{3,27},{4,6},{5,29},{6,4},{7,31},{8,10},{9,17},... | collective-permute-start | bytes 589832 | tf_op jit(solution)/shard_map/ppermute | solution.py:334
  36.7 0.9 %collective-permute-start.14 = (bf16[24,4096]{1,0:T(8,128)(2,1)S(1)}, bf16[24,4096]{1,0:T(8,128)(2,1)S(1)}, u32[]{:S(2)}, u32[]{:S(2)}) collective-permute-start(bf16[24,4096]{1,0:T(8,128)(2,1)S(1)} %get-tuple-element.42), channel_id=1, source_target_pairs={{0,4},{1,17},{2,6},{3,19},{4,0},{5,21},{6,2},{7,23},{8,12},{9,1},{... | collective-permute-start | bytes 589832 | tf_op jit(solution)/shard_map/ppermute | solution.py:334
  37.6 0.3 weigh.1.weights_ref
  37.9 2.8 %collective-permute-done.12.refs_1_ = bf16[24,4096]{1,0:T(8,128)(2,1)S(1)} collective-permute-done((bf16[24,4096]{1,0:T(8,128)(2,1)S(1)}, bf16[24,4096]{1,0:T(8,128)(2,1)S(1)}, u32[]{:S(2)}, u32[]{:S(2)}) %collective-permute-start.12) | collective-permute-done | bytes 196640 | tf_op jit(solution)/shard_map/ppermute | solution.py:334
  40.7 1.7 %collective-permute-done.13.refs_2_ = bf16[24,4096]{1,0:T(8,128)(2,1)S(1)} collective-permute-done((bf16[24,4096]{1,0:T(8,128)(2,1)S(1)}, bf16[24,4096]{1,0:T(8,128)(2,1)S(1)}, u32[]{:S(2)}, u32[]{:S(2)}) %collective-permute-start.13) | collective-permute-done | bytes 196640 | tf_op jit(solution)/shard_map/ppermute | solution.py:334
  42.4 0.4 collective-permute-done.14.refs_3_
  42.8 0.6 %blend.1 = (bf16[8,6144]{1,0:T(8,128)(2,1)S(1)}, bf16[8,6144]{1,0:T(8,128)(2,1)S(1)}, bf16[8,6144]{1,0:T(8,128)(2,1)S(1)}, bf16[8,6144]{1,0:T(8,128)(2,1)S(1)}) custom-call(bf16[192,96]{1,0:T(8,128)(2,1)S(1)} %weigh.1.weights_ref, bf16[24,4096]{1,0:T(8,128)(2,1)S(1)} %get-tuple-element.39.refs_0_, bf16[24,4096]{1,0:T(8,128)(2,1)S(1)} %collective-permute-done.12.refs_1_, ...), custom_call_target="tpu_custom_call" | custom-call | tf_op jit(solution)/shard_map/blend/pallas_call | solution.py:41
  43.3 0.1 collective-permute-start.15
  43.4 2.2 %collective-permute-start.16 = (bf16[8,6144]{1,0:T(8,128)(2,1)S(1)}, bf16[8,6144]{1,0:T(8,128)(2,1)S(1)}, u32[]{:S(2)}, u32[]{:S(2)}) collective-permute-start(bf16[8,6144]{1,0:T(8,128)(2,1)S(1)} %get-tuple-element.45), channel_id=1, source_target_pairs={{0,24},{1,3},{2,26},{3,1},{4,28},{5,7},{6,30},{7,5},{8,16},{9,11},... | collective-permute-start | bytes 294920 | tf_op jit(solution)/shard_map/ppermute | solution.py:334
  45.6 1.9 %collective-permute-start.17 = (bf16[8,6144]{1,0:T(8,128)(2,1)S(1)}, bf16[8,6144]{1,0:T(8,128)(2,1)S(1)}, u32[]{:S(2)}, u32[]{:S(2)}) collective-permute-start(bf16[8,6144]{1,0:T(8,128)(2,1)S(1)} %get-tuple-element.46), channel_id=1, source_target_pairs={{0,16},{1,5},{2,18},{3,7},{4,20},{5,1},{6,22},{7,3},{8,0},{9,13},{... | collective-permute-start | bytes 294920 | tf_op jit(solution)/shard_map/ppermute | solution.py:334
  47.6 1.3 %collective-permute-done.15.refs_1_ = bf16[8,6144]{1,0:T(8,128)(2,1)S(1)} collective-permute-done((bf16[8,6144]{1,0:T(8,128)(2,1)S(1)}, bf16[8,6144]{1,0:T(8,128)(2,1)S(1)}, u32[]{:S(2)}, u32[]{:S(2)}) %collective-permute-start.15) | collective-permute-done | bytes 98336 | tf_op jit(solution)/shard_map/ppermute | solution.py:334
  48.9 1.1 %collective-permute-done.16.refs_2_ = bf16[8,6144]{1,0:T(8,128)(2,1)S(1)} collective-permute-done((bf16[8,6144]{1,0:T(8,128)(2,1)S(1)}, bf16[8,6144]{1,0:T(8,128)(2,1)S(1)}, u32[]{:S(2)}, u32[]{:S(2)}) %collective-permute-start.16) | collective-permute-done | bytes 98336 | tf_op jit(solution)/shard_map/ppermute | solution.py:334
  50.1 1.0 %collective-permute-done.17.refs_3_ = bf16[8,6144]{1,0:T(8,128)(2,1)S(1)} collective-permute-done((bf16[8,6144]{1,0:T(8,128)(2,1)S(1)}, bf16[8,6144]{1,0:T(8,128)(2,1)S(1)}, u32[]{:S(2)}, u32[]{:S(2)}) %collective-permute-start.17) | collective-permute-done | bytes 98336 | tf_op jit(solution)/shard_map/ppermute | solution.py:334
  51.0 0.7 %finish.1 = bf16[6,2,4096]{2,1,0:T(2,128)(2,1)} custom-call(bf16[24,128]{1,0:T(8,128)(2,1)S(1)} %get-tuple-element.26.table_ref, bf16[8,6144]{1,0:T(8,128)(2,1)S(1)} %get-tuple-element.43.refs_0_, bf16[8,6144]{1,0:T(8,128)(2,1)S(1)} %collective-permute-done.15.refs_1_, bf16[8,6144]{1,0:T(8,128)(2,1)S(1)} %collective-permute-done.16.refs_2_, ...), custom_call_target="tpu_custom_call" | custom-call | tf_op jit(solution)/shard_map/finish/pallas_call | solution.py:41
  (3 shorter events, 0.0 us)
Async XLA Ops:
  0.0 24.1 %slice-start.3 = ((s8[12582912]{0:T(1024)(128)(4,1)}), s8[4194304]{0:T(1024)(128)(4,1)S(1)}, s32[]{:S(2)}) async-start(s8[12582912]{0:T(1024)(128)(4,1)} %bitcast.11), calls=%async_computation.3 | async-start | bytes 8388608
  0.0 24.1 %slice-start.4 = ((s8[12582912]{0:T(1024)(128)(4,1)}), s8[4194304]{0:T(1024)(128)(4,1)S(1)}, s32[]{:S(2)}) async-start(s8[12582912]{0:T(1024)(128)(4,1)} %bitcast.11), calls=%async_computation.4 | async-start | bytes 8388608
  0.0 24.1 %slice-start.6 = ((s8[12582912]{0:T(1024)(128)(4,1)}), s8[4194304]{0:T(1024)(128)(4,1)S(1)}, s32[]{:S(2)}) async-start(s8[12582912]{0:T(1024)(128)(4,1)} %bitcast.14), calls=%async_computation.6 | async-start | bytes 8388608
  0.0 24.1 %slice-start.7 = ((s8[12582912]{0:T(1024)(128)(4,1)}), s8[4194304]{0:T(1024)(128)(4,1)S(1)}, s32[]{:S(2)}) async-start(s8[12582912]{0:T(1024)(128)(4,1)} %bitcast.14), calls=%async_computation.7 | async-start | bytes 8388608
  1.2 6.4 %collective-permute-start = (bf16[8,6528]{1,0:T(8,128)(2,1)S(1)}, bf16[8,6528]{1,0:T(8,128)(2,1)S(1)}, u32[]{:S(2)}, u32[]{:S(2)}) collective-permute-start(bf16[8,6528]{1,0:T(8,128)(2,1)S(1)} %get-tuple-element.28), channel_id=1, source_target_pairs={{0,16},{1,7},{2,18},{3,5},{4,20},{5,3},{6,22},{7,1},{8,0},{9,15},{... | collective-permute-start | bytes 313352 | tf_op jit(solution)/shard_map/ppermute | solution.py:334
  5.3 6.6 %collective-permute-start.1 = (bf16[8,6528]{1,0:T(8,128)(2,1)S(1)}, bf16[8,6528]{1,0:T(8,128)(2,1)S(1)}, u32[]{:S(2)}, u32[]{:S(2)}) collective-permute-start(bf16[8,6528]{1,0:T(8,128)(2,1)S(1)} %get-tuple-element.29), channel_id=1, source_target_pairs={{0,24},{1,3},{2,26},{3,1},{4,28},{5,7},{6,30},{7,5},{8,16},{9,11},... | collective-permute-start | bytes 313352 | tf_op jit(solution)/shard_map/ppermute | solution.py:334
  6.6 6.4 %collective-permute-start.2 = (bf16[8,6528]{1,0:T(8,128)(2,1)S(1)}, bf16[8,6528]{1,0:T(8,128)(2,1)S(1)}, u32[]{:S(2)}, u32[]{:S(2)}) collective-permute-start(bf16[8,6528]{1,0:T(8,128)(2,1)S(1)} %get-tuple-element.30), channel_id=1, source_target_pairs={{0,8},{1,5},{2,10},{3,7},{4,12},{5,1},{6,14},{7,3},{8,24},{9,13},{... | collective-permute-start | bytes 313352 | tf_op jit(solution)/shard_map/ppermute | solution.py:334
  13.0 11.1 %slice-start.5 = ((s8[12582912]{0:T(1024)(128)(4,1)}), s8[4194304]{0:T(1024)(128)(4,1)S(1)}, s32[]{:S(2)}) async-start(s8[12582912]{0:T(1024)(128)(4,1)} %bitcast.11), calls=%async_computation.5 | async-start | bytes 8388608
  13.0 11.2 %slice-start.8 = ((s8[12582912]{0:T(1024)(128)(4,1)}), s8[4194304]{0:T(1024)(128)(4,1)S(1)}, s32[]{:S(2)}) async-start(s8[12582912]{0:T(1024)(128)(4,1)} %bitcast.14), calls=%async_computation.8 | async-start | bytes 8388608
  13.0 16.2 %slice-start = ((s8[12582912]{0:T(1024)(128)(4,1)}), s8[4194304]{0:T(1024)(128)(4,1)S(1)}, s32[]{:S(2)}) async-start(s8[12582912]{0:T(1024)(128)(4,1)} %bitcast.7), calls=%async_computation | async-start | bytes 8388608
  13.0 16.2 %slice-start.1 = ((s8[12582912]{0:T(1024)(128)(4,1)}), s8[4194304]{0:T(1024)(128)(4,1)S(1)}, s32[]{:S(2)}) async-start(s8[12582912]{0:T(1024)(128)(4,1)} %bitcast.7), calls=%async_computation.1 | async-start | bytes 8388608
  13.6 6.6 %collective-permute-start.3 = (bf16[24,4096]{1,0:T(8,128)(2,1)S(1)}, bf16[24,4096]{1,0:T(8,128)(2,1)S(1)}, u32[]{:S(2)}, u32[]{:S(2)}) collective-permute-start(bf16[24,4096]{1,0:T(8,128)(2,1)S(1)} %get-tuple-element.32), channel_id=1, source_target_pairs={{0,6},{1,17},{2,4},{3,19},{4,2},{5,21},{6,0},{7,23},{8,14},{9,1},{... | collective-permute-start | bytes 589832 | tf_op jit(solution)/shard_map/ppermute | solution.py:334
  16.1 6.3 %collective-permute-start.4 = (bf16[24,4096]{1,0:T(8,128)(2,1)S(1)}, bf16[24,4096]{1,0:T(8,128)(2,1)S(1)}, u32[]{:S(2)}, u32[]{:S(2)}) collective-permute-start(bf16[24,4096]{1,0:T(8,128)(2,1)S(1)} %get-tuple-element.33), channel_id=1, source_target_pairs={{0,2},{1,25},{2,0},{3,27},{4,6},{5,29},{6,4},{7,31},{8,10},{9,17},... | collective-permute-start | bytes 589832 | tf_op jit(solution)/shard_map/ppermute | solution.py:334
  16.6 5.8 %collective-permute-start.5 = (bf16[24,4096]{1,0:T(8,128)(2,1)S(1)}, bf16[24,4096]{1,0:T(8,128)(2,1)S(1)}, u32[]{:S(2)}, u32[]{:S(2)}) collective-permute-start(bf16[24,4096]{1,0:T(8,128)(2,1)S(1)} %get-tuple-element.34), channel_id=1, source_target_pairs={{0,4},{1,9},{2,6},{3,11},{4,0},{5,13},{6,2},{7,15},{8,12},{9,25},{... | collective-permute-start | bytes 589832 | tf_op jit(solution)/shard_map/ppermute | solution.py:334
  17.1 5.8 %collective-permute-start.6 = (bf16[24,4096]{1,0:T(8,128)(2,1)S(1)}, bf16[24,4096]{1,0:T(8,128)(2,1)S(1)}, u32[]{:S(2)}, u32[]{:S(2)}) collective-permute-start(bf16[24,4096]{1,0:T(8,128)(2,1)S(1)} %get-tuple-element.31.refs_0_), channel_id=1, source_target_pairs={{0,1},{1,0},{2,3},{3,2},{4,5},{5,4},{6,7},{7,6},{8,9},{9,8},{10,11... | collective-permute-start | bytes 589832 | tf_op jit(solution)/shard_map/ppermute | solution.py:338
  20.2 2.7 %collective-permute-start.7 = (bf16[24,4096]{1,0:T(8,128)(2,1)S(1)}, bf16[24,4096]{1,0:T(8,128)(2,1)S(1)}, u32[]{:S(2)}, u32[]{:S(2)}) collective-permute-start(bf16[24,4096]{1,0:T(8,128)(2,1)S(1)} %collective-permute-done.3.refs_1_), channel_id=1, source_target_pairs={{0,1},{1,0},{2,3},{3,2},{4,5},{5,4},{6,7},{7,6},{8,9},{9,8},{10,11... | collective-permute-start | bytes 589832 | tf_op jit(solution)/shard_map/ppermute | solution.py:338
  22.4 1.4 %collective-permute-start.8 = (bf16[24,4096]{1,0:T(8,128)(2,1)S(1)}, bf16[24,4096]{1,0:T(8,128)(2,1)S(1)}, u32[]{:S(2)}, u32[]{:S(2)}) collective-permute-start(bf16[24,4096]{1,0:T(8,128)(2,1)S(1)} %collective-permute-done.4.refs_2_), channel_id=1, source_target_pairs={{0,1},{1,0},{2,3},{3,2},{4,5},{5,4},{6,7},{7,6},{8,9},{9,8},{10,11... | collective-permute-start | bytes 589832 | tf_op jit(solution)/shard_map/ppermute | solution.py:338
  22.4 1.7 %collective-permute-start.9 = (bf16[24,4096]{1,0:T(8,128)(2,1)S(1)}, bf16[24,4096]{1,0:T(8,128)(2,1)S(1)}, u32[]{:S(2)}, u32[]{:S(2)}) collective-permute-start(bf16[24,4096]{1,0:T(8,128)(2,1)S(1)} %collective-permute-done.5.refs_3_), channel_id=1, source_target_pairs={{0,1},{1,0},{2,3},{3,2},{4,5},{5,4},{6,7},{7,6},{8,9},{9,8},{10,11... | collective-permute-start | bytes 589832 | tf_op jit(solution)/shard_map/ppermute | solution.py:338
  24.2 5.1 %slice-start.2 = ((s8[12582912]{0:T(1024)(128)(4,1)}), s8[4194304]{0:T(1024)(128)(4,1)S(1)}, s32[]{:S(2)}) async-start(s8[12582912]{0:T(1024)(128)(4,1)} %bitcast.7), calls=%async_computation.2 | async-start | bytes 8388608
  31.3 2.6 %collective-permute-start.10 = (bf16[96,3072]{1,0:T(8,128)(2,1)S(1)}, bf16[96,3072]{1,0:T(8,128)(2,1)S(1)}, u32[]{:S(2)}, u32[]{:S(2)}) collective-permute-start(bf16[96,3072]{1,0:T(8,128)(2,1)S(1)} %get-tuple-element.37), channel_id=1, source_target_pairs={{0,1},{1,0},{2,3},{3,2},{4,5},{5,4},{6,7},{7,6},{8,9},{9,8},{10,11... | collective-permute-start | bytes 1769480 | tf_op jit(solution)/shard_map/ppermute | solution.py:338
  32.4 1.5 %collective-permute-start.11 = (bf16[96,1024]{1,0:T(8,128)(2,1)S(1)}, bf16[96,1024]{1,0:T(8,128)(2,1)S(1)}, u32[]{:S(2)}, u32[]{:S(2)}) collective-permute-start(bf16[96,1024]{1,0:T(8,128)(2,1)S(1)} %get-tuple-element.38), channel_id=1, source_target_pairs={{0,1},{1,0},{2,3},{3,2},{4,5},{5,4},{6,7},{7,6},{8,9},{9,8},{10,11... | collective-permute-start | bytes 589832 | tf_op jit(solution)/shard_map/ppermute | solution.py:338
  34.1 6.7 %collective-permute-start.12 = (bf16[24,4096]{1,0:T(8,128)(2,1)S(1)}, bf16[24,4096]{1,0:T(8,128)(2,1)S(1)}, u32[]{:S(2)}, u32[]{:S(2)}) collective-permute-start(bf16[24,4096]{1,0:T(8,128)(2,1)S(1)} %get-tuple-element.40), channel_id=1, source_target_pairs={{0,6},{1,9},{2,4},{3,11},{4,2},{5,13},{6,0},{7,15},{8,14},{9,25},{... | collective-permute-start | bytes 589832 | tf_op jit(solution)/shard_map/ppermute | solution.py:334
  36.1 6.3 %collective-permute-start.13 = (bf16[24,4096]{1,0:T(8,128)(2,1)S(1)}, bf16[24,4096]{1,0:T(8,128)(2,1)S(1)}, u32[]{:S(2)}, u32[]{:S(2)}) collective-permute-start(bf16[24,4096]{1,0:T(8,128)(2,1)S(1)} %get-tuple-element.41), channel_id=1, source_target_pairs={{0,2},{1,25},{2,0},{3,27},{4,6},{5,29},{6,4},{7,31},{8,10},{9,17},... | collective-permute-start | bytes 589832 | tf_op jit(solution)/shard_map/ppermute | solution.py:334
  36.7 6.1 %collective-permute-start.14 = (bf16[24,4096]{1,0:T(8,128)(2,1)S(1)}, bf16[24,4096]{1,0:T(8,128)(2,1)S(1)}, u32[]{:S(2)}, u32[]{:S(2)}) collective-permute-start(bf16[24,4096]{1,0:T(8,128)(2,1)S(1)} %get-tuple-element.42), channel_id=1, source_target_pairs={{0,4},{1,17},{2,6},{3,19},{4,0},{5,21},{6,2},{7,23},{8,12},{9,1},{... | collective-permute-start | bytes 589832 | tf_op jit(solution)/shard_map/ppermute | solution.py:334
  43.3 5.6 %collective-permute-start.15 = (bf16[8,6144]{1,0:T(8,128)(2,1)S(1)}, bf16[8,6144]{1,0:T(8,128)(2,1)S(1)}, u32[]{:S(2)}, u32[]{:S(2)}) collective-permute-start(bf16[8,6144]{1,0:T(8,128)(2,1)S(1)} %get-tuple-element.44), channel_id=1, source_target_pairs={{0,8},{1,7},{2,10},{3,5},{4,12},{5,3},{6,14},{7,1},{8,24},{9,15},{... | collective-permute-start | bytes 294920 | tf_op jit(solution)/shard_map/ppermute | solution.py:334
  43.4 6.6 %collective-permute-start.16 = (bf16[8,6144]{1,0:T(8,128)(2,1)S(1)}, bf16[8,6144]{1,0:T(8,128)(2,1)S(1)}, u32[]{:S(2)}, u32[]{:S(2)}) collective-permute-start(bf16[8,6144]{1,0:T(8,128)(2,1)S(1)} %get-tuple-element.45), channel_id=1, source_target_pairs={{0,24},{1,3},{2,26},{3,1},{4,28},{5,7},{6,30},{7,5},{8,16},{9,11},... | collective-permute-start | bytes 294920 | tf_op jit(solution)/shard_map/ppermute | solution.py:334
  45.6 5.4 %collective-permute-start.17 = (bf16[8,6144]{1,0:T(8,128)(2,1)S(1)}, bf16[8,6144]{1,0:T(8,128)(2,1)S(1)}, u32[]{:S(2)}, u32[]{:S(2)}) collective-permute-start(bf16[8,6144]{1,0:T(8,128)(2,1)S(1)} %get-tuple-element.46), channel_id=1, source_target_pairs={{0,16},{1,5},{2,18},{3,7},{4,20},{5,1},{6,22},{7,3},{8,0},{9,13},{... | collective-permute-start | bytes 294920 | tf_op jit(solution)/shard_map/ppermute | solution.py:334

commit v5 on v4

--- a/solution.py
+++ b/solution.py
@@ -230,6 +230,12 @@
         other_ref[:, cols] = value[mine:]
 
 
+def up_down_body(members, experts, pair, *refs):
+    ins, (down_ref, hidden_ref, own_ref, other_ref, rows_ref) = refs[:-5], refs[-5:]
+    up_body(members, experts, pair, *ins, hidden_ref, rows_ref)
+    down_body(0, hidden_ref, down_ref, own_ref, other_ref)
+
+
 def add_body(members, experts, pair, *refs):
     parts = len(CUTS) - 1
     owns, gots, outs = refs[:parts], refs[parts : 2 * parts], refs[2 * parts :]
@@ -370,23 +376,22 @@
         arrived[:members],
         "weigh",
     )
-    (hidden,) = call(
-        functools.partial(up_body, members, experts, pair),
-        [(2 * rows_half, hidden_units)],
-        (*mine, *theirs, gate_weight[0], up_weight[0]),
-        "gate_up",
-        [pltpu.VMEM] * (2 * count + 2),
+    cuts = [cut * width // CUTS[-1] for cut in CUTS]
+    hidden, own, other = call(
+        functools.partial(up_down_body, members, experts, pair),
+        [(2 * rows_half, hidden_units)] + [(rows_half, cuts[1])] * 2,
+        (*mine, *theirs, gate_weight[0], up_weight[0], down_weight[0]),
+        "gate_up_down",
         scratch=[pltpu.VMEM((2 * rows_half, width), BF)],
         flops=8 * rows_half * width * hidden_units,
     )
-    owns, others = [], []
-    for p, (low, high) in enumerate(zip(CUTS, CUTS[1:])):
-        low, high = low * width // CUTS[-1], high * width // CUTS[-1]
+    owns, others = [own], [swap(other)]
+    for p, (low, high) in enumerate(zip(cuts[1:], cuts[2:])):
         own, other = call(
             functools.partial(down_body, low),
             [(rows_half, high - low)] * 2,
             (hidden, down_weight[0]),
-            "down_%d" % p,
+            "down_%d" % (p + 1),
             flops=4 * rows_half * (high - low) * hidden_units,
         )
         owns.append(own)

time: 51.9 us -> 51.7 us (level)
    pallas_call x9 -> x8, Pallas kernels: 11.3 us -> 11.1 us  [call(): pl.pallas_call(body, out_shape=[jax.ShapeDtypeStruct(s, BF) if isinstance...]
where the time goes in v5:
time: 51.7 us; the launch traced here: 51.5 us
  waiting for transfers between devices  21.5 us (42%)
  starting transfers between devices  18.7 us (36%)
  Pallas kernels  11.1 us (21%)
    ppermute x12, waiting for transfers between devices, send(): got[i] = lax.ppermute(arrays[i], ('group', 'dev'), pairs)  19.1 us
    ppermute x12, starting transfers between devices, send(): got[i] = lax.ppermute(arrays[i], ('group', 'dev'), pairs)  17.5 us
    pallas_call x8, Pallas kernels, call(): pl.pallas_call(body, out_shape=[jax.ShapeDtypeStruct(s, BF) if isinstance...  11.1 us
    ppermute x6, waiting for transfers between devices, swap(): return lax.ppermute(array, 'dev', [(i, i ^ 1) for i in range(devices)])  2.38 us
    ppermute x6, starting transfers between devices, swap(): return lax.ppermute(array, 'dev', [(i, i ^ 1) for i in range(devices)])  1.15 us
  transfers between devices with their start and end apart: 18, of which 14 were waited for; matrix products, arithmetic and copies ran while one was open for 0% of the time, Pallas kernels for 2%

profile of v5, /device:TPU:0, one launch (start us, length us, event | category | flops | bytes accessed | tf_op | source)
XLA Modules:
  0.0 51.5 jit_solution(14515167529102702224)
XLA Ops:
  0.0 0.0 slice-start
  0.0 0.0 slice-start.1
  0.0 0.0 slice-start.3
  0.0 0.0 slice-start.4
  0.0 0.0 slice-start.6
  0.0 0.0 slice-start.7
  0.0 1.2 %pack.1 = (bf16[8,6528]{1,0:T(8,128)(2,1)S(1)}, bf16[8,6528]{1,0:T(8,128)(2,1)S(1)}, bf16[8,6528]{1,0:T(8,128)(2,1)S(1)}, bf16[8,6528]{1,0:T(8,128)(2,1)S(1)}, bf16[24,128]{1,0:T(8,128)(2,1)S(1)}) custom-call(s32[2,2,6]{2,1,0:T(2,128)} %bitcast.18, f32[2,2,6]{2,1,0:T(2,128)} %bitcast.19, bf16[6,2,4096]{2,1,0:T(2,128)(2,1)} %bitcast.17), custom_call_target="tpu_custom_call" | custom-call | flops 10000000000 | tf_op jit(solution)/shard_map/pack/pallas_call | solution.py:41
  1.2 4.1 %collective-permute-start = (bf16[8,6528]{1,0:T(8,128)(2,1)S(1)}, bf16[8,6528]{1,0:T(8,128)(2,1)S(1)}, u32[]{:S(2)}, u32[]{:S(2)}) collective-permute-start(bf16[8,6528]{1,0:T(8,128)(2,1)S(1)} %get-tuple-element.29), channel_id=1, source_target_pairs={{0,16},{1,7},{2,18},{3,5},{4,20},{5,3},{6,22},{7,1},{8,0},{9,15},{... | collective-permute-start | bytes 313352 | tf_op jit(solution)/shard_map/ppermute | solution.py:340
  5.3 1.3 %collective-permute-start.1 = (bf16[8,6528]{1,0:T(8,128)(2,1)S(1)}, bf16[8,6528]{1,0:T(8,128)(2,1)S(1)}, u32[]{:S(2)}, u32[]{:S(2)}) collective-permute-start(bf16[8,6528]{1,0:T(8,128)(2,1)S(1)} %get-tuple-element.30), channel_id=1, source_target_pairs={{0,24},{1,3},{2,26},{3,1},{4,28},{5,7},{6,30},{7,5},{8,16},{9,11},... | collective-permute-start | bytes 313352 | tf_op jit(solution)/shard_map/ppermute | solution.py:340
  6.7 0.8 %collective-permute-start.2 = (bf16[8,6528]{1,0:T(8,128)(2,1)S(1)}, bf16[8,6528]{1,0:T(8,128)(2,1)S(1)}, u32[]{:S(2)}, u32[]{:S(2)}) collective-permute-start(bf16[8,6528]{1,0:T(8,128)(2,1)S(1)} %get-tuple-element.31), channel_id=1, source_target_pairs={{0,8},{1,5},{2,10},{3,7},{4,12},{5,1},{6,14},{7,3},{8,24},{9,13},{... | collective-permute-start | bytes 313352 | tf_op jit(solution)/shard_map/ppermute | solution.py:340
  7.4 0.1 collective-permute-done.refs_1_
  7.6 4.3 %collective-permute-done.1.refs_2_ = bf16[8,6528]{1,0:T(8,128)(2,1)S(1)} collective-permute-done((bf16[8,6528]{1,0:T(8,128)(2,1)S(1)}, bf16[8,6528]{1,0:T(8,128)(2,1)S(1)}, u32[]{:S(2)}, u32[]{:S(2)}) %collective-permute-start.1) | collective-permute-done | bytes 104480 | tf_op jit(solution)/shard_map/ppermute | solution.py:340
  11.9 1.1 %collective-permute-done.2.refs_3_ = bf16[8,6528]{1,0:T(8,128)(2,1)S(1)} collective-permute-done((bf16[8,6528]{1,0:T(8,128)(2,1)S(1)}, bf16[8,6528]{1,0:T(8,128)(2,1)S(1)}, u32[]{:S(2)}, u32[]{:S(2)}) %collective-permute-start.2) | collective-permute-done | bytes 104480 | tf_op jit(solution)/shard_map/ppermute | solution.py:340
  13.0 0.0 slice-start.2
  13.0 0.0 slice-start.5
  13.0 0.0 slice-start.8
  13.0 0.6 %route.1 = (bf16[24,4096]{1,0:T(8,128)(2,1)S(1)}, bf16[24,4096]{1,0:T(8,128)(2,1)S(1)}, bf16[24,4096]{1,0:T(8,128)(2,1)S(1)}, bf16[24,4096]{1,0:T(8,128)(2,1)S(1)}) custom-call(bf16[8,6528]{1,0:T(8,128)(2,1)S(1)} %get-tuple-element.28.refs_0_, bf16[8,6528]{1,0:T(8,128)(2,1)S(1)} %collective-permute-done.refs_1_, ...), custom_call_target="tpu_custom_call" | custom-call | flops 10000000000 | tf_op jit(solution)/shard_map/route/pallas_call | solution.py:41
  13.6 2.5 %collective-permute-start.3 = (bf16[24,4096]{1,0:T(8,128)(2,1)S(1)}, bf16[24,4096]{1,0:T(8,128)(2,1)S(1)}, u32[]{:S(2)}, u32[]{:S(2)}) collective-permute-start(bf16[24,4096]{1,0:T(8,128)(2,1)S(1)} %get-tuple-element.33), channel_id=1, source_target_pairs={{0,6},{1,17},{2,4},{3,19},{4,2},{5,21},{6,0},{7,23},{8,14},{9,1},{... | collective-permute-start | bytes 589832 | tf_op jit(solution)/shard_map/ppermute | solution.py:340
  16.1 0.5 %collective-permute-start.4 = (bf16[24,4096]{1,0:T(8,128)(2,1)S(1)}, bf16[24,4096]{1,0:T(8,128)(2,1)S(1)}, u32[]{:S(2)}, u32[]{:S(2)}) collective-permute-start(bf16[24,4096]{1,0:T(8,128)(2,1)S(1)} %get-tuple-element.34), channel_id=1, source_target_pairs={{0,2},{1,25},{2,0},{3,27},{4,6},{5,29},{6,4},{7,31},{8,10},{9,17},... | collective-permute-start | bytes 589832 | tf_op jit(solution)/shard_map/ppermute | solution.py:340
  16.6 0.5 collective-permute-start.5
  17.1 0.0 collective-permute-start.6
  17.1 3.1 %collective-permute-done.3.refs_1_ = bf16[24,4096]{1,0:T(8,128)(2,1)S(1)} collective-permute-done((bf16[24,4096]{1,0:T(8,128)(2,1)S(1)}, bf16[24,4096]{1,0:T(8,128)(2,1)S(1)}, u32[]{:S(2)}, u32[]{:S(2)}) %collective-permute-start.3) | collective-permute-done | bytes 196640 | tf_op jit(solution)/shard_map/ppermute | solution.py:340
  20.2 0.0 collective-permute-start.7
  20.2 2.2 %collective-permute-done.4.refs_2_ = bf16[24,4096]{1,0:T(8,128)(2,1)S(1)} collective-permute-done((bf16[24,4096]{1,0:T(8,128)(2,1)S(1)}, bf16[24,4096]{1,0:T(8,128)(2,1)S(1)}, u32[]{:S(2)}, u32[]{:S(2)}) %collective-permute-start.4) | collective-permute-done | bytes 196640 | tf_op jit(solution)/shard_map/ppermute | solution.py:340
  22.4 0.0 collective-permute-start.8
  22.4 0.0 collective-permute-done.5.refs_3_
  22.4 0.5 collective-permute-start.9
  22.9 0.0 collective-permute-done.6.refs_4_
  22.9 0.0 collective-permute-done.7.refs_5_
  22.9 0.9 %collective-permute-done.8.refs_6_ = bf16[24,4096]{1,0:T(8,128)(2,1)S(1)} collective-permute-done((bf16[24,4096]{1,0:T(8,128)(2,1)S(1)}, bf16[24,4096]{1,0:T(8,128)(2,1)S(1)}, u32[]{:S(2)}, u32[]{:S(2)}) %collective-permute-start.8) | collective-permute-done | bytes 196640 | tf_op jit(solution)/shard_map/ppermute | solution.py:344
  23.8 0.3 collective-permute-done.9.refs_7_
  24.1 0.0 slice-done
  24.1 0.0 slice-done.1
  24.1 0.0 slice-done.3
  24.1 0.0 slice-done.4
  24.1 0.0 slice-done.6
  24.1 0.0 slice-done.7
  24.1 0.0 slice-done.2
  24.2 0.0 slice-done.5
  24.2 0.0 slice-done.8
  24.2 6.9 %gate_up_down.1 = (bf16[192,1536]{1,0:T(8,128)(2,1)S(1)}, bf16[96,3072]{1,0:T(8,128)(2,1)S(1)}, bf16[96,3072]{1,0:T(8,128)(2,1)S(1)}) custom-call(bf16[24,4096]{1,0:T(8,128)(2,1)S(1)} %get-tuple-element.32.refs_0_, bf16[24,4096]{1,0:T(8,128)(2,1)S(1)} %collective-permute-done.3.refs_1_, bf16[24,4096]{1,0:T(8,128)(2,1)S(1)} %collective-permute-done.4.refs_2_, ...), custom_call_target="tpu_custom_call" | custom-call | flops 4831838208 | tf_op jit(solution)/shard_map/gate_up_down/pallas_call | solution.py:41
  31.1 0.3 collective-permute-start.10
  31.4 0.8 %down_1.1 = (bf16[96,1024]{1,0:T(8,128)(2,1)S(1)}, bf16[96,1024]{1,0:T(8,128)(2,1)S(1)}) custom-call(bf16[192,1536]{1,0:T(8,128)(2,1)S(1)} %get-tuple-element.37.hidden_ref, bf16[1536,4096]{1,0:T(8,128)(2,1)S(1)} %bitcast.10), custom_call_target="tpu_custom_call" | custom-call | flops 603979776 | tf_op jit(solution)/shard_map/down_1/pallas_call | solution.py:41
  32.2 0.3 collective-permute-start.11
  32.5 1.2 %collective-permute-done.11.refs_3_ = bf16[96,1024]{1,0:T(8,128)(2,1)S(1)} collective-permute-done((bf16[96,1024]{1,0:T(8,128)(2,1)S(1)}, bf16[96,1024]{1,0:T(8,128)(2,1)S(1)}, u32[]{:S(2)}, u32[]{:S(2)}) %collective-permute-start.11) | collective-permute-done | bytes 196640 | tf_op jit(solution)/shard_map/ppermute | solution.py:344
  33.7 0.0 collective-permute-done.10.refs_2_
  33.7 0.2 add.1
  33.9 2.1 %collective-permute-start.12 = (bf16[24,4096]{1,0:T(8,128)(2,1)S(1)}, bf16[24,4096]{1,0:T(8,128)(2,1)S(1)}, u32[]{:S(2)}, u32[]{:S(2)}) collective-permute-start(bf16[24,4096]{1,0:T(8,128)(2,1)S(1)} %get-tuple-element.42), channel_id=1, source_target_pairs={{0,6},{1,9},{2,4},{3,11},{4,2},{5,13},{6,0},{7,15},{8,14},{9,25},{... | collective-permute-start | bytes 589832 | tf_op jit(solution)/shard_map/ppermute | solution.py:340
  35.9 0.5 %collective-permute-start.13 = (bf16[24,4096]{1,0:T(8,128)(2,1)S(1)}, bf16[24,4096]{1,0:T(8,128)(2,1)S(1)}, u32[]{:S(2)}, u32[]{:S(2)}) collective-permute-start(bf16[24,4096]{1,0:T(8,128)(2,1)S(1)} %get-tuple-element.43), channel_id=1, source_target_pairs={{0,2},{1,25},{2,0},{3,27},{4,6},{5,29},{6,4},{7,31},{8,10},{9,17},... | collective-permute-start | bytes 589832 | tf_op jit(solution)/shard_map/ppermute | solution.py:340
  36.5 0.9 %collective-permute-start.14 = (bf16[24,4096]{1,0:T(8,128)(2,1)S(1)}, bf16[24,4096]{1,0:T(8,128)(2,1)S(1)}, u32[]{:S(2)}, u32[]{:S(2)}) collective-permute-start(bf16[24,4096]{1,0:T(8,128)(2,1)S(1)} %get-tuple-element.44), channel_id=1, source_target_pairs={{0,4},{1,17},{2,6},{3,19},{4,0},{5,21},{6,2},{7,23},{8,12},{9,1},{... | collective-permute-start | bytes 589832 | tf_op jit(solution)/shard_map/ppermute | solution.py:340
  37.4 0.3 weigh.1.weights_ref
  37.7 2.8 %collective-permute-done.12.refs_1_ = bf16[24,4096]{1,0:T(8,128)(2,1)S(1)} collective-permute-done((bf16[24,4096]{1,0:T(8,128)(2,1)S(1)}, bf16[24,4096]{1,0:T(8,128)(2,1)S(1)}, u32[]{:S(2)}, u32[]{:S(2)}) %collective-permute-start.12) | collective-permute-done | bytes 196640 | tf_op jit(solution)/shard_map/ppermute | solution.py:340
  40.5 1.7 %collective-permute-done.13.refs_2_ = bf16[24,4096]{1,0:T(8,128)(2,1)S(1)} collective-permute-done((bf16[24,4096]{1,0:T(8,128)(2,1)S(1)}, bf16[24,4096]{1,0:T(8,128)(2,1)S(1)}, u32[]{:S(2)}, u32[]{:S(2)}) %collective-permute-start.13) | collective-permute-done | bytes 196640 | tf_op jit(solution)/shard_map/ppermute | solution.py:340
  42.2 0.4 collective-permute-done.14.refs_3_
  42.6 0.6 %blend.1 = (bf16[8,6144]{1,0:T(8,128)(2,1)S(1)}, bf16[8,6144]{1,0:T(8,128)(2,1)S(1)}, bf16[8,6144]{1,0:T(8,128)(2,1)S(1)}, bf16[8,6144]{1,0:T(8,128)(2,1)S(1)}) custom-call(bf16[192,96]{1,0:T(8,128)(2,1)S(1)} %weigh.1.weights_ref, bf16[24,4096]{1,0:T(8,128)(2,1)S(1)} %get-tuple-element.41.refs_0_, bf16[24,4096]{1,0:T(8,128)(2,1)S(1)} %collective-permute-done.12.refs_1_, ...), custom_call_target="tpu_custom_call" | custom-call | tf_op jit(solution)/shard_map/blend/pallas_call | solution.py:41
  43.2 0.1 collective-permute-start.15
  43.2 2.2 %collective-permute-start.16 = (bf16[8,6144]{1,0:T(8,128)(2,1)S(1)}, bf16[8,6144]{1,0:T(8,128)(2,1)S(1)}, u32[]{:S(2)}, u32[]{:S(2)}) collective-permute-start(bf16[8,6144]{1,0:T(8,128)(2,1)S(1)} %get-tuple-element.47), channel_id=1, source_target_pairs={{0,24},{1,3},{2,26},{3,1},{4,28},{5,7},{6,30},{7,5},{8,16},{9,11},... | collective-permute-start | bytes 294920 | tf_op jit(solution)/shard_map/ppermute | solution.py:340
  45.4 1.9 %collective-permute-start.17 = (bf16[8,6144]{1,0:T(8,128)(2,1)S(1)}, bf16[8,6144]{1,0:T(8,128)(2,1)S(1)}, u32[]{:S(2)}, u32[]{:S(2)}) collective-permute-start(bf16[8,6144]{1,0:T(8,128)(2,1)S(1)} %get-tuple-element.48), channel_id=1, source_target_pairs={{0,16},{1,5},{2,18},{3,7},{4,20},{5,1},{6,22},{7,3},{8,0},{9,13},{... | collective-permute-start | bytes 294920 | tf_op jit(solution)/shard_map/ppermute | solution.py:340
  47.4 1.4 %collective-permute-done.15.refs_1_ = bf16[8,6144]{1,0:T(8,128)(2,1)S(1)} collective-permute-done((bf16[8,6144]{1,0:T(8,128)(2,1)S(1)}, bf16[8,6144]{1,0:T(8,128)(2,1)S(1)}, u32[]{:S(2)}, u32[]{:S(2)}) %collective-permute-start.15) | collective-permute-done | bytes 98336 | tf_op jit(solution)/shard_map/ppermute | solution.py:340
  48.7 1.1 %collective-permute-done.16.refs_2_ = bf16[8,6144]{1,0:T(8,128)(2,1)S(1)} collective-permute-done((bf16[8,6144]{1,0:T(8,128)(2,1)S(1)}, bf16[8,6144]{1,0:T(8,128)(2,1)S(1)}, u32[]{:S(2)}, u32[]{:S(2)}) %collective-permute-start.16) | collective-permute-done | bytes 98336 | tf_op jit(solution)/shard_map/ppermute | solution.py:340
  49.9 1.0 %collective-permute-done.17.refs_3_ = bf16[8,6144]{1,0:T(8,128)(2,1)S(1)} collective-permute-done((bf16[8,6144]{1,0:T(8,128)(2,1)S(1)}, bf16[8,6144]{1,0:T(8,128)(2,1)S(1)}, u32[]{:S(2)}, u32[]{:S(2)}) %collective-permute-start.17) | collective-permute-done | bytes 98336 | tf_op jit(solution)/shard_map/ppermute | solution.py:340
  50.8 0.7 %finish.1 = bf16[6,2,4096]{2,1,0:T(2,128)(2,1)} custom-call(bf16[24,128]{1,0:T(8,128)(2,1)S(1)} %get-tuple-element.27.table_ref, bf16[8,6144]{1,0:T(8,128)(2,1)S(1)} %get-tuple-element.45.refs_0_, bf16[8,6144]{1,0:T(8,128)(2,1)S(1)} %collective-permute-done.15.refs_1_, bf16[8,6144]{1,0:T(8,128)(2,1)S(1)} %collective-permute-done.16.refs_2_, ...), custom_call_target="tpu_custom_call" | custom-call | tf_op jit(solution)/shard_map/finish/pallas_call | solution.py:41
  (3 shorter events, 0.0 us)
Async XLA Ops:
  0.0 24.1 %slice-start = ((s8[12582912]{0:T(1024)(128)(4,1)}), s8[4194304]{0:T(1024)(128)(4,1)S(1)}, s32[]{:S(2)}) async-start(s8[12582912]{0:T(1024)(128)(4,1)} %bitcast.7), calls=%async_computation | async-start | bytes 8388608
  0.0 24.1 %slice-start.1 = ((s8[12582912]{0:T(1024)(128)(4,1)}), s8[4194304]{0:T(1024)(128)(4,1)S(1)}, s32[]{:S(2)}) async-start(s8[12582912]{0:T(1024)(128)(4,1)} %bitcast.7), calls=%async_computation.1 | async-start | bytes 8388608
  0.0 24.1 %slice-start.3 = ((s8[12582912]{0:T(1024)(128)(4,1)}), s8[4194304]{0:T(1024)(128)(4,1)S(1)}, s32[]{:S(2)}) async-start(s8[12582912]{0:T(1024)(128)(4,1)} %bitcast.11), calls=%async_computation.3 | async-start | bytes 8388608
  0.0 24.1 %slice-start.4 = ((s8[12582912]{0:T(1024)(128)(4,1)}), s8[4194304]{0:T(1024)(128)(4,1)S(1)}, s32[]{:S(2)}) async-start(s8[12582912]{0:T(1024)(128)(4,1)} %bitcast.11), calls=%async_computation.4 | async-start | bytes 8388608
  0.0 24.1 %slice-start.6 = ((s8[12582912]{0:T(1024)(128)(4,1)}), s8[4194304]{0:T(1024)(128)(4,1)S(1)}, s32[]{:S(2)}) async-start(s8[12582912]{0:T(1024)(128)(4,1)} %bitcast.14), calls=%async_computation.6 | async-start | bytes 8388608
  0.0 24.1 %slice-start.7 = ((s8[12582912]{0:T(1024)(128)(4,1)}), s8[4194304]{0:T(1024)(128)(4,1)S(1)}, s32[]{:S(2)}) async-start(s8[12582912]{0:T(1024)(128)(4,1)} %bitcast.14), calls=%async_computation.7 | async-start | bytes 8388608
  1.2 6.4 %collective-permute-start = (bf16[8,6528]{1,0:T(8,128)(2,1)S(1)}, bf16[8,6528]{1,0:T(8,128)(2,1)S(1)}, u32[]{:S(2)}, u32[]{:S(2)}) collective-permute-start(bf16[8,6528]{1,0:T(8,128)(2,1)S(1)} %get-tuple-element.29), channel_id=1, source_target_pairs={{0,16},{1,7},{2,18},{3,5},{4,20},{5,3},{6,22},{7,1},{8,0},{9,15},{... | collective-permute-start | bytes 313352 | tf_op jit(solution)/shard_map/ppermute | solution.py:340
  5.3 6.6 %collective-permute-start.1 = (bf16[8,6528]{1,0:T(8,128)(2,1)S(1)}, bf16[8,6528]{1,0:T(8,128)(2,1)S(1)}, u32[]{:S(2)}, u32[]{:S(2)}) collective-permute-start(bf16[8,6528]{1,0:T(8,128)(2,1)S(1)} %get-tuple-element.30), channel_id=1, source_target_pairs={{0,24},{1,3},{2,26},{3,1},{4,28},{5,7},{6,30},{7,5},{8,16},{9,11},... | collective-permute-start | bytes 313352 | tf_op jit(solution)/shard_map/ppermute | solution.py:340
  6.7 6.4 %collective-permute-start.2 = (bf16[8,6528]{1,0:T(8,128)(2,1)S(1)}, bf16[8,6528]{1,0:T(8,128)(2,1)S(1)}, u32[]{:S(2)}, u32[]{:S(2)}) collective-permute-start(bf16[8,6528]{1,0:T(8,128)(2,1)S(1)} %get-tuple-element.31), channel_id=1, source_target_pairs={{0,8},{1,5},{2,10},{3,7},{4,12},{5,1},{6,14},{7,3},{8,24},{9,13},{... | collective-permute-start | bytes 313352 | tf_op jit(solution)/shard_map/ppermute | solution.py:340
  13.0 11.1 %slice-start.2 = ((s8[12582912]{0:T(1024)(128)(4,1)}), s8[4194304]{0:T(1024)(128)(4,1)S(1)}, s32[]{:S(2)}) async-start(s8[12582912]{0:T(1024)(128)(4,1)} %bitcast.7), calls=%async_computation.2 | async-start | bytes 8388608
  13.0 11.2 %slice-start.5 = ((s8[12582912]{0:T(1024)(128)(4,1)}), s8[4194304]{0:T(1024)(128)(4,1)S(1)}, s32[]{:S(2)}) async-start(s8[12582912]{0:T(1024)(128)(4,1)} %bitcast.11), calls=%async_computation.5 | async-start | bytes 8388608
  13.0 11.2 %slice-start.8 = ((s8[12582912]{0:T(1024)(128)(4,1)}), s8[4194304]{0:T(1024)(128)(4,1)S(1)}, s32[]{:S(2)}) async-start(s8[12582912]{0:T(1024)(128)(4,1)} %bitcast.14), calls=%async_computation.8 | async-start | bytes 8388608
  13.6 6.6 %collective-permute-start.3 = (bf16[24,4096]{1,0:T(8,128)(2,1)S(1)}, bf16[24,4096]{1,0:T(8,128)(2,1)S(1)}, u32[]{:S(2)}, u32[]{:S(2)}) collective-permute-start(bf16[24,4096]{1,0:T(8,128)(2,1)S(1)} %get-tuple-element.33), channel_id=1, source_target_pairs={{0,6},{1,17},{2,4},{3,19},{4,2},{5,21},{6,0},{7,23},{8,14},{9,1},{... | collective-permute-start | bytes 589832 | tf_op jit(solution)/shard_map/ppermute | solution.py:340
  16.1 6.3 %collective-permute-start.4 = (bf16[24,4096]{1,0:T(8,128)(2,1)S(1)}, bf16[24,4096]{1,0:T(8,128)(2,1)S(1)}, u32[]{:S(2)}, u32[]{:S(2)}) collective-permute-start(bf16[24,4096]{1,0:T(8,128)(2,1)S(1)} %get-tuple-element.34), channel_id=1, source_target_pairs={{0,2},{1,25},{2,0},{3,27},{4,6},{5,29},{6,4},{7,31},{8,10},{9,17},... | collective-permute-start | bytes 589832 | tf_op jit(solution)/shard_map/ppermute | solution.py:340
  16.6 5.8 %collective-permute-start.5 = (bf16[24,4096]{1,0:T(8,128)(2,1)S(1)}, bf16[24,4096]{1,0:T(8,128)(2,1)S(1)}, u32[]{:S(2)}, u32[]{:S(2)}) collective-permute-start(bf16[24,4096]{1,0:T(8,128)(2,1)S(1)} %get-tuple-element.35), channel_id=1, source_target_pairs={{0,4},{1,9},{2,6},{3,11},{4,0},{5,13},{6,2},{7,15},{8,12},{9,25},{... | collective-permute-start | bytes 589832 | tf_op jit(solution)/shard_map/ppermute | solution.py:340
  17.1 5.8 %collective-permute-start.6 = (bf16[24,4096]{1,0:T(8,128)(2,1)S(1)}, bf16[24,4096]{1,0:T(8,128)(2,1)S(1)}, u32[]{:S(2)}, u32[]{:S(2)}) collective-permute-start(bf16[24,4096]{1,0:T(8,128)(2,1)S(1)} %get-tuple-element.32.refs_0_), channel_id=1, source_target_pairs={{0,1},{1,0},{2,3},{3,2},{4,5},{5,4},{6,7},{7,6},{8,9},{9,8},{10,11... | collective-permute-start | bytes 589832 | tf_op jit(solution)/shard_map/ppermute | solution.py:344
  20.2 2.7 %collective-permute-start.7 = (bf16[24,4096]{1,0:T(8,128)(2,1)S(1)}, bf16[24,4096]{1,0:T(8,128)(2,1)S(1)}, u32[]{:S(2)}, u32[]{:S(2)}) collective-permute-start(bf16[24,4096]{1,0:T(8,128)(2,1)S(1)} %collective-permute-done.3.refs_1_), channel_id=1, source_target_pairs={{0,1},{1,0},{2,3},{3,2},{4,5},{5,4},{6,7},{7,6},{8,9},{9,8},{10,11... | collective-permute-start | bytes 589832 | tf_op jit(solution)/shard_map/ppermute | solution.py:344
  22.4 1.4 %collective-permute-start.8 = (bf16[24,4096]{1,0:T(8,128)(2,1)S(1)}, bf16[24,4096]{1,0:T(8,128)(2,1)S(1)}, u32[]{:S(2)}, u32[]{:S(2)}) collective-permute-start(bf16[24,4096]{1,0:T(8,128)(2,1)S(1)} %collective-permute-done.4.refs_2_), channel_id=1, source_target_pairs={{0,1},{1,0},{2,3},{3,2},{4,5},{5,4},{6,7},{7,6},{8,9},{9,8},{10,11... | collective-permute-start | bytes 589832 | tf_op jit(solution)/shard_map/ppermute | solution.py:344
  22.4 1.7 %collective-permute-start.9 = (bf16[24,4096]{1,0:T(8,128)(2,1)S(1)}, bf16[24,4096]{1,0:T(8,128)(2,1)S(1)}, u32[]{:S(2)}, u32[]{:S(2)}) collective-permute-start(bf16[24,4096]{1,0:T(8,128)(2,1)S(1)} %collective-permute-done.5.refs_3_), channel_id=1, source_target_pairs={{0,1},{1,0},{2,3},{3,2},{4,5},{5,4},{6,7},{7,6},{8,9},{9,8},{10,11... | collective-permute-start | bytes 589832 | tf_op jit(solution)/shard_map/ppermute | solution.py:344
  31.1 2.6 %collective-permute-start.10 = (bf16[96,3072]{1,0:T(8,128)(2,1)S(1)}, bf16[96,3072]{1,0:T(8,128)(2,1)S(1)}, u32[]{:S(2)}, u32[]{:S(2)}) collective-permute-start(bf16[96,3072]{1,0:T(8,128)(2,1)S(1)} %get-tuple-element.39), channel_id=1, source_target_pairs={{0,1},{1,0},{2,3},{3,2},{4,5},{5,4},{6,7},{7,6},{8,9},{9,8},{10,11... | collective-permute-start | bytes 1769480 | tf_op jit(solution)/shard_map/ppermute | solution.py:344
  32.2 1.5 %collective-permute-start.11 = (bf16[96,1024]{1,0:T(8,128)(2,1)S(1)}, bf16[96,1024]{1,0:T(8,128)(2,1)S(1)}, u32[]{:S(2)}, u32[]{:S(2)}) collective-permute-start(bf16[96,1024]{1,0:T(8,128)(2,1)S(1)} %get-tuple-element.40), channel_id=1, source_target_pairs={{0,1},{1,0},{2,3},{3,2},{4,5},{5,4},{6,7},{7,6},{8,9},{9,8},{10,11... | collective-permute-start | bytes 589832 | tf_op jit(solution)/shard_map/ppermute | solution.py:344
  33.9 6.7 %collective-permute-start.12 = (bf16[24,4096]{1,0:T(8,128)(2,1)S(1)}, bf16[24,4096]{1,0:T(8,128)(2,1)S(1)}, u32[]{:S(2)}, u32[]{:S(2)}) collective-permute-start(bf16[24,4096]{1,0:T(8,128)(2,1)S(1)} %get-tuple-element.42), channel_id=1, source_target_pairs={{0,6},{1,9},{2,4},{3,11},{4,2},{5,13},{6,0},{7,15},{8,14},{9,25},{... | collective-permute-start | bytes 589832 | tf_op jit(solution)/shard_map/ppermute | solution.py:340
  35.9 6.3 %collective-permute-start.13 = (bf16[24,4096]{1,0:T(8,128)(2,1)S(1)}, bf16[24,4096]{1,0:T(8,128)(2,1)S(1)}, u32[]{:S(2)}, u32[]{:S(2)}) collective-permute-start(bf16[24,4096]{1,0:T(8,128)(2,1)S(1)} %get-tuple-element.43), channel_id=1, source_target_pairs={{0,2},{1,25},{2,0},{3,27},{4,6},{5,29},{6,4},{7,31},{8,10},{9,17},... | collective-permute-start | bytes 589832 | tf_op jit(solution)/shard_map/ppermute | solution.py:340
  36.5 6.1 %collective-permute-start.14 = (bf16[24,4096]{1,0:T(8,128)(2,1)S(1)}, bf16[24,4096]{1,0:T(8,128)(2,1)S(1)}, u32[]{:S(2)}, u32[]{:S(2)}) collective-permute-start(bf16[24,4096]{1,0:T(8,128)(2,1)S(1)} %get-tuple-element.44), channel_id=1, source_target_pairs={{0,4},{1,17},{2,6},{3,19},{4,0},{5,21},{6,2},{7,23},{8,12},{9,1},{... | collective-permute-start | bytes 589832 | tf_op jit(solution)/shard_map/ppermute | solution.py:340
  43.2 5.6 %collective-permute-start.15 = (bf16[8,6144]{1,0:T(8,128)(2,1)S(1)}, bf16[8,6144]{1,0:T(8,128)(2,1)S(1)}, u32[]{:S(2)}, u32[]{:S(2)}) collective-permute-start(bf16[8,6144]{1,0:T(8,128)(2,1)S(1)} %get-tuple-element.46), channel_id=1, source_target_pairs={{0,8},{1,7},{2,10},{3,5},{4,12},{5,3},{6,14},{7,1},{8,24},{9,15},{... | collective-permute-start | bytes 294920 | tf_op jit(solution)/shard_map/ppermute | solution.py:340
  43.2 6.6 %collective-permute-start.16 = (bf16[8,6144]{1,0:T(8,128)(2,1)S(1)}, bf16[8,6144]{1,0:T(8,128)(2,1)S(1)}, u32[]{:S(2)}, u32[]{:S(2)}) collective-permute-start(bf16[8,6144]{1,0:T(8,128)(2,1)S(1)} %get-tuple-element.47), channel_id=1, source_target_pairs={{0,24},{1,3},{2,26},{3,1},{4,28},{5,7},{6,30},{7,5},{8,16},{9,11},... | collective-permute-start | bytes 294920 | tf_op jit(solution)/shard_map/ppermute | solution.py:340
  45.4 5.4 %collective-permute-start.17 = (bf16[8,6144]{1,0:T(8,128)(2,1)S(1)}, bf16[8,6144]{1,0:T(8,128)(2,1)S(1)}, u32[]{:S(2)}, u32[]{:S(2)}) collective-permute-start(bf16[8,6144]{1,0:T(8,128)(2,1)S(1)} %get-tuple-element.48), channel_id=1, source_target_pairs={{0,16},{1,5},{2,18},{3,7},{4,20},{5,1},{6,22},{7,3},{8,0},{9,13},{... | collective-permute-start | bytes 294920 | tf_op jit(solution)/shard_map/ppermute | solution.py:340

commit v6 on v5

--- a/solution.py
+++ b/solution.py
@@ -212,8 +212,9 @@
         fill(0)
     else:
         by_core(lambda: fill(0), lambda: fill(1))
-    for j in range(hidden_ref.shape[1] // UNIT_TILE):
-        cols = slice(j * UNIT_TILE, (j + 1) * UNIT_TILE)
+    tile = UNIT_TILE * (2 if rows_ref.shape[0] <= UNIT_TILE else 1)
+    for j in range(hidden_ref.shape[1] // tile):
+        cols = slice(j * tile, (j + 1) * tile)
         gate = jnp.dot(rows_ref[...], gate_ref[:, cols], preferred_element_type=F32)
         up = jnp.dot(rows_ref[...], up_ref[:, cols], preferred_element_type=F32)
         hidden_ref[:, cols] = (jax.nn.silu(gate) * up).astype(BF)

time: 51.7 us -> 51.7 us (level)
  no operation moved by 1% of the time
where the time goes in v6:
time: 51.7 us; the launch traced here: 51.5 us
  waiting for transfers between devices  21.5 us (42%)
  starting transfers between devices  18.7 us (36%)
  Pallas kernels  11.1 us (21%)
    ppermute x12, waiting for transfers between devices, send(): got[i] = lax.ppermute(arrays[i], ('group', 'dev'), pairs)  19.1 us
    ppermute x12, starting transfers between devices, send(): got[i] = lax.ppermute(arrays[i], ('group', 'dev'), pairs)  17.6 us
    pallas_call x8, Pallas kernels, call(): pl.pallas_call(body, out_shape=[jax.ShapeDtypeStruct(s, BF) if isinstance...  11.1 us
    ppermute x6, waiting for transfers between devices, swap(): return lax.ppermute(array, 'dev', [(i, i ^ 1) for i in range(devices)])  2.38 us
    ppermute x6, starting transfers between devices, swap(): return lax.ppermute(array, 'dev', [(i, i ^ 1) for i in range(devices)])  1.16 us
  transfers between devices with their start and end apart: 18, of which 14 were waited for; matrix products, arithmetic and copies ran while one was open for 0% of the time, Pallas kernels for 2%

profile of v6, /device:TPU:0, one launch (start us, length us, event | category | flops | bytes accessed | tf_op | source)
XLA Modules:
  0.0 51.5 jit_solution(20545826656714816)
XLA Ops:
  0.0 0.0 slice-start
  0.0 0.0 slice-start.1
  0.0 0.0 slice-start.3
  0.0 0.0 slice-start.4
  0.0 0.0 slice-start.6
  0.0 0.0 slice-start.7
  0.0 1.2 %pack.1 = (bf16[8,6528]{1,0:T(8,128)(2,1)S(1)}, bf16[8,6528]{1,0:T(8,128)(2,1)S(1)}, bf16[8,6528]{1,0:T(8,128)(2,1)S(1)}, bf16[8,6528]{1,0:T(8,128)(2,1)S(1)}, bf16[24,128]{1,0:T(8,128)(2,1)S(1)}) custom-call(s32[2,2,6]{2,1,0:T(2,128)} %bitcast.18, f32[2,2,6]{2,1,0:T(2,128)} %bitcast.19, bf16[6,2,4096]{2,1,0:T(2,128)(2,1)} %bitcast.17), custom_call_target="tpu_custom_call" | custom-call | flops 10000000000 | tf_op jit(solution)/shard_map/pack/pallas_call | solution.py:41
  1.2 4.1 %collective-permute-start = (bf16[8,6528]{1,0:T(8,128)(2,1)S(1)}, bf16[8,6528]{1,0:T(8,128)(2,1)S(1)}, u32[]{:S(2)}, u32[]{:S(2)}) collective-permute-start(bf16[8,6528]{1,0:T(8,128)(2,1)S(1)} %get-tuple-element.29), channel_id=1, source_target_pairs={{0,16},{1,7},{2,18},{3,5},{4,20},{5,3},{6,22},{7,1},{8,0},{9,15},{... | collective-permute-start | bytes 313352 | tf_op jit(solution)/shard_map/ppermute | solution.py:341
  5.3 1.3 %collective-permute-start.1 = (bf16[8,6528]{1,0:T(8,128)(2,1)S(1)}, bf16[8,6528]{1,0:T(8,128)(2,1)S(1)}, u32[]{:S(2)}, u32[]{:S(2)}) collective-permute-start(bf16[8,6528]{1,0:T(8,128)(2,1)S(1)} %get-tuple-element.30), channel_id=1, source_target_pairs={{0,24},{1,3},{2,26},{3,1},{4,28},{5,7},{6,30},{7,5},{8,16},{9,11},... | collective-permute-start | bytes 313352 | tf_op jit(solution)/shard_map/ppermute | solution.py:341
  6.7 0.8 %collective-permute-start.2 = (bf16[8,6528]{1,0:T(8,128)(2,1)S(1)}, bf16[8,6528]{1,0:T(8,128)(2,1)S(1)}, u32[]{:S(2)}, u32[]{:S(2)}) collective-permute-start(bf16[8,6528]{1,0:T(8,128)(2,1)S(1)} %get-tuple-element.31), channel_id=1, source_target_pairs={{0,8},{1,5},{2,10},{3,7},{4,12},{5,1},{6,14},{7,3},{8,24},{9,13},{... | collective-permute-start | bytes 313352 | tf_op jit(solution)/shard_map/ppermute | solution.py:341
  7.4 0.1 collective-permute-done.refs_1_
  7.6 4.3 %collective-permute-done.1.refs_2_ = bf16[8,6528]{1,0:T(8,128)(2,1)S(1)} collective-permute-done((bf16[8,6528]{1,0:T(8,128)(2,1)S(1)}, bf16[8,6528]{1,0:T(8,128)(2,1)S(1)}, u32[]{:S(2)}, u32[]{:S(2)}) %collective-permute-start.1) | collective-permute-done | bytes 104480 | tf_op jit(solution)/shard_map/ppermute | solution.py:341
  11.9 1.1 %collective-permute-done.2.refs_3_ = bf16[8,6528]{1,0:T(8,128)(2,1)S(1)} collective-permute-done((bf16[8,6528]{1,0:T(8,128)(2,1)S(1)}, bf16[8,6528]{1,0:T(8,128)(2,1)S(1)}, u32[]{:S(2)}, u32[]{:S(2)}) %collective-permute-start.2) | collective-permute-done | bytes 104480 | tf_op jit(solution)/shard_map/ppermute | solution.py:341
  13.0 0.0 slice-start.2
  13.0 0.0 slice-start.5
  13.0 0.0 slice-start.8
  13.0 0.6 %route.1 = (bf16[24,4096]{1,0:T(8,128)(2,1)S(1)}, bf16[24,4096]{1,0:T(8,128)(2,1)S(1)}, bf16[24,4096]{1,0:T(8,128)(2,1)S(1)}, bf16[24,4096]{1,0:T(8,128)(2,1)S(1)}) custom-call(bf16[8,6528]{1,0:T(8,128)(2,1)S(1)} %get-tuple-element.28.refs_0_, bf16[8,6528]{1,0:T(8,128)(2,1)S(1)} %collective-permute-done.refs_1_, ...), custom_call_target="tpu_custom_call" | custom-call | flops 10000000000 | tf_op jit(solution)/shard_map/route/pallas_call | solution.py:41
  13.6 2.5 %collective-permute-start.3 = (bf16[24,4096]{1,0:T(8,128)(2,1)S(1)}, bf16[24,4096]{1,0:T(8,128)(2,1)S(1)}, u32[]{:S(2)}, u32[]{:S(2)}) collective-permute-start(bf16[24,4096]{1,0:T(8,128)(2,1)S(1)} %get-tuple-element.33), channel_id=1, source_target_pairs={{0,6},{1,17},{2,4},{3,19},{4,2},{5,21},{6,0},{7,23},{8,14},{9,1},{... | collective-permute-start | bytes 589832 | tf_op jit(solution)/shard_map/ppermute | solution.py:341
  16.1 0.5 %collective-permute-start.4 = (bf16[24,4096]{1,0:T(8,128)(2,1)S(1)}, bf16[24,4096]{1,0:T(8,128)(2,1)S(1)}, u32[]{:S(2)}, u32[]{:S(2)}) collective-permute-start(bf16[24,4096]{1,0:T(8,128)(2,1)S(1)} %get-tuple-element.34), channel_id=1, source_target_pairs={{0,2},{1,25},{2,0},{3,27},{4,6},{5,29},{6,4},{7,31},{8,10},{9,17},... | collective-permute-start | bytes 589832 | tf_op jit(solution)/shard_map/ppermute | solution.py:341
  16.6 0.5 collective-permute-start.5
  17.1 0.0 collective-permute-start.6
  17.1 3.1 %collective-permute-done.3.refs_1_ = bf16[24,4096]{1,0:T(8,128)(2,1)S(1)} collective-permute-done((bf16[24,4096]{1,0:T(8,128)(2,1)S(1)}, bf16[24,4096]{1,0:T(8,128)(2,1)S(1)}, u32[]{:S(2)}, u32[]{:S(2)}) %collective-permute-start.3) | collective-permute-done | bytes 196640 | tf_op jit(solution)/shard_map/ppermute | solution.py:341
  20.2 0.0 collective-permute-start.7
  20.2 2.2 %collective-permute-done.4.refs_2_ = bf16[24,4096]{1,0:T(8,128)(2,1)S(1)} collective-permute-done((bf16[24,4096]{1,0:T(8,128)(2,1)S(1)}, bf16[24,4096]{1,0:T(8,128)(2,1)S(1)}, u32[]{:S(2)}, u32[]{:S(2)}) %collective-permute-start.4) | collective-permute-done | bytes 196640 | tf_op jit(solution)/shard_map/ppermute | solution.py:341
  22.4 0.0 collective-permute-start.8
  22.4 0.0 collective-permute-done.5.refs_3_
  22.4 0.5 collective-permute-start.9
  22.9 0.0 collective-permute-done.6.refs_4_
  22.9 0.0 collective-permute-done.7.refs_5_
  22.9 0.9 %collective-permute-done.8.refs_6_ = bf16[24,4096]{1,0:T(8,128)(2,1)S(1)} collective-permute-done((bf16[24,4096]{1,0:T(8,128)(2,1)S(1)}, bf16[24,4096]{1,0:T(8,128)(2,1)S(1)}, u32[]{:S(2)}, u32[]{:S(2)}) %collective-permute-start.8) | collective-permute-done | bytes 196640 | tf_op jit(solution)/shard_map/ppermute | solution.py:345
  23.8 0.3 collective-permute-done.9.refs_7_
  24.1 0.0 slice-done
  24.1 0.0 slice-done.1
  24.1 0.0 slice-done.3
  24.1 0.0 slice-done.4
  24.1 0.0 slice-done.6
  24.1 0.0 slice-done.7
  24.1 0.0 slice-done.2
  24.2 0.0 slice-done.5
  24.2 0.0 slice-done.8
  24.2 6.9 %gate_up_down.1 = (bf16[192,1536]{1,0:T(8,128)(2,1)S(1)}, bf16[96,3072]{1,0:T(8,128)(2,1)S(1)}, bf16[96,3072]{1,0:T(8,128)(2,1)S(1)}) custom-call(bf16[24,4096]{1,0:T(8,128)(2,1)S(1)} %get-tuple-element.32.refs_0_, bf16[24,4096]{1,0:T(8,128)(2,1)S(1)} %collective-permute-done.3.refs_1_, bf16[24,4096]{1,0:T(8,128)(2,1)S(1)} %collective-permute-done.4.refs_2_, ...), custom_call_target="tpu_custom_call" | custom-call | flops 4831838208 | tf_op jit(solution)/shard_map/gate_up_down/pallas_call | solution.py:41
  31.1 0.3 collective-permute-start.10
  31.4 0.8 %down_1.1 = (bf16[96,1024]{1,0:T(8,128)(2,1)S(1)}, bf16[96,1024]{1,0:T(8,128)(2,1)S(1)}) custom-call(bf16[192,1536]{1,0:T(8,128)(2,1)S(1)} %get-tuple-element.37.hidden_ref, bf16[1536,4096]{1,0:T(8,128)(2,1)S(1)} %bitcast.10), custom_call_target="tpu_custom_call" | custom-call | flops 603979776 | tf_op jit(solution)/shard_map/down_1/pallas_call | solution.py:41
  32.2 0.3 collective-permute-start.11
  32.5 1.2 %collective-permute-done.11.refs_3_ = bf16[96,1024]{1,0:T(8,128)(2,1)S(1)} collective-permute-done((bf16[96,1024]{1,0:T(8,128)(2,1)S(1)}, bf16[96,1024]{1,0:T(8,128)(2,1)S(1)}, u32[]{:S(2)}, u32[]{:S(2)}) %collective-permute-start.11) | collective-permute-done | bytes 196640 | tf_op jit(solution)/shard_map/ppermute | solution.py:345
  33.7 0.0 collective-permute-done.10.refs_2_
  33.7 0.2 add.1
  33.9 2.1 %collective-permute-start.12 = (bf16[24,4096]{1,0:T(8,128)(2,1)S(1)}, bf16[24,4096]{1,0:T(8,128)(2,1)S(1)}, u32[]{:S(2)}, u32[]{:S(2)}) collective-permute-start(bf16[24,4096]{1,0:T(8,128)(2,1)S(1)} %get-tuple-element.42), channel_id=1, source_target_pairs={{0,6},{1,9},{2,4},{3,11},{4,2},{5,13},{6,0},{7,15},{8,14},{9,25},{... | collective-permute-start | bytes 589832 | tf_op jit(solution)/shard_map/ppermute | solution.py:341
  35.9 0.5 %collective-permute-start.13 = (bf16[24,4096]{1,0:T(8,128)(2,1)S(1)}, bf16[24,4096]{1,0:T(8,128)(2,1)S(1)}, u32[]{:S(2)}, u32[]{:S(2)}) collective-permute-start(bf16[24,4096]{1,0:T(8,128)(2,1)S(1)} %get-tuple-element.43), channel_id=1, source_target_pairs={{0,2},{1,25},{2,0},{3,27},{4,6},{5,29},{6,4},{7,31},{8,10},{9,17},... | collective-permute-start | bytes 589832 | tf_op jit(solution)/shard_map/ppermute | solution.py:341
  36.5 0.9 %collective-permute-start.14 = (bf16[24,4096]{1,0:T(8,128)(2,1)S(1)}, bf16[24,4096]{1,0:T(8,128)(2,1)S(1)}, u32[]{:S(2)}, u32[]{:S(2)}) collective-permute-start(bf16[24,4096]{1,0:T(8,128)(2,1)S(1)} %get-tuple-element.44), channel_id=1, source_target_pairs={{0,4},{1,17},{2,6},{3,19},{4,0},{5,21},{6,2},{7,23},{8,12},{9,1},{... | collective-permute-start | bytes 589832 | tf_op jit(solution)/shard_map/ppermute | solution.py:341
  37.4 0.3 weigh.1.weights_ref
  37.7 2.8 %collective-permute-done.12.refs_1_ = bf16[24,4096]{1,0:T(8,128)(2,1)S(1)} collective-permute-done((bf16[24,4096]{1,0:T(8,128)(2,1)S(1)}, bf16[24,4096]{1,0:T(8,128)(2,1)S(1)}, u32[]{:S(2)}, u32[]{:S(2)}) %collective-permute-start.12) | collective-permute-done | bytes 196640 | tf_op jit(solution)/shard_map/ppermute | solution.py:341
  40.5 1.7 %collective-permute-done.13.refs_2_ = bf16[24,4096]{1,0:T(8,128)(2,1)S(1)} collective-permute-done((bf16[24,4096]{1,0:T(8,128)(2,1)S(1)}, bf16[24,4096]{1,0:T(8,128)(2,1)S(1)}, u32[]{:S(2)}, u32[]{:S(2)}) %collective-permute-start.13) | collective-permute-done | bytes 196640 | tf_op jit(solution)/shard_map/ppermute | solution.py:341
  42.2 0.4 collective-permute-done.14.refs_3_
  42.6 0.6 %blend.1 = (bf16[8,6144]{1,0:T(8,128)(2,1)S(1)}, bf16[8,6144]{1,0:T(8,128)(2,1)S(1)}, bf16[8,6144]{1,0:T(8,128)(2,1)S(1)}, bf16[8,6144]{1,0:T(8,128)(2,1)S(1)}) custom-call(bf16[192,96]{1,0:T(8,128)(2,1)S(1)} %weigh.1.weights_ref, bf16[24,4096]{1,0:T(8,128)(2,1)S(1)} %get-tuple-element.41.refs_0_, bf16[24,4096]{1,0:T(8,128)(2,1)S(1)} %collective-permute-done.12.refs_1_, ...), custom_call_target="tpu_custom_call" | custom-call | tf_op jit(solution)/shard_map/blend/pallas_call | solution.py:41
  43.2 0.1 collective-permute-start.15
  43.2 2.2 %collective-permute-start.16 = (bf16[8,6144]{1,0:T(8,128)(2,1)S(1)}, bf16[8,6144]{1,0:T(8,128)(2,1)S(1)}, u32[]{:S(2)}, u32[]{:S(2)}) collective-permute-start(bf16[8,6144]{1,0:T(8,128)(2,1)S(1)} %get-tuple-element.47), channel_id=1, source_target_pairs={{0,24},{1,3},{2,26},{3,1},{4,28},{5,7},{6,30},{7,5},{8,16},{9,11},... | collective-permute-start | bytes 294920 | tf_op jit(solution)/shard_map/ppermute | solution.py:341
  45.4 1.9 %collective-permute-start.17 = (bf16[8,6144]{1,0:T(8,128)(2,1)S(1)}, bf16[8,6144]{1,0:T(8,128)(2,1)S(1)}, u32[]{:S(2)}, u32[]{:S(2)}) collective-permute-start(bf16[8,6144]{1,0:T(8,128)(2,1)S(1)} %get-tuple-element.48), channel_id=1, source_target_pairs={{0,16},{1,5},{2,18},{3,7},{4,20},{5,1},{6,22},{7,3},{8,0},{9,13},{... | collective-permute-start | bytes 294920 | tf_op jit(solution)/shard_map/ppermute | solution.py:341
  47.4 1.3 %collective-permute-done.15.refs_1_ = bf16[8,6144]{1,0:T(8,128)(2,1)S(1)} collective-permute-done((bf16[8,6144]{1,0:T(8,128)(2,1)S(1)}, bf16[8,6144]{1,0:T(8,128)(2,1)S(1)}, u32[]{:S(2)}, u32[]{:S(2)}) %collective-permute-start.15) | collective-permute-done | bytes 98336 | tf_op jit(solution)/shard_map/ppermute | solution.py:341
  48.7 1.1 %collective-permute-done.16.refs_2_ = bf16[8,6144]{1,0:T(8,128)(2,1)S(1)} collective-permute-done((bf16[8,6144]{1,0:T(8,128)(2,1)S(1)}, bf16[8,6144]{1,0:T(8,128)(2,1)S(1)}, u32[]{:S(2)}, u32[]{:S(2)}) %collective-permute-start.16) | collective-permute-done | bytes 98336 | tf_op jit(solution)/shard_map/ppermute | solution.py:341
  49.9 1.0 %collective-permute-done.17.refs_3_ = bf16[8,6144]{1,0:T(8,128)(2,1)S(1)} collective-permute-done((bf16[8,6144]{1,0:T(8,128)(2,1)S(1)}, bf16[8,6144]{1,0:T(8,128)(2,1)S(1)}, u32[]{:S(2)}, u32[]{:S(2)}) %collective-permute-start.17) | collective-permute-done | bytes 98336 | tf_op jit(solution)/shard_map/ppermute | solution.py:341
  50.8 0.7 %finish.1 = bf16[6,2,4096]{2,1,0:T(2,128)(2,1)} custom-call(bf16[24,128]{1,0:T(8,128)(2,1)S(1)} %get-tuple-element.27.table_ref, bf16[8,6144]{1,0:T(8,128)(2,1)S(1)} %get-tuple-element.45.refs_0_, bf16[8,6144]{1,0:T(8,128)(2,1)S(1)} %collective-permute-done.15.refs_1_, bf16[8,6144]{1,0:T(8,128)(2,1)S(1)} %collective-permute-done.16.refs_2_, ...), custom_call_target="tpu_custom_call" | custom-call | tf_op jit(solution)/shard_map/finish/pallas_call | solution.py:41
  (3 shorter events, 0.0 us)
Async XLA Ops:
  0.0 24.1 %slice-start = ((s8[12582912]{0:T(1024)(128)(4,1)}), s8[4194304]{0:T(1024)(128)(4,1)S(1)}, s32[]{:S(2)}) async-start(s8[12582912]{0:T(1024)(128)(4,1)} %bitcast.7), calls=%async_computation | async-start | bytes 8388608
  0.0 24.1 %slice-start.1 = ((s8[12582912]{0:T(1024)(128)(4,1)}), s8[4194304]{0:T(1024)(128)(4,1)S(1)}, s32[]{:S(2)}) async-start(s8[12582912]{0:T(1024)(128)(4,1)} %bitcast.7), calls=%async_computation.1 | async-start | bytes 8388608
  0.0 24.1 %slice-start.3 = ((s8[12582912]{0:T(1024)(128)(4,1)}), s8[4194304]{0:T(1024)(128)(4,1)S(1)}, s32[]{:S(2)}) async-start(s8[12582912]{0:T(1024)(128)(4,1)} %bitcast.11), calls=%async_computation.3 | async-start | bytes 8388608
  0.0 24.1 %slice-start.4 = ((s8[12582912]{0:T(1024)(128)(4,1)}), s8[4194304]{0:T(1024)(128)(4,1)S(1)}, s32[]{:S(2)}) async-start(s8[12582912]{0:T(1024)(128)(4,1)} %bitcast.11), calls=%async_computation.4 | async-start | bytes 8388608
  0.0 24.1 %slice-start.6 = ((s8[12582912]{0:T(1024)(128)(4,1)}), s8[4194304]{0:T(1024)(128)(4,1)S(1)}, s32[]{:S(2)}) async-start(s8[12582912]{0:T(1024)(128)(4,1)} %bitcast.14), calls=%async_computation.6 | async-start | bytes 8388608
  0.0 24.1 %slice-start.7 = ((s8[12582912]{0:T(1024)(128)(4,1)}), s8[4194304]{0:T(1024)(128)(4,1)S(1)}, s32[]{:S(2)}) async-start(s8[12582912]{0:T(1024)(128)(4,1)} %bitcast.14), calls=%async_computation.7 | async-start | bytes 8388608
  1.2 6.4 %collective-permute-start = (bf16[8,6528]{1,0:T(8,128)(2,1)S(1)}, bf16[8,6528]{1,0:T(8,128)(2,1)S(1)}, u32[]{:S(2)}, u32[]{:S(2)}) collective-permute-start(bf16[8,6528]{1,0:T(8,128)(2,1)S(1)} %get-tuple-element.29), channel_id=1, source_target_pairs={{0,16},{1,7},{2,18},{3,5},{4,20},{5,3},{6,22},{7,1},{8,0},{9,15},{... | collective-permute-start | bytes 313352 | tf_op jit(solution)/shard_map/ppermute | solution.py:341
  5.3 6.6 %collective-permute-start.1 = (bf16[8,6528]{1,0:T(8,128)(2,1)S(1)}, bf16[8,6528]{1,0:T(8,128)(2,1)S(1)}, u32[]{:S(2)}, u32[]{:S(2)}) collective-permute-start(bf16[8,6528]{1,0:T(8,128)(2,1)S(1)} %get-tuple-element.30), channel_id=1, source_target_pairs={{0,24},{1,3},{2,26},{3,1},{4,28},{5,7},{6,30},{7,5},{8,16},{9,11},... | collective-permute-start | bytes 313352 | tf_op jit(solution)/shard_map/ppermute | solution.py:341
  6.7 6.4 %collective-permute-start.2 = (bf16[8,6528]{1,0:T(8,128)(2,1)S(1)}, bf16[8,6528]{1,0:T(8,128)(2,1)S(1)}, u32[]{:S(2)}, u32[]{:S(2)}) collective-permute-start(bf16[8,6528]{1,0:T(8,128)(2,1)S(1)} %get-tuple-element.31), channel_id=1, source_target_pairs={{0,8},{1,5},{2,10},{3,7},{4,12},{5,1},{6,14},{7,3},{8,24},{9,13},{... | collective-permute-start | bytes 313352 | tf_op jit(solution)/shard_map/ppermute | solution.py:341
  13.0 11.1 %slice-start.2 = ((s8[12582912]{0:T(1024)(128)(4,1)}), s8[4194304]{0:T(1024)(128)(4,1)S(1)}, s32[]{:S(2)}) async-start(s8[12582912]{0:T(1024)(128)(4,1)} %bitcast.7), calls=%async_computation.2 | async-start | bytes 8388608
  13.0 11.2 %slice-start.5 = ((s8[12582912]{0:T(1024)(128)(4,1)}), s8[4194304]{0:T(1024)(128)(4,1)S(1)}, s32[]{:S(2)}) async-start(s8[12582912]{0:T(1024)(128)(4,1)} %bitcast.11), calls=%async_computation.5 | async-start | bytes 8388608
  13.0 11.2 %slice-start.8 = ((s8[12582912]{0:T(1024)(128)(4,1)}), s8[4194304]{0:T(1024)(128)(4,1)S(1)}, s32[]{:S(2)}) async-start(s8[12582912]{0:T(1024)(128)(4,1)} %bitcast.14), calls=%async_computation.8 | async-start | bytes 8388608
  13.6 6.6 %collective-permute-start.3 = (bf16[24,4096]{1,0:T(8,128)(2,1)S(1)}, bf16[24,4096]{1,0:T(8,128)(2,1)S(1)}, u32[]{:S(2)}, u32[]{:S(2)}) collective-permute-start(bf16[24,4096]{1,0:T(8,128)(2,1)S(1)} %get-tuple-element.33), channel_id=1, source_target_pairs={{0,6},{1,17},{2,4},{3,19},{4,2},{5,21},{6,0},{7,23},{8,14},{9,1},{... | collective-permute-start | bytes 589832 | tf_op jit(solution)/shard_map/ppermute | solution.py:341
  16.1 6.3 %collective-permute-start.4 = (bf16[24,4096]{1,0:T(8,128)(2,1)S(1)}, bf16[24,4096]{1,0:T(8,128)(2,1)S(1)}, u32[]{:S(2)}, u32[]{:S(2)}) collective-permute-start(bf16[24,4096]{1,0:T(8,128)(2,1)S(1)} %get-tuple-element.34), channel_id=1, source_target_pairs={{0,2},{1,25},{2,0},{3,27},{4,6},{5,29},{6,4},{7,31},{8,10},{9,17},... | collective-permute-start | bytes 589832 | tf_op jit(solution)/shard_map/ppermute | solution.py:341
  16.6 5.8 %collective-permute-start.5 = (bf16[24,4096]{1,0:T(8,128)(2,1)S(1)}, bf16[24,4096]{1,0:T(8,128)(2,1)S(1)}, u32[]{:S(2)}, u32[]{:S(2)}) collective-permute-start(bf16[24,4096]{1,0:T(8,128)(2,1)S(1)} %get-tuple-element.35), channel_id=1, source_target_pairs={{0,4},{1,9},{2,6},{3,11},{4,0},{5,13},{6,2},{7,15},{8,12},{9,25},{... | collective-permute-start | bytes 589832 | tf_op jit(solution)/shard_map/ppermute | solution.py:341
  17.1 5.8 %collective-permute-start.6 = (bf16[24,4096]{1,0:T(8,128)(2,1)S(1)}, bf16[24,4096]{1,0:T(8,128)(2,1)S(1)}, u32[]{:S(2)}, u32[]{:S(2)}) collective-permute-start(bf16[24,4096]{1,0:T(8,128)(2,1)S(1)} %get-tuple-element.32.refs_0_), channel_id=1, source_target_pairs={{0,1},{1,0},{2,3},{3,2},{4,5},{5,4},{6,7},{7,6},{8,9},{9,8},{10,11... | collective-permute-start | bytes 589832 | tf_op jit(solution)/shard_map/ppermute | solution.py:345
  20.2 2.7 %collective-permute-start.7 = (bf16[24,4096]{1,0:T(8,128)(2,1)S(1)}, bf16[24,4096]{1,0:T(8,128)(2,1)S(1)}, u32[]{:S(2)}, u32[]{:S(2)}) collective-permute-start(bf16[24,4096]{1,0:T(8,128)(2,1)S(1)} %collective-permute-done.3.refs_1_), channel_id=1, source_target_pairs={{0,1},{1,0},{2,3},{3,2},{4,5},{5,4},{6,7},{7,6},{8,9},{9,8},{10,11... | collective-permute-start | bytes 589832 | tf_op jit(solution)/shard_map/ppermute | solution.py:345
  22.4 1.4 %collective-permute-start.8 = (bf16[24,4096]{1,0:T(8,128)(2,1)S(1)}, bf16[24,4096]{1,0:T(8,128)(2,1)S(1)}, u32[]{:S(2)}, u32[]{:S(2)}) collective-permute-start(bf16[24,4096]{1,0:T(8,128)(2,1)S(1)} %collective-permute-done.4.refs_2_), channel_id=1, source_target_pairs={{0,1},{1,0},{2,3},{3,2},{4,5},{5,4},{6,7},{7,6},{8,9},{9,8},{10,11... | collective-permute-start | bytes 589832 | tf_op jit(solution)/shard_map/ppermute | solution.py:345
  22.4 1.7 %collective-permute-start.9 = (bf16[24,4096]{1,0:T(8,128)(2,1)S(1)}, bf16[24,4096]{1,0:T(8,128)(2,1)S(1)}, u32[]{:S(2)}, u32[]{:S(2)}) collective-permute-start(bf16[24,4096]{1,0:T(8,128)(2,1)S(1)} %collective-permute-done.5.refs_3_), channel_id=1, source_target_pairs={{0,1},{1,0},{2,3},{3,2},{4,5},{5,4},{6,7},{7,6},{8,9},{9,8},{10,11... | collective-permute-start | bytes 589832 | tf_op jit(solution)/shard_map/ppermute | solution.py:345
  31.1 2.6 %collective-permute-start.10 = (bf16[96,3072]{1,0:T(8,128)(2,1)S(1)}, bf16[96,3072]{1,0:T(8,128)(2,1)S(1)}, u32[]{:S(2)}, u32[]{:S(2)}) collective-permute-start(bf16[96,3072]{1,0:T(8,128)(2,1)S(1)} %get-tuple-element.39), channel_id=1, source_target_pairs={{0,1},{1,0},{2,3},{3,2},{4,5},{5,4},{6,7},{7,6},{8,9},{9,8},{10,11... | collective-permute-start | bytes 1769480 | tf_op jit(solution)/shard_map/ppermute | solution.py:345
  32.2 1.5 %collective-permute-start.11 = (bf16[96,1024]{1,0:T(8,128)(2,1)S(1)}, bf16[96,1024]{1,0:T(8,128)(2,1)S(1)}, u32[]{:S(2)}, u32[]{:S(2)}) collective-permute-start(bf16[96,1024]{1,0:T(8,128)(2,1)S(1)} %get-tuple-element.40), channel_id=1, source_target_pairs={{0,1},{1,0},{2,3},{3,2},{4,5},{5,4},{6,7},{7,6},{8,9},{9,8},{10,11... | collective-permute-start | bytes 589832 | tf_op jit(solution)/shard_map/ppermute | solution.py:345
  33.9 6.7 %collective-permute-start.12 = (bf16[24,4096]{1,0:T(8,128)(2,1)S(1)}, bf16[24,4096]{1,0:T(8,128)(2,1)S(1)}, u32[]{:S(2)}, u32[]{:S(2)}) collective-permute-start(bf16[24,4096]{1,0:T(8,128)(2,1)S(1)} %get-tuple-element.42), channel_id=1, source_target_pairs={{0,6},{1,9},{2,4},{3,11},{4,2},{5,13},{6,0},{7,15},{8,14},{9,25},{... | collective-permute-start | bytes 589832 | tf_op jit(solution)/shard_map/ppermute | solution.py:341
  35.9 6.3 %collective-permute-start.13 = (bf16[24,4096]{1,0:T(8,128)(2,1)S(1)}, bf16[24,4096]{1,0:T(8,128)(2,1)S(1)}, u32[]{:S(2)}, u32[]{:S(2)}) collective-permute-start(bf16[24,4096]{1,0:T(8,128)(2,1)S(1)} %get-tuple-element.43), channel_id=1, source_target_pairs={{0,2},{1,25},{2,0},{3,27},{4,6},{5,29},{6,4},{7,31},{8,10},{9,17},... | collective-permute-start | bytes 589832 | tf_op jit(solution)/shard_map/ppermute | solution.py:341
  36.5 6.1 %collective-permute-start.14 = (bf16[24,4096]{1,0:T(8,128)(2,1)S(1)}, bf16[24,4096]{1,0:T(8,128)(2,1)S(1)}, u32[]{:S(2)}, u32[]{:S(2)}) collective-permute-start(bf16[24,4096]{1,0:T(8,128)(2,1)S(1)} %get-tuple-element.44), channel_id=1, source_target_pairs={{0,4},{1,17},{2,6},{3,19},{4,0},{5,21},{6,2},{7,23},{8,12},{9,1},{... | collective-permute-start | bytes 589832 | tf_op jit(solution)/shard_map/ppermute | solution.py:341
  43.2 5.6 %collective-permute-start.15 = (bf16[8,6144]{1,0:T(8,128)(2,1)S(1)}, bf16[8,6144]{1,0:T(8,128)(2,1)S(1)}, u32[]{:S(2)}, u32[]{:S(2)}) collective-permute-start(bf16[8,6144]{1,0:T(8,128)(2,1)S(1)} %get-tuple-element.46), channel_id=1, source_target_pairs={{0,8},{1,7},{2,10},{3,5},{4,12},{5,3},{6,14},{7,1},{8,24},{9,15},{... | collective-permute-start | bytes 294920 | tf_op jit(solution)/shard_map/ppermute | solution.py:341
  43.2 6.6 %collective-permute-start.16 = (bf16[8,6144]{1,0:T(8,128)(2,1)S(1)}, bf16[8,6144]{1,0:T(8,128)(2,1)S(1)}, u32[]{:S(2)}, u32[]{:S(2)}) collective-permute-start(bf16[8,6144]{1,0:T(8,128)(2,1)S(1)} %get-tuple-element.47), channel_id=1, source_target_pairs={{0,24},{1,3},{2,26},{3,1},{4,28},{5,7},{6,30},{7,5},{8,16},{9,11},... | collective-permute-start | bytes 294920 | tf_op jit(solution)/shard_map/ppermute | solution.py:341
  45.4 5.4 %collective-permute-start.17 = (bf16[8,6144]{1,0:T(8,128)(2,1)S(1)}, bf16[8,6144]{1,0:T(8,128)(2,1)S(1)}, u32[]{:S(2)}, u32[]{:S(2)}) collective-permute-start(bf16[8,6144]{1,0:T(8,128)(2,1)S(1)} %get-tuple-element.48), channel_id=1, source_target_pairs={{0,16},{1,5},{2,18},{3,7},{4,20},{5,1},{6,22},{7,3},{8,0},{9,13},{... | collective-permute-start | bytes 294920 | tf_op jit(solution)/shard_map/ppermute | solution.py:341
